TPU v7x, 256 devices: a whole 4x4x8 slice. The times are simulated.
256 devices in a mesh: ctx: 64 (over x, z, core), head: 4 (over y).
Axes of the slice: x: 4, y: 4, z: 8, core: 2. Of those that a mesh axis runs over, the one named last changes fastest.
Arguments:
- lin_q: bfloat16 [8192, 64, 128], P('ctx', 'head'), may hold values from -6 to 6
- lin_k: bfloat16 [8192, 64, 128], P('ctx', 'head'), may hold values from -0.5 to 0.5
- lin_v: bfloat16 [8192, 64, 128], P('ctx', 'head'), may hold values from -6 to 6
- decay_rate: float32 [64], P('head'), may hold values from 2.4414062e-06 to 0.03
- norm_gain: float32 [64, 128], P('head'), may hold values from 0.1 to 1.9
- soft_q: bfloat16 [8192, 64, 128], P('ctx', 'head'), may hold values from -6 to 6
- soft_k: bfloat16 [8192, 8, 128], P('ctx', 'head'), may hold values from -6 to 6
- soft_v: bfloat16 [8192, 8, 128], P('ctx', 'head'), may hold values from -6 to 6
- doc_ids: int32 [64], P('ctx'), may hold values from 0 to 7, never falling along the last dimension, each value on 1 to 32 neighbouring positions
- block_mask: int32 [64, 64], P('ctx'), may hold values 0 or 1
Outputs:
- lin_out: bfloat16 [8192, 64, 128], P('ctx', 'head')
- soft_out: bfloat16 [8192, 64, 128], P('ctx', 'head')
Inputs may be any that keep to these rules, and one draw needn't show every extreme that they name: `doc_ids`: document ids never fall along the sequence; each document covers 1 to 32 whole tiles, and one covers exactly 32.
All inputs are finite; a program needn't handle non-finite values. No bound on the sum of `block_mask` on one device may be relied on, other than what follows from the above.
Results may differ from a plain program's by a relative error of at most 0.0045.
Values may be sent and summed in bfloat16 or wider, within the bound.
No kernel may reach another device: no remote copies, remote signals or barrier semaphores. Data moves between devices by JAX's collectives and lax.ppermute only.
A program may use at most 320 MiB of HBM per device.

v0:
```python
import jax
import jax.numpy as jnp
from jax import lax
from jax.sharding import PartitionSpec as P

HEAD_DIM = 128
HEADS = 64
TILE = 128


def entering(value, axis, join, neutral):
    count, mine = (lax.axis_size(axis), lax.axis_index(axis))
    pieces = jax.tree.map(lambda part: lax.all_gather(part, axis), value)
    subtotal = jax.tree.map(
        lambda part, zero: jnp.full_like(part, 0) + jnp.asarray(zero, part.dtype), value, neutral
    )

    def hop(position, subtotal):
        longer = join(subtotal, jax.tree.map(lambda part: part[position], pieces))
        return jax.tree.map(lambda new, old: jnp.where(position < mine, new, old), longer, subtotal)

    return lax.fori_loop(0, count - 1, hop, subtotal)


def shifted(value, axis, steps):
    count = lax.axis_size(axis)
    first, last = (max(0, -steps), min(count, count - steps))
    return lax.ppermute(value, axis, [(source, source + steps) for source in range(first, last)])


def chain_states(earlier, later):
    return (earlier[0] * later[0], later[0][:, None, None] * earlier[1] + later[1])


def lightning_local(lin_q, lin_k, lin_v, decay_rate, norm_gain):
    highest = lax.Precision.HIGHEST
    query = lin_q.astype(jnp.float32)
    keys = lin_k.astype(jnp.float32)
    values = lin_v.astype(jnp.float32)
    length = lin_q.shape[0]
    position = jnp.arange(length).astype(jnp.float32)
    distance = position[:, None] - position[None, :]
    within = jnp.where(
        (distance >= 0)[None],
        jnp.exp(-decay_rate[:, None, None] * jnp.maximum(distance, 0.0)[None]),
        0.0,
    )
    tail = jnp.exp(-decay_rate[None, :] * (length - position)[:, None])
    local_state = jnp.einsum("shd,she->hde", keys * tail[:, :, None], values, precision=highest)
    carry_decay = jnp.exp(-decay_rate * length)
    identity = (jnp.ones_like(carry_decay), jnp.zeros_like(local_state))
    incoming = entering((carry_decay, local_state), "ctx", chain_states, identity)
    scores = jnp.einsum("thd,shd->hts", lin_q, lin_k, preferred_element_type=jnp.float32) * within
    inner = jnp.einsum("hts,she->the", scores, values, precision=highest)
    head_decay = jnp.exp(-decay_rate[None, :] * position[:, None])
    outer = jnp.einsum(
        "thd,hde->the", query * head_decay[:, :, None], incoming[1], precision=highest
    )
    mixed = inner + outer
    squares = jnp.sum(mixed * mixed, axis=(1, 2))
    summed_squares = lax.psum(squares, "head")
    inverse = lax.rsqrt(summed_squares / (HEADS * HEAD_DIM) + 1e-05)
    return (mixed * inverse[:, None, None] * norm_gain[None]).astype(jnp.bfloat16)


def softmax_local(soft_q, soft_k, soft_v, doc_ids, block_mask):
    length = soft_q.shape[0]
    query_heads = soft_q.shape[1]
    key_heads = soft_k.shape[1]
    head_size = soft_q.shape[2]
    groups = query_heads // key_heads
    local_tiles = doc_ids.shape[0]
    devices = lax.axis_size("ctx")
    own_index = lax.axis_index("ctx")
    scale_factor = 1.0 / head_size**0.5
    queries = soft_q.reshape(length, key_heads, groups, head_size)
    query_pos = own_index * length + jnp.arange(length, dtype=jnp.int32)
    query_tiles = own_index * local_tiles + jnp.arange(local_tiles, dtype=jnp.int32)

    def tile_allowed(key_docs, key_start, valid):
        key_count = key_docs.shape[0]
        first_tile = key_start // TILE
        columns = lax.dynamic_slice_in_dim(block_mask, first_tile, key_count, 1)
        key_tiles = first_tile + jnp.arange(key_count, dtype=jnp.int32)
        diagonal = query_tiles[:, None] == key_tiles[None, :]
        return ((columns == 1) | diagonal) & (doc_ids[:, None] == key_docs[None, :]) & valid

    def update(state, keys, values, tile_ok, key_start):
        peak, total, accum = state
        key_pos = key_start + jnp.arange(keys.shape[0], dtype=jnp.int32)
        token_ok = jnp.repeat(jnp.repeat(tile_ok, TILE, axis=0), TILE, axis=1)
        allowed = token_ok & (key_pos[None, :] <= query_pos[:, None])
        scores = (
            jnp.einsum("tkgd,skd->kgts", queries, keys, preferred_element_type=jnp.float32)
            * scale_factor
        )
        masked = jnp.where(allowed, scores, -1e30)
        new_peak = jnp.maximum(peak, jnp.max(masked, axis=-1))
        weights = jnp.where(allowed, jnp.exp(masked - new_peak[..., None]), 0.0)
        fade = jnp.exp(peak - new_peak)
        total = total * fade + jnp.sum(weights, axis=-1)
        product = jnp.einsum(
            "kgts,skd->kgtd",
            weights.astype(jnp.bfloat16),
            values,
            preferred_element_type=jnp.float32,
        )
        accum = accum * fade[..., None] + product
        return (new_peak, total, accum)

    def attend(state, keys, values, key_docs, key_start, valid):
        tile_ok = tile_allowed(key_docs, key_start, valid)
        return update(state, keys, values, tile_ok, key_start)

    start_state = (
        jnp.full((key_heads, groups, length), -1e30, jnp.float32),
        jnp.zeros((key_heads, groups, length), jnp.float32),
        jnp.zeros((key_heads, groups, length, head_size), jnp.float32),
    )
    state = attend(start_state, soft_k, soft_v, doc_ids, own_index * length, jnp.array(True))
    reach = devices - 1

    def turn_step(turn, carry):
        current, keys, values, key_docs = carry
        keys, values, key_docs = shifted((keys, values, key_docs), "ctx", 1)
        source = own_index - turn
        current = attend(
            current, keys, values, key_docs, jnp.maximum(source, 0) * length, source >= 0
        )
        return (current, keys, values, key_docs)

    state, _, _, _ = lax.fori_loop(1, reach + 1, turn_step, (state, soft_k, soft_v, doc_ids))
    result = state[2] / state[1][..., None]
    result = jnp.transpose(result, (2, 0, 1, 3)).reshape(length, query_heads, head_size)
    return result.astype(jnp.bfloat16)


def on_device(
    lin_q, lin_k, lin_v, decay_rate, norm_gain, soft_q, soft_k, soft_v, doc_ids, block_mask
):
    lin_out = lightning_local(lin_q, lin_k, lin_v, decay_rate, norm_gain)
    soft_out = softmax_local(soft_q, soft_k, soft_v, doc_ids, block_mask)
    return (lin_out, soft_out)


def solution(mesh):
    return jax.shard_map(
        on_device,
        mesh=mesh,
        in_specs=(
            P("ctx", "head", None),
            P("ctx", "head", None),
            P("ctx", "head", None),
            P("head"),
            P("head", None),
            P("ctx", "head", None),
            P("ctx", "head", None),
            P("ctx", "head", None),
            P("ctx"),
            P("ctx", None),
        ),
        out_specs=(P("ctx", "head", None), P("ctx", "head", None)),
        check_vma=False,
    )
```

profile of v0, /device:TPU:1, one launch (start us, length us, event | category | flops | bytes accessed | tf_op | source)
XLA Modules:
  0.0 1168.3 jit_solution(7444158586305711602)
XLA Ops:
  22.2 899.1 %while.40 = (s32[]{:T(128)}, f32[2,8,128]{2,1,0:T(8,128)S(1)}, f32[2,8,128]{2,1,0:T(8,128)S(1)}, f32[2,8,128,128]{3,2,1,0:T(8,128)S(1)}, bf16[128,2,128]{2,0,1:T...) while((s32[]{:T(128)}, f32[2,8,128]{2,1,0:T(8,128)S(1)}, ...), condition=%wide.region_9.10_spmd.clone, body=%wide.region_6.9_spmd.clone.sunk | while | flops 137138464 | bytes 6883919 | solution.py:132
  22.2 5.6 collective-permute-start.1
  30.0 3.7 collective-permute-start.2
  38.9 3.7 collective-permute-start.1
  53.7 4.9 collective-permute-start.1
  69.8 4.0 collective-permute-start.1
  98.4 4.2 collective-permute-start.1
  113.0 3.8 collective-permute-start.1
  126.7 3.8 collective-permute-start.1
  141.0 4.7 collective-permute-start.1
  156.9 3.8 collective-permute-start.1
  171.3 4.0 collective-permute-start.1
  186.5 4.2 collective-permute-start.1
  201.8 4.2 collective-permute-start.1
  217.2 4.2 collective-permute-start.1
  232.5 4.2 collective-permute-start.1
  247.9 4.2 collective-permute-start.1
  263.2 4.2 collective-permute-start.1
  278.6 4.2 collective-permute-start.1
  293.1 5.0 collective-permute-start.1
  308.5 3.8 collective-permute-start.1
  329.6 3.9 collective-permute-start.2
  338.7 3.6 collective-permute-start.1
  352.5 3.6 collective-permute-start.1
  366.3 3.6 collective-permute-start.1
  380.1 3.6 collective-permute-start.1
  393.9 3.6 collective-permute-start.1
  408.1 3.6 collective-permute-start.1
  423.0 3.6 collective-permute-start.1
  436.9 3.6 collective-permute-start.1
  450.6 3.6 collective-permute-start.1
  464.5 3.6 collective-permute-start.1
  478.2 3.6 collective-permute-start.1
  492.2 3.6 collective-permute-start.1
  507.3 3.6 collective-permute-start.1
  521.1 3.6 collective-permute-start.1
  534.9 3.6 collective-permute-start.1
  548.7 3.6 collective-permute-start.1
  562.5 3.6 collective-permute-start.1
  576.3 3.6 collective-permute-start.1
  590.1 3.6 collective-permute-start.1
  603.9 3.6 collective-permute-start.1
  617.7 3.6 collective-permute-start.1
  631.5 3.6 collective-permute-start.1
  659.1 3.6 collective-permute-start.1
  672.9 3.6 collective-permute-start.1
  686.7 3.6 collective-permute-start.1
  700.5 3.6 collective-permute-start.1
  714.3 3.6 collective-permute-start.1
  728.1 3.6 collective-permute-start.1
  741.9 3.6 collective-permute-start.1
  755.7 3.6 collective-permute-start.1
  783.3 3.6 collective-permute-start.1
  810.9 3.6 collective-permute-start.1
  824.7 3.6 collective-permute-start.1
  838.5 3.6 collective-permute-start.1
  852.3 3.6 collective-permute-start.1
  866.1 3.6 collective-permute-start.1
  879.9 3.6 collective-permute-start.1
  907.5 3.6 collective-permute-start.1
  922.7 123.0 %all-reduce = f32[1024]{0:T(1024)S(1)} all-reduce(f32[1024]{0:T(1024)S(1)} %get-tuple-element.530), channel_id=2, replica_groups=mesh['ctx'=64,'head'=4] {'ctx'}, use_global_device_ids=true, to_apply=%add | all-reduce | flops 1024 | bytes 8192
  1051.4 94.4 %while.41 = (s32[]{:T(128)}, f32[16,128,128]{2,1,0:T(8,128)S(1)}, s32[]{:T(128)}, f32[64,16]{1,0:T(8,128)S(1)}, f32[64,16,128,128]{3,2,1,0:T(8,128)}, /*index=5*/s32[]{:T(128)}, s32[]{:T(128)}) while((s32[]{:T(128)}, f32[16,128,128]{2,1,0:T(8,128)S(1)}, s32[]{:T(128)}, f32[64,16]{1,0:T(8,128)S(1)}, f32[64,16,128,128]{3,2,1,0:T(8,128)}, ...), condition=%wide.region_1.2_spmd.clone, body=%wide.region_0.1_spmd.clone.sunk | while | flops 1048580 | bytes 3146025 | solution.py:22
  1145.8 4.4 multiply_reduce_fusion
  1150.2 8.5 psum.7
  (1241 shorter events, 621.7 us)
Async XLA Ops:
  7.2 1044.2 %all-gather.4.cloned.1.call-start = ((), (), s32[]{:S(2)}) async-start(), calls=%async_computation | async-start | bytes 68157440 | tf_op jit(solution)/shard_map/all_gather | solution.py:13
  22.2 13.4 %collective-permute-start.1 = (s32[1]{0:T(128)}, s32[1]{0:T(128)}, u32[]{:S(2)}, u32[]{:S(2)}) collective-permute-start(s32[1]{0:T(128)} %copy.127), channel_id=1, source_target_pairs={{0,4},{4,8},{8,12},{12,16},{16,20},{20,24},{24,28},{28,32},{32,36}... | collective-permute-start | bytes 20 | tf_op jit(solution)/shard_map/while/body/eval_jaxpr/ppermute | solution.py:28
  38.9 11.5 collective-permute-start.1
  53.7 12.7 %collective-permute-start.1 = (s32[1]{0:T(128)}, s32[1]{0:T(128)}, u32[]{:S(2)}, u32[]{:S(2)}) collective-permute-start(s32[1]{0:T(128)} %copy.127), channel_id=1, source_target_pairs={{0,4},{4,8},{8,12},{12,16},{16,20},{20,24},{24,28},{28,32},{32,36}... | collective-permute-start | bytes 20 | tf_op jit(solution)/shard_map/while/body/eval_jaxpr/ppermute | solution.py:28
  69.8 11.8 %collective-permute-start.1 = (s32[1]{0:T(128)}, s32[1]{0:T(128)}, u32[]{:S(2)}, u32[]{:S(2)}) collective-permute-start(s32[1]{0:T(128)} %copy.127), channel_id=1, source_target_pairs={{0,4},{4,8},{8,12},{12,16},{16,20},{20,24},{24,28},{28,32},{32,36}... | collective-permute-start | bytes 20 | tf_op jit(solution)/shard_map/while/body/eval_jaxpr/ppermute | solution.py:28
  84.9 10.2 collective-permute-start.1
  98.4 11.3 collective-permute-start.1
  113.0 10.4 collective-permute-start.1
  126.7 11.0 collective-permute-start.1
  141.0 12.5 %collective-permute-start.1 = (s32[1]{0:T(128)}, s32[1]{0:T(128)}, u32[]{:S(2)}, u32[]{:S(2)}) collective-permute-start(s32[1]{0:T(128)} %copy.127), channel_id=1, source_target_pairs={{0,4},{4,8},{8,12},{12,16},{16,20},{20,24},{24,28},{28,32},{32,36}... | collective-permute-start | bytes 20 | tf_op jit(solution)/shard_map/while/body/eval_jaxpr/ppermute | solution.py:28
  156.9 11.1 collective-permute-start.1
  171.3 11.8 %collective-permute-start.1 = (s32[1]{0:T(128)}, s32[1]{0:T(128)}, u32[]{:S(2)}, u32[]{:S(2)}) collective-permute-start(s32[1]{0:T(128)} %copy.127), channel_id=1, source_target_pairs={{0,4},{4,8},{8,12},{12,16},{16,20},{20,24},{24,28},{28,32},{32,36}... | collective-permute-start | bytes 20 | tf_op jit(solution)/shard_map/while/body/eval_jaxpr/ppermute | solution.py:28
  186.5 12.0 %collective-permute-start.1 = (s32[1]{0:T(128)}, s32[1]{0:T(128)}, u32[]{:S(2)}, u32[]{:S(2)}) collective-permute-start(s32[1]{0:T(128)} %copy.127), channel_id=1, source_target_pairs={{0,4},{4,8},{8,12},{12,16},{16,20},{20,24},{24,28},{28,32},{32,36}... | collective-permute-start | bytes 20 | tf_op jit(solution)/shard_map/while/body/eval_jaxpr/ppermute | solution.py:28
  201.8 12.0 %collective-permute-start.1 = (s32[1]{0:T(128)}, s32[1]{0:T(128)}, u32[]{:S(2)}, u32[]{:S(2)}) collective-permute-start(s32[1]{0:T(128)} %copy.127), channel_id=1, source_target_pairs={{0,4},{4,8},{8,12},{12,16},{16,20},{20,24},{24,28},{28,32},{32,36}... | collective-permute-start | bytes 20 | tf_op jit(solution)/shard_map/while/body/eval_jaxpr/ppermute | solution.py:28
  217.2 12.0 %collective-permute-start.1 = (s32[1]{0:T(128)}, s32[1]{0:T(128)}, u32[]{:S(2)}, u32[]{:S(2)}) collective-permute-start(s32[1]{0:T(128)} %copy.127), channel_id=1, source_target_pairs={{0,4},{4,8},{8,12},{12,16},{16,20},{20,24},{24,28},{28,32},{32,36}... | collective-permute-start | bytes 20 | tf_op jit(solution)/shard_map/while/body/eval_jaxpr/ppermute | solution.py:28
  232.5 12.1 %collective-permute-start.1 = (s32[1]{0:T(128)}, s32[1]{0:T(128)}, u32[]{:S(2)}, u32[]{:S(2)}) collective-permute-start(s32[1]{0:T(128)} %copy.127), channel_id=1, source_target_pairs={{0,4},{4,8},{8,12},{12,16},{16,20},{20,24},{24,28},{28,32},{32,36}... | collective-permute-start | bytes 20 | tf_op jit(solution)/shard_map/while/body/eval_jaxpr/ppermute | solution.py:28
  247.9 12.0 %collective-permute-start.1 = (s32[1]{0:T(128)}, s32[1]{0:T(128)}, u32[]{:S(2)}, u32[]{:S(2)}) collective-permute-start(s32[1]{0:T(128)} %copy.127), channel_id=1, source_target_pairs={{0,4},{4,8},{8,12},{12,16},{16,20},{20,24},{24,28},{28,32},{32,36}... | collective-permute-start | bytes 20 | tf_op jit(solution)/shard_map/while/body/eval_jaxpr/ppermute | solution.py:28
  263.2 12.0 %collective-permute-start.1 = (s32[1]{0:T(128)}, s32[1]{0:T(128)}, u32[]{:S(2)}, u32[]{:S(2)}) collective-permute-start(s32[1]{0:T(128)} %copy.127), channel_id=1, source_target_pairs={{0,4},{4,8},{8,12},{12,16},{16,20},{20,24},{24,28},{28,32},{32,36}... | collective-permute-start | bytes 20 | tf_op jit(solution)/shard_map/while/body/eval_jaxpr/ppermute | solution.py:28
  278.6 11.2 collective-permute-start.1
  293.1 12.0 %collective-permute-start.1 = (s32[1]{0:T(128)}, s32[1]{0:T(128)}, u32[]{:S(2)}, u32[]{:S(2)}) collective-permute-start(s32[1]{0:T(128)} %copy.127), channel_id=1, source_target_pairs={{0,4},{4,8},{8,12},{12,16},{16,20},{20,24},{24,28},{28,32},{32,36}... | collective-permute-start | bytes 20 | tf_op jit(solution)/shard_map/while/body/eval_jaxpr/ppermute | solution.py:28
  308.5 12.0 %collective-permute-start.1 = (s32[1]{0:T(128)}, s32[1]{0:T(128)}, u32[]{:S(2)}, u32[]{:S(2)}) collective-permute-start(s32[1]{0:T(128)} %copy.127), channel_id=1, source_target_pairs={{0,4},{4,8},{8,12},{12,16},{16,20},{20,24},{24,28},{28,32},{32,36}... | collective-permute-start | bytes 20 | tf_op jit(solution)/shard_map/while/body/eval_jaxpr/ppermute | solution.py:28
  323.9 11.6 collective-permute-start.1
  338.7 10.5 collective-permute-start.1
  352.5 10.5 collective-permute-start.1
  366.3 10.5 collective-permute-start.1
  380.1 10.5 collective-permute-start.1
  393.9 10.9 collective-permute-start.1
  408.1 11.6 collective-permute-start.1
  423.0 10.5 collective-permute-start.1
  436.9 10.5 collective-permute-start.1
  450.6 10.5 collective-permute-start.1
  464.5 10.5 collective-permute-start.1
  478.2 10.6 collective-permute-start.1
  492.2 11.8 %collective-permute-start.1 = (s32[1]{0:T(128)}, s32[1]{0:T(128)}, u32[]{:S(2)}, u32[]{:S(2)}) collective-permute-start(s32[1]{0:T(128)} %copy.127), channel_id=1, source_target_pairs={{0,4},{4,8},{8,12},{12,16},{16,20},{20,24},{24,28},{28,32},{32,36}... | collective-permute-start | bytes 20 | tf_op jit(solution)/shard_map/while/body/eval_jaxpr/ppermute | solution.py:28
  507.3 10.5 collective-permute-start.1
  521.1 10.5 collective-permute-start.1
  534.9 10.5 collective-permute-start.1
  548.7 10.5 collective-permute-start.1
  562.5 10.5 collective-permute-start.1
  576.3 10.5 collective-permute-start.1
  590.1 10.5 collective-permute-start.1
  603.9 10.5 collective-permute-start.1
  617.7 10.5 collective-permute-start.1
  631.5 10.5 collective-permute-start.1
  645.3 10.5 collective-permute-start.1
  659.1 10.5 collective-permute-start.1
  672.9 10.5 collective-permute-start.1
  686.7 10.5 collective-permute-start.1
  700.5 10.5 collective-permute-start.1
  714.3 10.5 collective-permute-start.1
  728.1 10.5 collective-permute-start.1
  741.9 10.5 collective-permute-start.1
  755.7 10.5 collective-permute-start.1
  769.5 10.5 collective-permute-start.1
  783.3 10.5 collective-permute-start.1
  797.1 10.5 collective-permute-start.1
  810.9 10.5 collective-permute-start.1
  824.7 10.5 collective-permute-start.1
  838.5 10.5 collective-permute-start.1
  852.3 10.5 collective-permute-start.1
  866.1 10.5 collective-permute-start.1
  879.9 10.5 collective-permute-start.1
  893.7 10.5 collective-permute-start.1
  907.5 10.5 collective-permute-start.1
  (128 other events, 2116.1 us)
Sparse Core Ops, SparseCore 0:
  13.9 257.6 all-gather.3
where the time goes:
time: 1180 us; the launch traced here: 1170 us
  starting transfers between devices  571 us (48%)
  other arithmetic  197 us (17%)
  loops' own time  168 us (14%)
  blocking collectives  131 us (11%)
  matrix products  76 us (6%)
  between operations  16.2 us (1%)
    ppermute x189, starting transfers between devices, shifted(): lax.ppermute(value, axis, [(source, source + steps) for source in range(f...  571 us
    another operation x1, loops' own time, softmax_local(): lax.fori_loop(1, reach + 1, turn_step, (state, soft_k, soft_v, doc_ids))  166 us
    unnamed x1, blocking collectives  123 us
    select_n x63, other arithmetic, hop(): jnp.where(position < mine, new, old)  91.8 us
    eq x64, other arithmetic, tile_allowed(): columns == 1  79.8 us
    dot_general x64, matrix products, update(): jnp.einsum('kgts,skd->kgtd', weights.astype(jnp.bfloat16), values, prefer...  44.4 us
  transfers between devices with their start and end apart: 190, of which 0 were waited for; matrix products, arithmetic and copies ran while one was open for 15% of the time, Pallas kernels for 0%

commit v1 on v0

v1 whole, which is shorter than its diff:
```python
import functools

import jax
import jax.numpy as jnp
from jax import lax
from jax.experimental import pallas as pl
from jax.experimental.pallas import tpu as pltpu
from jax.sharding import Mesh, PartitionSpec as P

D = 128
TILE = 128
HEADS = 64
LOCAL = 16
KV = 2
GROUPS = 8
ROWS = TILE * GROUPS
BLOCK = 4 * TILE + 16
CHUNK = 256
SCALE = 1.4426950408889634 / D**0.5
LOWEST = -1e30
bf16, f32 = jnp.bfloat16, jnp.float32
CHIPS = ("x", "zh", "zl")
VMEM = pl.BlockSpec(memory_space=pltpu.VMEM)
SMEM = pl.BlockSpec(memory_space=pltpu.SMEM)


def dot(a, b, ca=1, cb=0):
    return lax.dot_general(a, b, (((ca,), (cb,)), ((), ())), preferred_element_type=f32)


def split(value):
    high = value.astype(bf16)
    return high, (value - high.astype(f32)).astype(bf16)


def iota(shape, axis):
    return lax.broadcasted_iota(jnp.int32, shape, axis)


def call(body, outs, ins, scratch=(), flops=0, nbytes=4 << 20):
    return pl.pallas_call(
        body,
        out_shape=outs,
        in_specs=ins,
        out_specs=jax.tree.map(lambda _: VMEM, outs),
        scratch_shapes=list(scratch),
        compiler_params=pltpu.CompilerParams(vmem_limit_bytes=40 << 20),
        cost_estimate=pl.CostEstimate(flops=flops, bytes_accessed=nbytes, transcendentals=0),
    )


def shape(dims, dtype):
    return jax.ShapeDtypeStruct(dims, dtype)


def flash_body(first, last, groups, *refs):
    refs = list(refs)
    place, doc, mask = refs[:3]
    blocks = refs[3 : 3 + len(groups)]
    refs = refs[3 + len(groups) :]
    if first:
        q_in, own = refs[:2]
        refs = refs[2:]
    else:
        qt, peak_in, total_in, acc_in = refs[:4]
        refs = refs[4:]
    if last:
        out = refs[0]
        refs = refs[1:]
        kbuf, vbuf, peak, total, acc = refs
    elif first:
        qt, peak, total, acc, kbuf, vbuf = refs
    else:
        peak, total, acc, kbuf, vbuf = refs

    chip, core = place[0], place[1]
    mine = 2 * chip + core

    def attend(h, keys, values_t, causal):
        for c in range(ROWS // CHUNK):
            cols = slice(c * CHUNK, (c + 1) * CHUNK)
            s = dot(keys, qt[h, :, cols])
            if causal:
                keep = iota(s.shape, 0) <= (c * CHUNK + iota(s.shape, 1)) // GROUPS
                s = jnp.where(keep, s, LOWEST)
                top = jnp.max(s, axis=0, keepdims=True)
                p = jnp.exp2((s - top) * SCALE)
                total[h, :, cols] = jnp.sum(p, axis=0, keepdims=True)
                acc[h, :, cols] = dot(values_t, p.astype(bf16))
            else:
                old = peak[h, :, cols]
                top = jnp.maximum(old, jnp.max(s, axis=0, keepdims=True))
                fade = jnp.exp2((old - top) * SCALE)
                p = jnp.exp2((s - top) * SCALE)
                total[h, :, cols] = total[h, :, cols] * fade + jnp.sum(p, axis=0, keepdims=True)
                acc[h, :, cols] = acc[h, :, cols] * fade + dot(values_t, p.astype(bf16))
            peak[h, :, cols] = top

    if first:
        q = q_in[...].astype(f32)
        for h in range(KV):
            qt[h] = q[:, h * GROUPS : (h + 1) * GROUPS, :].reshape(ROWS, D).T.astype(bf16)
        for h in range(KV):
            attend(h, own[h * D : (h + 1) * D], own[(KV + h) * D : (KV + h + 1) * D], True)
    else:
        peak[...] = peak_in[...]
        total[...] = total_in[...]
        acc[...] = acc_in[...]

    entries = [(r, i, dist, other) for r, (dists, other) in enumerate(groups) for i, dist in enumerate(dists)]
    docs = jnp.concatenate([blocks[r][i, 4 * D : 4 * D + 16, :].astype(f32)[0:1] for r, i, _, _ in entries], axis=0)
    weight = jnp.left_shift(1, iota(docs.shape, 0)).astype(f32)
    same = (docs == doc[0].astype(f32)) & (iota(docs.shape, 1) == 0)
    bits = jnp.sum(jnp.where(same, weight, 0.0)).astype(jnp.int32)
    count = jnp.int32(0)
    for n, (r, i, dist, other) in enumerate(entries):
        tile = 2 * (chip - dist) + (1 - core if other else core)
        ok = (jnp.bitwise_and(lax.shift_right_logical(bits, n), 1) == 1) & (tile >= 0) & (tile < mine)
        ok = ok & (mask[0, jnp.maximum(tile, 0)] == 1)

        @pl.when(ok)
        def _(r=r, i=i, count=count):
            for h in range(KV):
                kbuf[h, count] = blocks[r][i, h * D : (h + 1) * D, :]
                vbuf[h, count] = blocks[r][i, (KV + h) * D : (KV + h + 1) * D, :]

        count = count + ok.astype(jnp.int32)

    def pair(n, carry):
        for h in range(KV):
            keys = jnp.concatenate([kbuf[h, 2 * n], kbuf[h, 2 * n + 1]], axis=0)
            values_t = jnp.concatenate([vbuf[h, 2 * n], vbuf[h, 2 * n + 1]], axis=1)
            attend(h, keys, values_t, False)
        return carry

    lax.fori_loop(0, lax.shift_right_logical(count, 1), pair, 0)

    @pl.when(jnp.bitwise_and(count, 1) == 1)
    def _():
        for h in range(KV):
            attend(h, kbuf[h, count - 1], vbuf[h, count - 1], False)

    if last:
        heads = [(acc[h] / total[h]).T.reshape(TILE, GROUPS, D) for h in range(KV)]
        out[...] = jnp.concatenate(heads, axis=1).astype(bf16)


def flash(place, doc, mask, blocks, groups, first=None, state=None, last=False):
    state_shapes = [shape((KV, 1, ROWS), f32), shape((KV, 1, ROWS), f32), shape((KV, D, ROWS), f32)]
    slots = sum(len(dists) for dists, _ in groups)
    buffers = [pltpu.VMEM((KV, slots, D, D), bf16)] * 2
    if last:
        outs = shape((TILE, LOCAL, D), bf16)
        scratch = buffers + [pltpu.VMEM(s.shape, s.dtype) for s in state_shapes]
    else:
        outs = state_shapes
        scratch = buffers
    if first is not None:
        outs = [shape((KV, D, ROWS), bf16)] + outs
        extra = list(first)
    else:
        extra = list(state)
    body = functools.partial(flash_body, first is not None, last, groups)
    return call(body, outs, [SMEM] * 3 + [VMEM] * (len(blocks) + len(extra)), scratch, flops=slots * (1 << 28))(
        place, doc, mask, *blocks, *extra
    )


def state_body(rate, k_in, v_in, high_out, state_out, kf, vf):
    kf[...] = k_in[...].astype(f32).reshape(TILE * LOCAL, D)
    vf[...] = v_in[...].astype(f32).reshape(TILE * LOCAL, D)
    left = (TILE - iota((TILE, D), 0)).astype(f32)
    for h in range(LOCAL):
        keys = kf[pl.ds(h, TILE, stride=LOCAL), :] * jnp.exp(-rate[h] * left)
        values = vf[pl.ds(h, TILE, stride=LOCAL), :].astype(bf16)
        high, low = split(keys)
        state = dot(high, values, 0, 0) + dot(low, values, 0, 0)
        state_out[h] = state
        high_out[h] = state.astype(bf16)


def inner_body(rate, q_in, k_in, v_in, inner_out, q_out, qf, kf, vf):
    qf[...] = q_in[...].astype(f32).reshape(TILE * LOCAL, D)
    kf[...] = k_in[...].astype(f32).reshape(TILE * LOCAL, D)
    vf[...] = v_in[...].astype(f32).reshape(TILE * LOCAL, D)
    distance = iota((TILE, TILE), 0) - iota((TILE, TILE), 1)
    steps = jnp.maximum(distance, 0).astype(f32)
    for h in range(LOCAL):
        query = qf[pl.ds(h, TILE, stride=LOCAL), :].astype(bf16)
        keys = kf[pl.ds(h, TILE, stride=LOCAL), :].astype(bf16)
        values = vf[pl.ds(h, TILE, stride=LOCAL), :].astype(bf16)
        within = jnp.where(distance >= 0, jnp.exp(-rate[h] * steps), 0.0)
        high, low = split(dot(query, keys, 1, 1) * within)
        inner_out[h] = dot(high, values) + dot(low, values)
        q_out[h] = query


def outer_body(place, rate, inner, q, near, far, before, mixed_out, sums_out, squares):
    core = place[1]
    upper = core == 1
    position = iota((TILE, D), 0).astype(f32)
    squares[...] = jnp.zeros_like(squares)
    for half, source in ((core, near), (1 - core, far)):
        for i in range(LOCAL // 2):
            h = half * (LOCAL // 2) + i
            r = rate[h]
            fade = jnp.exp(jnp.full((1, D), -TILE, f32) * r)
            entering = source[i].astype(f32)
            entering = jnp.where(upper, fade * entering + before[h].astype(f32), entering)
            high, low = split(entering)
            query = q[h]
            outer = (dot(query, high) + dot(query, low)) * jnp.exp(-r * position)
            mixed = inner[h] + outer
            mixed_out[h] = mixed
            squares[...] += mixed * mixed
    sums_out[...] = jnp.broadcast_to(jnp.sum(squares[...].T, axis=0, keepdims=True), (8, TILE))


def norm_body(mixed, own, s1, s2, s3, gain, out, rows):
    sums = own[...] + s1[...] + s2[...] + s3[...]
    inverse = lax.rsqrt(sums / (HEADS * D) + 1e-5)
    inverse = jnp.broadcast_to(inverse[0:1], (D, TILE)).T
    for h in range(LOCAL):
        rows[pl.ds(h, TILE, stride=LOCAL), :] = mixed[h] * inverse * gain[h : h + 1, :]
    out[...] = rows[...].reshape(TILE, LOCAL, D).astype(bf16)


def chip_shift(value, steps):
    return lax.ppermute(value, CHIPS, [(i, (i + steps) % 32) for i in range(32)])


def x_shift(value, steps):
    return lax.ppermute(value, "x", [(i, (i + steps) % 4) for i in range(4)])


def head_shift(value, steps):
    return lax.ppermute(value, "head", [(i, (i + steps) % 4) for i in range(4)])


def swap(value, axis="core"):
    return lax.ppermute(value, axis, [(0, 1), (1, 0)])


def on_device(lin_q, lin_k, lin_v, decay_rate, norm_gain, soft_q, soft_k, soft_v, doc_ids, block_mask):
    x, zh, zl, core = (lax.axis_index(a) for a in ("x", "zh", "zl", "core"))
    chip = (x * 2 + zh) * 4 + zl
    place = jnp.stack([chip, core]).astype(jnp.int32)
    big = pltpu.VMEM((TILE * LOCAL, D), f32)
    heads = (LOCAL, D, D)

    state_high, state = call(
        state_body, [shape(heads, bf16), shape(heads, f32)], [SMEM, VMEM, VMEM], [big, big], flops=1 << 27
    )(decay_rate, lin_k, lin_v)

    block = jnp.concatenate(
        [
            jnp.transpose(soft_k, (1, 0, 2)).reshape(KV * D, D),
            jnp.transpose(soft_v, (1, 2, 0)).reshape(KV * D, D),
            jnp.broadcast_to(doc_ids.astype(bf16)[:, None], (16, D)),
        ],
        axis=0,
    )[None]

    other_state = swap(state_high)
    half = LOCAL // 2
    half_rate = lax.dynamic_slice_in_dim(decay_rate, core * half, half, 0)
    tile_fade = jnp.exp(-half_rate * TILE)[:, None, None]
    state_mine = lax.dynamic_slice_in_dim(state, core * half, half, 0)
    state_other = lax.dynamic_slice_in_dim(other_state, core * half, half, 0).astype(f32)
    chip_state = jnp.where(core == 0, tile_fade * state_mine + state_other, state_mine + tile_fade * state_other)
    pieces = lax.all_to_all(chip_state.astype(bf16), "zl", 0, 0, tiled=True)

    first_blocks = [chip_shift(block, s) for s in (8, 16, 1, 9)]
    up = jnp.concatenate([first_blocks[2], first_blocks[3]], axis=0)
    down = jnp.concatenate([first_blocks[0], first_blocks[1]], axis=0)
    mate = swap(block)
    qt, *flow = flash(place, doc_ids, block_mask, [mate], [((0,), True)], first=(soft_q, block[0]))

    inner, query = call(
        inner_body, [shape(heads, f32), shape(heads, bf16)], [SMEM, VMEM, VMEM, VMEM], [big] * 3, flops=1 << 28
    )(decay_rate, lin_q, lin_k, lin_v)

    rate = lax.dynamic_slice_in_dim(decay_rate, core * half + 2 * zl, 2, 0)[:, None, None]
    pieces = pieces.reshape(4, 2, D, D).astype(f32)
    chip_fade = jnp.exp(-rate * (2 * TILE))
    row4 = pieces[0]
    prefix = [jnp.zeros_like(row4), row4]
    for k in range(1, 4):
        row4 = row4 * chip_fade + pieces[k]
        prefix.append(row4)
    four_fade = jnp.exp(-rate * (8 * TILE))
    eight_fade = jnp.exp(-rate * (16 * TILE))
    row4_other = swap(row4, "zh")
    row8 = jnp.where(zh == 0, four_fade * row4 + row4_other, row4 + four_fade * row4_other)
    earlier = jnp.zeros_like(row8)
    for k in (3, 2, 1):
        earlier = earlier * eight_fade + jnp.where(x >= k, x_shift(row8, k), 0.0)
    earlier = jnp.where(zh == 1, four_fade * earlier + row4_other, earlier)
    entering = jnp.stack([prefix[k] + jnp.exp(-rate * (2 * TILE * k)) * earlier for k in range(4)])
    near = lax.all_to_all(entering.astype(bf16).reshape(half, D, D), "zl", 0, 0, tiled=True)
    far = swap(near)

    mixed, sums = call(
        outer_body,
        [shape(heads, f32), shape((8, TILE), f32)],
        [SMEM, SMEM] + [VMEM] * 5,
        [pltpu.VMEM((TILE, D), f32)],
        flops=1 << 28,
    )(place, decay_rate, inner, query, near, far, other_state)
    others = [head_shift(sums, s) for s in (1, 2, 3)]

    up_at, down_at = (1, 9), (8, 16)
    for step in range(4):
        groups = [(up_at, False), (down_at, False), (up_at, True), (down_at, True)]
        blocks = [up, down, swap(up), swap(down)]
        done = flash(place, doc_ids, block_mask, blocks, groups, state=(qt, *flow), last=step == 3)
        if step < 3:
            flow = done
            up, down = chip_shift(up, 1), chip_shift(down, -1)
            up_at, down_at = tuple(d + 1 for d in up_at), tuple(d - 1 for d in down_at)

    lin_out = call(norm_body, shape((TILE, LOCAL, D), bf16), [VMEM] * 6, [big])(mixed, sums, *others, norm_gain)
    return lin_out, done


def solution(mesh):
    names = ("x", "zh", "zl", "core", "head")
    fine = Mesh(mesh.devices.reshape(4, 2, 4, 2, 4), names)
    ctx = ("x", "zh", "zl", "core")
    wide = P(ctx, "head", None)
    return jax.shard_map(
        on_device,
        mesh=fine,
        in_specs=(wide, wide, wide, P("head"), P("head", None), wide, wide, wide, P(ctx), P(ctx, None)),
        out_specs=(wide, wide),
        check_vma=False,
    )
```

time: 1180 us -> 108 us (0.09)
  the two profiles are of different devices: /device:TPU:1 before, /device:TPU:133 now
where the time goes in v1:
time: 108 us; the launch traced here: 107 us
  starting transfers between devices  48.3 us (45%)
  Pallas kernels  32 us (30%)
  local copies, waits for them, and re-layouts  13.8 us (13%)
  waiting for transfers between devices  8.37 us (8%)
  other arithmetic  2.54 us (2%)
  between operations  1.66 us (2%)
    pallas_call x5, Pallas kernels, flash(): call(body, outs, [SMEM] * 3 + [VMEM] * (len(blocks) + len(extra)), scratc...  25.7 us
    ppermute x12, starting transfers between devices, swap(): return lax.ppermute(value, axis, [(0, 1), (1, 0)])  17.6 us
    ppermute x10, starting transfers between devices, chip_shift(): lax.ppermute(value, CHIPS, [(i, (i + steps) % 32) for i in range(32)])  15.3 us
    unnamed x50, local copies, waits for them, and re-layouts  13 us
    all_to_all x1, waiting for transfers between devices, on_device(): pieces = lax.all_to_all(chip_state.astype(bf16), 'zl', 0, 0, tiled=True)  6.17 us
    ppermute x3, starting transfers between devices, head_shift(): return lax.ppermute(value, 'head', [(i, (i + steps) % 4) for i in range(4)])  5.07 us
    ppermute x3, starting transfers between devices, x_shift(): return lax.ppermute(value, 'x', [(i, (i + steps) % 4) for i in range(4)])  3.59 us
    all_to_all x1, starting transfers between devices, on_device(): pieces = lax.all_to_all(chip_state.astype(bf16), 'zl', 0, 0, tiled=True)  3.41 us
  transfers between devices with their start and end apart: 30, of which 3 were waited for; matrix products, arithmetic and copies ran while one was open for 5% of the time, Pallas kernels for 27%

profile of v1, /device:TPU:133, one launch (start us, length us, event | category | flops | bytes accessed | tf_op | source)
XLA Modules:
  0.0 106.7 jit_solution(3714812510320985599)
XLA Ops:
  0.6 1.0 copy-done
  1.7 1.0 copy-done.2
  2.7 0.7 copy-done.8
  3.4 1.6 %shard_map.114 = (bf16[16,128,128]{2,1,0:T(8,128)(2,1)S(1)}, f32[16,128,128]{2,1,0:T(8,128)S(1)}) custom-call(f32[16]{0:T(128)S(1)} %copy-done.8, bf16[128,16,128]{2,1,0:T(8,128)(2,1)S(1)} %copy-done, bf16[128,16,128]{2,1,0:T(8,128)(2,1)S(1)} %copy-done.2), custom_call_target="tpu_custom_call" | custom-call | flops 134217728 | bytes 4194304 | tf_op jit(solution)/shard_map/pallas_call | solution.py:251
  5.0 0.8 collective-permute-start
  6.5 0.1 copy.13
  6.6 0.7 copy-done.23
  7.3 0.1 maximum_maximum_fusion
  7.5 0.8 collective-permute-start.9
  8.3 1.4 %collective-permute-start.10 = (bf16[1,528,128]{2,1,0:T(8,128)(2,1)S(1)}, bf16[1,528,128]{2,1,0:T(8,128)(2,1)S(1)}, u32[]{:S(2)}, u32[]{:S(2)}) collective-permute-start(bf16[1,528,128]{2,1,0:T(8,128)(2,1)S(1)} %get-tuple-element.48), channel_id=1, source_target_pairs={{0,72},{8,80},{16,88},{24,96},{32,104},{40,112},{48,120},{56,128},... | collective-permute-start | bytes 405512 | tf_op jit(solution)/shard_map/ppermute | solution.py:229
  9.7 0.2 collective-permute-start.14
  9.9 1.5 %collective-permute-start.15 = (bf16[1,528,128]{2,1,0:T(8,128)(2,1)S(1)}, bf16[1,528,128]{2,1,0:T(8,128)(2,1)S(1)}, u32[]{:S(2)}, u32[]{:S(2)}) collective-permute-start(bf16[1,528,128]{2,1,0:T(8,128)(2,1)S(1)} %get-tuple-element.48), channel_id=1, source_target_pairs={{0,128},{8,136},{16,144},{24,152},{32,160},{40,168},{48,176},{56,1... | collective-permute-start | bytes 405512 | tf_op jit(solution)/shard_map/ppermute | solution.py:229
  11.4 0.7 copy-done.9
  12.1 0.1 multiply_exponential_fusion.6
  12.2 0.9 fusion.1
  13.1 3.4 %all-to-all-start = ((bf16[8,128,128]{2,1,0:T(8,128)(2,1)}), bf16[8,128,128]{2,1,0:T(8,128)(2,1)S(1)}, u32[]{:S(2)}, u32[]{:S(2)}) async-start(bf16[8,128,128]{2,1,0:T(8,128)(2,1)} %fusion.1), calls=%async_computation | async-start | bytes 524288 | tf_op jit(solution)/shard_map/all_to_all | solution.py:271
  16.6 0.2 collective-permute-done.10
  16.9 1.3 %collective-permute-start.11 = (bf16[2,528,128]{2,1,0:T(8,128)(2,1)S(1)}, bf16[2,528,128]{2,1,0:T(8,128)(2,1)}, u32[]{:S(2)}, u32[]{:S(2)}) collective-permute-start(bf16[2,528,128]{2,1,0:T(8,128)(2,1)S(1)} %constant_dynamic-update-slice_fusion.refs_3_), channel_id=1, source_target_pairs={{0,8},{8,16},{16,24},{24,32},{32,40},{40,48},{48,56},{56,64},{64,7... | collective-permute-start | bytes 811016 | tf_op jit(solution)/shard_map/ppermute | solution.py:229
  18.2 6.2 %all-to-all-done = bf16[8,128,128]{2,1,0:T(8,128)(2,1)S(1)} async-done(((bf16[8,128,128]{2,1,0:T(8,128)(2,1)}), bf16[8,128,128]{2,1,0:T(8,128)(2,1)S(1)}, u32[]{:S(2)}, u32[]{:S(2)}) %all-to-all-start) | async-done | bytes 262176 | tf_op jit(solution)/shard_map/all_to_all | solution.py:271
  24.4 0.1 slice_add_fusion
  24.5 0.9 collective-permute-start.1
  25.4 1.6 %constant_dynamic-update-slice_fusion.3 = bf16[2,528,128]{2,1,0:T(8,128)(2,1)} fusion(bf16[1,528,128]{2,1,0:T(8,128)(2,1)} %collective-permute-done.14), kind=kLoop, calls=%fused_computation.23 | loop fusion | bytes 270336
  26.9 0.7 constant_dynamic-update-slice_fusion.2.refs_4_
  27.6 2.9 %collective-permute-start.16 = (bf16[2,528,128]{2,1,0:T(8,128)(2,1)}, bf16[2,528,128]{2,1,0:T(8,128)(2,1)}, u32[]{:S(2)}, u32[]{:S(2)}) collective-permute-start(bf16[2,528,128]{2,1,0:T(8,128)(2,1)} %constant_dynamic-update-slice_fusion.2.refs_4_), channel_id=1, source_target_pairs={{0,248},{8,0},{16,8},{24,16},{32,24},{40,32},{48,40},{56,48},{64,5... | collective-permute-start | bytes 811016 | tf_op jit(solution)/shard_map/ppermute | solution.py:229
  30.5 1.9 %collective-permute-done.1 = f32[2,128,128]{2,1,0:T(8,128)S(1)} collective-permute-done((f32[2,128,128]{2,1,0:T(8,128)S(1)}, f32[2,128,128]{2,1,0:T(8,128)S(1)}, u32[]{:S(2)}, u32[]{:S(2)}) %collective-permute-start.1) | collective-permute-done | bytes 131104 | tf_op jit(solution)/shard_map/ppermute | solution.py:241
  32.4 0.1 add_select_fusion.1
  32.5 0.9 collective-permute-start.2
  33.5 2.5 %collective-permute-start.3 = (f32[2,128,128]{2,1,0:T(8,128)S(1)}, f32[2,128,128]{2,1,0:T(8,128)S(1)}, u32[]{:S(2)}, u32[]{:S(2)}) collective-permute-start(f32[2,128,128]{2,1,0:T(8,128)S(1)} %add_select_fusion.1), channel_id=1, source_target_pairs={{0,128},{64,192},{128,0},{192,64},{1,129},{65,193},{129,1},{193,65... | collective-permute-start | bytes 393224 | tf_op jit(solution)/shard_map/ppermute | solution.py:233
  35.9 0.2 collective-permute-start.4
  36.1 5.5 %collective-permute-start.21 = (bf16[1,528,128]{2,1,0:T(8,128)(2,1)S(1)}, bf16[1,528,128]{2,1,0:T(8,128)(2,1)S(1)}, u32[]{:S(2)}, u32[]{:S(2)}) collective-permute-start(bf16[1,528,128]{2,1,0:T(8,128)(2,1)S(1)} %get-tuple-element.48), channel_id=1, source_target_pairs={{0,4},{4,0},{1,5},{5,1},{2,6},{6,2},{3,7},{7,3},{8,12},{12,8},{9,1... | collective-permute-start | bytes 405512 | tf_op jit(solution)/shard_map/ppermute | solution.py:241
  41.6 0.1 collective-permute-start.26
  41.7 0.5 collective-permute-start.27
  42.2 3.3 %collective-permute-start.17 = (bf16[2,528,128]{2,1,0:T(8,128)(2,1)}, bf16[2,528,128]{2,1,0:T(8,128)(2,1)}, u32[]{:S(2)}, u32[]{:S(2)}) collective-permute-start(bf16[2,528,128]{2,1,0:T(8,128)(2,1)} %collective-permute-done.16.refs_4_), channel_id=1, source_target_pairs={{0,248},{8,0},{16,8},{24,16},{32,24},{40,32},{48,40},{56,48},{64,5... | collective-permute-start | bytes 811016 | tf_op jit(solution)/shard_map/ppermute | solution.py:229
  45.5 0.1 fusion.3
  45.6 0.1 fusion.4
  45.8 4.1 %collective-permute-start.24 = (bf16[2,528,128]{2,1,0:T(8,128)(2,1)}, bf16[2,528,128]{2,1,0:T(8,128)(2,1)}, u32[]{:S(2)}, u32[]{:S(2)}) collective-permute-start(bf16[2,528,128]{2,1,0:T(8,128)(2,1)} %collective-permute-done.11.refs_3_), channel_id=1, source_target_pairs={{0,4},{4,0},{1,5},{5,1},{2,6},{6,2},{3,7},{7,3},{8,12},{12,8},{9,1... | collective-permute-start | bytes 811016 | tf_op jit(solution)/shard_map/ppermute | solution.py:241
  50.0 0.7 pad_maximum_fusion
  50.7 3.4 %all-to-all-start.1 = ((bf16[8,128,128]{2,1,0:T(8,128)(2,1)}), bf16[8,128,128]{2,1,0:T(8,128)(2,1)S(1)}, u32[]{:S(2)}, u32[]{:S(2)}) async-start(bf16[8,128,128]{2,1,0:T(8,128)(2,1)} %bitcast.6), calls=%async_computation.1 | async-start | bytes 524288 | tf_op jit(solution)/shard_map/all_to_all | solution.py:300
  54.1 0.7 copy-done.11
  54.9 1.7 %collective-permute-start.13 = (bf16[2,528,128]{2,1,0:T(8,128)(2,1)}, bf16[2,528,128]{2,1,0:T(8,128)(2,1)}, u32[]{:S(2)}, u32[]{:S(2)}) collective-permute-start(bf16[2,528,128]{2,1,0:T(8,128)(2,1)} %collective-permute-done.12.refs_3_), channel_id=1, source_target_pairs={{0,8},{8,16},{16,24},{24,32},{32,40},{40,48},{48,56},{56,64},{64,7... | collective-permute-start | bytes 811016 | tf_op jit(solution)/shard_map/ppermute | solution.py:229
  56.6 2.2 %collective-permute-start.18 = (bf16[2,528,128]{2,1,0:T(8,128)(2,1)}, bf16[2,528,128]{2,1,0:T(8,128)(2,1)}, u32[]{:S(2)}, u32[]{:S(2)}) collective-permute-start(bf16[2,528,128]{2,1,0:T(8,128)(2,1)} %collective-permute-done.17.refs_4_), channel_id=1, source_target_pairs={{0,248},{8,0},{16,8},{24,16},{32,24},{40,32},{48,40},{56,48},{64,5... | collective-permute-start | bytes 811016 | tf_op jit(solution)/shard_map/ppermute | solution.py:229
  58.8 1.0 copy-done.4
  59.9 2.0 %shard_map.113 = (f32[16,128,128]{2,1,0:T(8,128)S(1)}, bf16[16,128,128]{2,1,0:T(8,128)(2,1)S(1)}) custom-call(f32[16]{0:T(128)S(1)} %copy-done.9, bf16[128,16,128]{2,1,0:T(8,128)(2,1)S(1)} %copy-done.4, bf16[128,16,128]{2,1,0:T(8,128)(2,1)S(1)} %copy-done.1, bf16[128,16,128]{2,1,0:T(8,128)(2,1)S(1)} %copy-done.3), custom_call_target="tpu_custom_call" | custom-call | flops 268435456 | bytes 4194304 | tf_op jit(solution)/shard_map/pallas_call | solution.py:279
  61.9 0.6 copy-done.17
  62.6 1.2 %shard_map.117 = (bf16[2,128,1024]{2,1,0:T(8,128)(2,1)S(1)}, f32[2,1,1024]{2,1,0:T(1,128)S(1)}, f32[2,1,1024]{2,1,0:T(1,128)S(1)}, f32[2,128,1024]{2,1,0:T(8,128)S(1)}) custom-call(s32[2]{0:T(128)S(1)} %pad_add_fusion.place.refs_0_, s32[1]{0:T(128)S(6)} %copy.16.refs_1_, s32[1,64]{1,0:T(1,128)S(1)} %copy-done.17, bf16[1,528,128]{2,1,0:T(8,128)(2,1)S(1)} %copy-done.16, ...), custom_call_target="tpu_custom_call" | custom-call | flops 268435456 | bytes 4194304 | tf_op jit(solution)/shard_map/pallas_call | solution.py:164
  63.8 0.6 collective-permute-start.22
  64.4 0.1 collective-permute-start.23
  64.5 2.0 %shard_map.118 = (f32[2,1,1024]{2,1,0:T(1,128)S(1)}, f32[2,1,1024]{2,1,0:T(1,128)S(1)}, f32[2,128,1024]{2,1,0:T(8,128)S(1)}) custom-call(s32[2]{0:T(128)S(1)} %pad_add_fusion.place.refs_0_, s32[1]{0:T(128)S(6)} %copy.16.refs_1_, s32[1,64]{1,0:T(1,128)S(1)} %copy-done.17, bf16[2,528,128]{2,1,0:T(8,128)(2,1)S(1)} %copy-done.6, ...), custom_call_target="tpu_custom_call" | custom-call | flops 2147483648 | bytes 4194304 | tf_op jit(solution)/shard_map/pallas_call | solution.py:164
  66.5 1.0 copy-done.20
  67.5 4.5 %collective-permute-start.19 = (bf16[2,528,128]{2,1,0:T(8,128)(2,1)}, bf16[2,528,128]{2,1,0:T(8,128)(2,1)S(1)}, u32[]{:S(2)}, u32[]{:S(2)}) collective-permute-start(bf16[2,528,128]{2,1,0:T(8,128)(2,1)} %collective-permute-done.13.refs_3_), channel_id=1, source_target_pairs={{0,4},{4,0},{1,5},{5,1},{2,6},{6,2},{3,7},{7,3},{8,12},{12,8},{9,1... | collective-permute-start | bytes 811016 | tf_op jit(solution)/shard_map/ppermute | solution.py:241
  72.0 0.1 collective-permute-start.20
  72.1 0.7 copy-done.13
  72.8 0.4 collective-permute-start.5
  73.2 1.0 copy-done.14
  74.2 1.0 copy-done.19
  75.2 1.2 %copy-done.21 = f32[2,128,1024]{2,1,0:T(8,128)S(1)} copy-done((f32[2,128,1024]{2,1,0:T(8,128)S(1)}, f32[2,128,1024]{2,1,0:T(8,128)}, u32[]{:S(2)}) %copy-start.21) | copy-done | bytes 1048600
  76.4 6.3 %shard_map.119 = (f32[2,1,1024]{2,1,0:T(1,128)S(1)}, f32[2,1,1024]{2,1,0:T(1,128)S(1)}, f32[2,128,1024]{2,1,0:T(8,128)S(1)}) custom-call(s32[2]{0:T(128)S(1)} %pad_add_fusion.place.refs_0_, s32[1]{0:T(128)S(6)} %copy.16.refs_1_, s32[1,64]{1,0:T(1,128)S(1)} %copy-done.17, bf16[2,528,128]{2,1,0:T(8,128)(2,1)} %collective-permute-done.11.refs_3_, ...), custom_call_target="tpu_custom_call" | custom-call | flops 2147483648 | bytes 4194304 | tf_op jit(solution)/shard_map/pallas_call | solution.py:164
  82.8 6.7 %shard_map.120 = (f32[2,1,1024]{2,1,0:T(1,128)S(1)}, f32[2,1,1024]{2,1,0:T(1,128)S(1)}, f32[2,128,1024]{2,1,0:T(8,128)S(1)}) custom-call(s32[2]{0:T(128)S(1)} %pad_add_fusion.place.refs_0_, s32[1]{0:T(128)S(6)} %copy.16.refs_1_, s32[1,64]{1,0:T(1,128)S(1)} %copy-done.17, bf16[2,528,128]{2,1,0:T(8,128)(2,1)} %collective-permute-done.12.refs_3_, ...), custom_call_target="tpu_custom_call" | custom-call | flops 2147483648 | bytes 4194304 | tf_op jit(solution)/shard_map/pallas_call | solution.py:164
  89.5 1.3 %shard_map.115 = (f32[16,128,128]{2,1,0:T(8,128)S(1)}, f32[8,128]{1,0:T(8,128)S(1)}) custom-call(s32[2]{0:T(128)S(1)} %pad_add_fusion.place.refs_0_, f32[16]{0:T(128)S(1)} %copy-done.9, f32[16,128,128]{2,1,0:T(8,128)S(1)} %get-tuple-element.21.inner, bf16[16,128,128]{2,1,0:T(8,128)(2,1)S(1)} %get-tuple-element.22.q, ...), custom_call_target="tpu_custom_call" | custom-call | flops 268435456 | bytes 4194304 | tf_op jit(solution)/shard_map/pallas_call | solution.py:303
  90.9 1.4 %collective-permute-start.6 = (f32[8,128]{1,0:T(8,128)S(1)}, f32[8,128]{1,0:T(8,128)S(1)}, u32[]{:S(2)}, u32[]{:S(2)}) collective-permute-start(f32[8,128]{1,0:T(8,128)S(1)} %get-tuple-element.26.own), channel_id=1, source_target_pairs={{0,1},{1,2},{2,3},{3,0},{4,5},{5,6},{6,7},{7,4},{8,9},{9,10},{10,1... | collective-permute-start | bytes 12296 | tf_op jit(solution)/shard_map/ppermute | solution.py:237
  92.2 2.6 %collective-permute-start.7 = (f32[8,128]{1,0:T(8,128)S(1)}, f32[8,128]{1,0:T(8,128)S(1)}, u32[]{:S(2)}, u32[]{:S(2)}) collective-permute-start(f32[8,128]{1,0:T(8,128)S(1)} %get-tuple-element.26.own), channel_id=1, source_target_pairs={{0,2},{1,3},{2,0},{3,1},{4,6},{5,7},{6,4},{7,5},{8,10},{9,11},{10,... | collective-permute-start | bytes 12296 | tf_op jit(solution)/shard_map/ppermute | solution.py:237
  94.9 1.1 %collective-permute-start.8 = (f32[8,128]{1,0:T(8,128)S(1)}, f32[8,128]{1,0:T(8,128)S(1)}, u32[]{:S(2)}, u32[]{:S(2)}) collective-permute-start(f32[8,128]{1,0:T(8,128)S(1)} %get-tuple-element.26.own), channel_id=1, source_target_pairs={{0,3},{1,0},{2,1},{3,2},{4,7},{5,4},{6,5},{7,6},{8,11},{9,8},{10,9... | collective-permute-start | bytes 12296 | tf_op jit(solution)/shard_map/ppermute | solution.py:237
  95.9 9.4 %shard_map.121 = bf16[128,16,128]{2,1,0:T(8,128)(2,1)} custom-call(s32[2]{0:T(128)S(1)} %pad_add_fusion.place.refs_0_, s32[1]{0:T(128)S(6)} %copy.16.refs_1_, s32[1,64]{1,0:T(1,128)S(1)} %copy-done.17, bf16[2,528,128]{2,1,0:T(8,128)(2,1)} %collective-permute-done.13.refs_3_, bf16[2,528,128]{2,1,0:T(8,128)(2,1)} %collective-permute-done.18.refs_4_, ...), custom_call_target="tpu_custom_call" | custom-call | flops 2147483648 | bytes 4194304 | tf_op jit(solution)/shard_map/pallas_call | solution.py:164
  105.4 1.4 %shard_map.116 = bf16[128,16,128]{2,1,0:T(8,128)(2,1)} custom-call(f32[16,128,128]{2,1,0:T(8,128)S(1)} %get-tuple-element.25.mixed, f32[8,128]{1,0:T(8,128)S(1)} %get-tuple-element.26.own, f32[8,128]{1,0:T(8,128)S(1)} %collective-permute-done.6.s1, f32[8,128]{1,0:T(8,128)S(1)} %collective-permute-done.7.s2, f32[8,128]{1,0:T(8,128)S(1)} %collective-permute-done.8.s3, ...), custom_call_target="tpu_custom_call" | custom-call | bytes 4194304 | tf_op jit(solution)/shard_map/pallas_call | solution.py:322
  (73 shorter events, 0.4 us)
Async XLA Ops:
  0.6 1.0 copy-start
  1.7 1.0 copy-start.2
  2.7 0.7 copy-start.8
  3.4 3.1 %copy-start.22 = (bf16[128,2,128]{2,1,0:T(2,128)(2,1)S(1)}, bf16[128,2,128]{2,1,0:T(2,128)(2,1)}, u32[]{:S(2)}) copy-start(bf16[128,2,128]{2,1,0:T(2,128)(2,1)} %param.17) | copy-start | bytes 196612
  5.0 7.2 %collective-permute-start = (bf16[16,128,128]{2,1,0:T(8,128)(2,1)S(1)}, bf16[16,128,128]{2,1,0:T(8,128)(2,1)S(1)}, u32[]{:S(2)}, u32[]{:S(2)}) collective-permute-start(bf16[16,128,128]{2,1,0:T(8,128)(2,1)S(1)} %get-tuple-element.24), channel_id=1, source_target_pairs={{0,4},{4,0},{1,5},{5,1},{2,6},{6,2},{3,7},{7,3},{8,12},{12,8},{9,1... | collective-permute-start | bytes 1572872 | tf_op jit(solution)/shard_map/ppermute | solution.py:241
  6.5 0.8 copy-start.23
  7.5 9.1 %collective-permute-start.9 = (bf16[1,528,128]{2,1,0:T(8,128)(2,1)S(1)}, bf16[1,528,128]{2,1,0:T(8,128)(2,1)S(1)}, u32[]{:S(2)}, u32[]{:S(2)}) collective-permute-start(bf16[1,528,128]{2,1,0:T(8,128)(2,1)S(1)} %get-tuple-element.48), channel_id=1, source_target_pairs={{0,8},{8,16},{16,24},{24,32},{32,40},{40,48},{48,56},{56,64},{64,7... | collective-permute-start | bytes 405512 | tf_op jit(solution)/shard_map/ppermute | solution.py:229
  8.3 8.6 %collective-permute-start.10 = (bf16[1,528,128]{2,1,0:T(8,128)(2,1)S(1)}, bf16[1,528,128]{2,1,0:T(8,128)(2,1)S(1)}, u32[]{:S(2)}, u32[]{:S(2)}) collective-permute-start(bf16[1,528,128]{2,1,0:T(8,128)(2,1)S(1)} %get-tuple-element.48), channel_id=1, source_target_pairs={{0,72},{8,80},{16,88},{24,96},{32,104},{40,112},{48,120},{56,128},... | collective-permute-start | bytes 405512 | tf_op jit(solution)/shard_map/ppermute | solution.py:229
  9.7 15.7 %collective-permute-start.14 = (bf16[1,528,128]{2,1,0:T(8,128)(2,1)S(1)}, bf16[1,528,128]{2,1,0:T(8,128)(2,1)}, u32[]{:S(2)}, u32[]{:S(2)}) collective-permute-start(bf16[1,528,128]{2,1,0:T(8,128)(2,1)S(1)} %get-tuple-element.48), channel_id=1, source_target_pairs={{0,64},{8,72},{16,80},{24,88},{32,96},{40,104},{48,112},{56,120},{... | collective-permute-start | bytes 405512 | tf_op jit(solution)/shard_map/ppermute | solution.py:229
  9.9 17.1 %collective-permute-start.15 = (bf16[1,528,128]{2,1,0:T(8,128)(2,1)S(1)}, bf16[1,528,128]{2,1,0:T(8,128)(2,1)S(1)}, u32[]{:S(2)}, u32[]{:S(2)}) collective-permute-start(bf16[1,528,128]{2,1,0:T(8,128)(2,1)S(1)} %get-tuple-element.48), channel_id=1, source_target_pairs={{0,128},{8,136},{16,144},{24,152},{32,160},{40,168},{48,176},{56,1... | collective-permute-start | bytes 405512 | tf_op jit(solution)/shard_map/ppermute | solution.py:229
  11.4 0.7 copy-start.9
  13.1 11.2 %all-to-all-start = ((bf16[8,128,128]{2,1,0:T(8,128)(2,1)}), bf16[8,128,128]{2,1,0:T(8,128)(2,1)S(1)}, u32[]{:S(2)}, u32[]{:S(2)}) async-start(bf16[8,128,128]{2,1,0:T(8,128)(2,1)} %fusion.1), calls=%async_computation | async-start | bytes 524288 | tf_op jit(solution)/shard_map/all_to_all | solution.py:271
  16.9 24.7 %copy-start.5 = (bf16[2,528,128]{2,1,0:T(8,128)(2,1)}, bf16[2,528,128]{2,1,0:T(8,128)(2,1)S(1)}, u32[]{:S(2)}) copy-start(bf16[2,528,128]{2,1,0:T(8,128)(2,1)S(1)} %constant_dynamic-update-slice_fusion.refs_3_) | copy-start | bytes 811012
  16.9 19.2 %collective-permute-start.11 = (bf16[2,528,128]{2,1,0:T(8,128)(2,1)S(1)}, bf16[2,528,128]{2,1,0:T(8,128)(2,1)}, u32[]{:S(2)}, u32[]{:S(2)}) collective-permute-start(bf16[2,528,128]{2,1,0:T(8,128)(2,1)S(1)} %constant_dynamic-update-slice_fusion.refs_3_), channel_id=1, source_target_pairs={{0,8},{8,16},{16,24},{24,32},{32,40},{40,48},{48,56},{56,64},{64,7... | collective-permute-start | bytes 811016 | tf_op jit(solution)/shard_map/ppermute | solution.py:229
  24.5 7.9 %collective-permute-start.1 = (f32[2,128,128]{2,1,0:T(8,128)S(1)}, f32[2,128,128]{2,1,0:T(8,128)S(1)}, u32[]{:S(2)}, u32[]{:S(2)}) collective-permute-start(f32[2,128,128]{2,1,0:T(8,128)S(1)} %slice_add_fusion), channel_id=1, source_target_pairs={{0,32},{32,0},{1,33},{33,1},{2,34},{34,2},{3,35},{35,3},{4,36},{36... | collective-permute-start | bytes 393224 | tf_op jit(solution)/shard_map/ppermute | solution.py:241
  27.6 14.0 %collective-permute-start.16 = (bf16[2,528,128]{2,1,0:T(8,128)(2,1)}, bf16[2,528,128]{2,1,0:T(8,128)(2,1)}, u32[]{:S(2)}, u32[]{:S(2)}) collective-permute-start(bf16[2,528,128]{2,1,0:T(8,128)(2,1)} %constant_dynamic-update-slice_fusion.2.refs_4_), channel_id=1, source_target_pairs={{0,248},{8,0},{16,8},{24,16},{32,24},{40,32},{48,40},{56,48},{64,5... | collective-permute-start | bytes 811016 | tf_op jit(solution)/shard_map/ppermute | solution.py:229
  32.5 9.2 %collective-permute-start.2 = (f32[2,128,128]{2,1,0:T(8,128)S(1)}, f32[2,128,128]{2,1,0:T(8,128)S(1)}, u32[]{:S(2)}, u32[]{:S(2)}) collective-permute-start(f32[2,128,128]{2,1,0:T(8,128)S(1)} %add_select_fusion.1), channel_id=1, source_target_pairs={{0,192},{64,0},{128,64},{192,128},{1,193},{65,1},{129,65},{193,129... | collective-permute-start | bytes 393224 | tf_op jit(solution)/shard_map/ppermute | solution.py:233
  33.5 8.7 %collective-permute-start.3 = (f32[2,128,128]{2,1,0:T(8,128)S(1)}, f32[2,128,128]{2,1,0:T(8,128)S(1)}, u32[]{:S(2)}, u32[]{:S(2)}) collective-permute-start(f32[2,128,128]{2,1,0:T(8,128)S(1)} %add_select_fusion.1), channel_id=1, source_target_pairs={{0,128},{64,192},{128,0},{192,64},{1,129},{65,193},{129,1},{193,65... | collective-permute-start | bytes 393224 | tf_op jit(solution)/shard_map/ppermute | solution.py:233
  35.9 6.3 %collective-permute-start.4 = (f32[2,128,128]{2,1,0:T(8,128)S(1)}, f32[2,128,128]{2,1,0:T(8,128)S(1)}, u32[]{:S(2)}, u32[]{:S(2)}) collective-permute-start(f32[2,128,128]{2,1,0:T(8,128)S(1)} %add_select_fusion.1), channel_id=1, source_target_pairs={{0,64},{64,128},{128,192},{192,0},{1,65},{65,129},{129,193},{193,1... | collective-permute-start | bytes 393224 | tf_op jit(solution)/shard_map/ppermute | solution.py:233
  36.1 9.7 %collective-permute-start.21 = (bf16[1,528,128]{2,1,0:T(8,128)(2,1)S(1)}, bf16[1,528,128]{2,1,0:T(8,128)(2,1)S(1)}, u32[]{:S(2)}, u32[]{:S(2)}) collective-permute-start(bf16[1,528,128]{2,1,0:T(8,128)(2,1)S(1)} %get-tuple-element.48), channel_id=1, source_target_pairs={{0,4},{4,0},{1,5},{5,1},{2,6},{6,2},{3,7},{7,3},{8,12},{12,8},{9,1... | collective-permute-start | bytes 405512 | tf_op jit(solution)/shard_map/ppermute | solution.py:241
  41.6 12.5 %collective-permute-start.26 = (bf16[2,528,128]{2,1,0:T(8,128)(2,1)S(1)}, bf16[2,528,128]{2,1,0:T(8,128)(2,1)S(1)}, u32[]{:S(2)}, u32[]{:S(2)}) collective-permute-start(bf16[2,528,128]{2,1,0:T(8,128)(2,1)S(1)} %constant_dynamic-update-slice_fusion.refs_3_), channel_id=1, source_target_pairs={{0,4},{4,0},{1,5},{5,1},{2,6},{6,2},{3,7},{7,3},{8,12},{12,8},{9,1... | collective-permute-start | bytes 811016 | tf_op jit(solution)/shard_map/ppermute | solution.py:241
  41.7 22.1 %collective-permute-start.27 = (bf16[2,528,128]{2,1,0:T(8,128)(2,1)}, bf16[2,528,128]{2,1,0:T(8,128)(2,1)}, u32[]{:S(2)}, u32[]{:S(2)}) collective-permute-start(bf16[2,528,128]{2,1,0:T(8,128)(2,1)} %constant_dynamic-update-slice_fusion.2.refs_4_), channel_id=1, source_target_pairs={{0,4},{4,0},{1,5},{5,1},{2,6},{6,2},{3,7},{7,3},{8,12},{12,8},{9,1... | collective-permute-start | bytes 811016 | tf_op jit(solution)/shard_map/ppermute | solution.py:241
  42.2 12.7 %collective-permute-start.12 = (bf16[2,528,128]{2,1,0:T(8,128)(2,1)}, bf16[2,528,128]{2,1,0:T(8,128)(2,1)}, u32[]{:S(2)}, u32[]{:S(2)}) collective-permute-start(bf16[2,528,128]{2,1,0:T(8,128)(2,1)} %collective-permute-done.11.refs_3_), channel_id=1, source_target_pairs={{0,8},{8,16},{16,24},{24,32},{32,40},{40,48},{48,56},{56,64},{64,7... | collective-permute-start | bytes 811016 | tf_op jit(solution)/shard_map/ppermute | solution.py:229
  42.2 14.3 %collective-permute-start.17 = (bf16[2,528,128]{2,1,0:T(8,128)(2,1)}, bf16[2,528,128]{2,1,0:T(8,128)(2,1)}, u32[]{:S(2)}, u32[]{:S(2)}) collective-permute-start(bf16[2,528,128]{2,1,0:T(8,128)(2,1)} %collective-permute-done.16.refs_4_), channel_id=1, source_target_pairs={{0,248},{8,0},{16,8},{24,16},{32,24},{40,32},{48,40},{56,48},{64,5... | collective-permute-start | bytes 811016 | tf_op jit(solution)/shard_map/ppermute | solution.py:229
  45.8 4.9 %copy-start.15 = (bf16[1,528,128]{2,1,0:T(8,128)(2,1)}, bf16[1,528,128]{2,1,0:T(8,128)(2,1)S(1)}, u32[]{:S(2)}) copy-start(bf16[1,528,128]{2,1,0:T(8,128)(2,1)S(1)} %collective-permute-done.21.refs_3_) | copy-start | bytes 405508
  45.8 18.6 %collective-permute-start.24 = (bf16[2,528,128]{2,1,0:T(8,128)(2,1)}, bf16[2,528,128]{2,1,0:T(8,128)(2,1)}, u32[]{:S(2)}, u32[]{:S(2)}) collective-permute-start(bf16[2,528,128]{2,1,0:T(8,128)(2,1)} %collective-permute-done.11.refs_3_), channel_id=1, source_target_pairs={{0,4},{4,0},{1,5},{5,1},{2,6},{6,2},{3,7},{7,3},{8,12},{12,8},{9,1... | collective-permute-start | bytes 811016 | tf_op jit(solution)/shard_map/ppermute | solution.py:241
  49.9 8.9 %copy-start.1 = (bf16[128,16,128]{2,1,0:T(8,128)(2,1)S(1)}, bf16[128,16,128]{2,1,0:T(8,128)(2,1)}, u32[]{:S(2)}) copy-start(bf16[128,16,128]{2,1,0:T(8,128)(2,1)} %k_in.3) | copy-start | bytes 1572868
  50.0 8.9 %copy-start.3 = (bf16[128,16,128]{2,1,0:T(8,128)(2,1)S(1)}, bf16[128,16,128]{2,1,0:T(8,128)(2,1)}, u32[]{:S(2)}) copy-start(bf16[128,16,128]{2,1,0:T(8,128)(2,1)} %v_in.3) | copy-start | bytes 1572868
  50.7 22.1 %all-to-all-start.1 = ((bf16[8,128,128]{2,1,0:T(8,128)(2,1)}), bf16[8,128,128]{2,1,0:T(8,128)(2,1)S(1)}, u32[]{:S(2)}, u32[]{:S(2)}) async-start(bf16[8,128,128]{2,1,0:T(8,128)(2,1)} %bitcast.6), calls=%async_computation.1 | async-start | bytes 524288 | tf_op jit(solution)/shard_map/all_to_all | solution.py:300
  54.1 0.7 copy-start.11
  54.8 17.2 %collective-permute-start.25 = (bf16[2,528,128]{2,1,0:T(8,128)(2,1)}, bf16[2,528,128]{2,1,0:T(8,128)(2,1)S(1)}, u32[]{:S(2)}, u32[]{:S(2)}) collective-permute-start(bf16[2,528,128]{2,1,0:T(8,128)(2,1)} %collective-permute-done.16.refs_4_), channel_id=1, source_target_pairs={{0,4},{4,0},{1,5},{5,1},{2,6},{6,2},{3,7},{7,3},{8,12},{12,8},{9,1... | collective-permute-start | bytes 811016 | tf_op jit(solution)/shard_map/ppermute | solution.py:241
  54.9 12.6 %collective-permute-start.13 = (bf16[2,528,128]{2,1,0:T(8,128)(2,1)}, bf16[2,528,128]{2,1,0:T(8,128)(2,1)}, u32[]{:S(2)}, u32[]{:S(2)}) collective-permute-start(bf16[2,528,128]{2,1,0:T(8,128)(2,1)} %collective-permute-done.12.refs_3_), channel_id=1, source_target_pairs={{0,8},{8,16},{16,24},{24,32},{32,40},{40,48},{48,56},{56,64},{64,7... | collective-permute-start | bytes 811016 | tf_op jit(solution)/shard_map/ppermute | solution.py:229
  56.6 15.4 %collective-permute-start.18 = (bf16[2,528,128]{2,1,0:T(8,128)(2,1)}, bf16[2,528,128]{2,1,0:T(8,128)(2,1)}, u32[]{:S(2)}, u32[]{:S(2)}) collective-permute-start(bf16[2,528,128]{2,1,0:T(8,128)(2,1)} %collective-permute-done.17.refs_4_), channel_id=1, source_target_pairs={{0,248},{8,0},{16,8},{24,16},{32,24},{40,32},{48,40},{56,48},{64,5... | collective-permute-start | bytes 811016 | tf_op jit(solution)/shard_map/ppermute | solution.py:229
  58.8 1.0 copy-start.4
  59.9 2.1 %copy-start.10 = (bf16[128,16,128]{2,1,0:T(8,128)(2,1)S(1)}, bf16[128,16,128]{2,1,0:T(8,128)(2,1)}, u32[]{:S(2)}) copy-start(bf16[128,16,128]{2,1,0:T(8,128)(2,1)} %refs_4_.1) | copy-start | bytes 1572868
  59.9 2.1 %copy-start.16 = (bf16[1,528,128]{2,1,0:T(8,128)(2,1)S(1)}, bf16[1,528,128]{2,1,0:T(8,128)(2,1)}, u32[]{:S(2)}) copy-start(bf16[1,528,128]{2,1,0:T(8,128)(2,1)} %copy-done.15) | copy-start | bytes 405508
  61.9 0.7 copy-start.17
  62.6 1.9 %copy-start.6 = (bf16[2,528,128]{2,1,0:T(8,128)(2,1)S(1)}, bf16[2,528,128]{2,1,0:T(8,128)(2,1)}, u32[]{:S(2)}) copy-start(bf16[2,528,128]{2,1,0:T(8,128)(2,1)} %copy-done.5) | copy-start | bytes 811012
  62.6 1.9 %copy-start.12 = (bf16[2,528,128]{2,1,0:T(8,128)(2,1)S(1)}, bf16[2,528,128]{2,1,0:T(8,128)(2,1)}, u32[]{:S(2)}) copy-start(bf16[2,528,128]{2,1,0:T(8,128)(2,1)} %copy-done.11) | copy-start | bytes 811012
  63.8 2.7 %copy-start.18 = (bf16[2,128,1024]{2,1,0:T(8,128)(2,1)}, bf16[2,128,1024]{2,1,0:T(8,128)(2,1)S(1)}, u32[]{:S(2)}) copy-start(bf16[2,128,1024]{2,1,0:T(8,128)(2,1)S(1)} %get-tuple-element.27.refs_7_) | copy-start | bytes 1572868
  63.8 18.9 %collective-permute-start.22 = (bf16[2,528,128]{2,1,0:T(8,128)(2,1)}, bf16[2,528,128]{2,1,0:T(8,128)(2,1)S(1)}, u32[]{:S(2)}, u32[]{:S(2)}) collective-permute-start(bf16[2,528,128]{2,1,0:T(8,128)(2,1)} %collective-permute-done.12.refs_3_), channel_id=1, source_target_pairs={{0,4},{4,0},{1,5},{5,1},{2,6},{6,2},{3,7},{7,3},{8,12},{12,8},{9,1... | collective-permute-start | bytes 811016 | tf_op jit(solution)/shard_map/ppermute | solution.py:241
  64.4 18.4 %collective-permute-start.23 = (bf16[2,528,128]{2,1,0:T(8,128)(2,1)}, bf16[2,528,128]{2,1,0:T(8,128)(2,1)}, u32[]{:S(2)}, u32[]{:S(2)}) collective-permute-start(bf16[2,528,128]{2,1,0:T(8,128)(2,1)} %collective-permute-done.17.refs_4_), channel_id=1, source_target_pairs={{0,4},{4,0},{1,5},{5,1},{2,6},{6,2},{3,7},{7,3},{8,12},{12,8},{9,1... | collective-permute-start | bytes 811016 | tf_op jit(solution)/shard_map/ppermute | solution.py:241
  66.5 1.0 copy-start.20
  67.5 28.4 %collective-permute-start.19 = (bf16[2,528,128]{2,1,0:T(8,128)(2,1)}, bf16[2,528,128]{2,1,0:T(8,128)(2,1)S(1)}, u32[]{:S(2)}, u32[]{:S(2)}) collective-permute-start(bf16[2,528,128]{2,1,0:T(8,128)(2,1)} %collective-permute-done.13.refs_3_), channel_id=1, source_target_pairs={{0,4},{4,0},{1,5},{5,1},{2,6},{6,2},{3,7},{7,3},{8,12},{12,8},{9,1... | collective-permute-start | bytes 811016 | tf_op jit(solution)/shard_map/ppermute | solution.py:241
  72.0 24.0 %collective-permute-start.20 = (bf16[2,528,128]{2,1,0:T(8,128)(2,1)}, bf16[2,528,128]{2,1,0:T(8,128)(2,1)S(1)}, u32[]{:S(2)}, u32[]{:S(2)}) collective-permute-start(bf16[2,528,128]{2,1,0:T(8,128)(2,1)} %collective-permute-done.18.refs_4_), channel_id=1, source_target_pairs={{0,4},{4,0},{1,5},{5,1},{2,6},{6,2},{3,7},{7,3},{8,12},{12,8},{9,1... | collective-permute-start | bytes 811016 | tf_op jit(solution)/shard_map/ppermute | solution.py:241
  72.1 0.7 copy-start.13
  72.8 16.7 %collective-permute-start.5 = (bf16[8,128,128]{2,1,0:T(8,128)(2,1)S(1)}, bf16[8,128,128]{2,1,0:T(8,128)(2,1)S(1)}, u32[]{:S(2)}, u32[]{:S(2)}) collective-permute-start(bf16[8,128,128]{2,1,0:T(8,128)(2,1)S(1)} %all-to-all-done.1.near), channel_id=1, source_target_pairs={{0,4},{4,0},{1,5},{5,1},{2,6},{6,2},{3,7},{7,3},{8,12},{12,8},{9,1... | collective-permute-start | bytes 786440 | tf_op jit(solution)/shard_map/ppermute | solution.py:241
  73.2 1.0 copy-start.14
  74.2 1.0 copy-start.19
  75.2 1.2 %copy-start.21 = (f32[2,128,1024]{2,1,0:T(8,128)S(1)}, f32[2,128,1024]{2,1,0:T(8,128)}, u32[]{:S(2)}) copy-start(f32[2,128,1024]{2,1,0:T(8,128)} %copy-done.20) | copy-start | bytes 3145732
  90.9 14.5 %collective-permute-start.6 = (f32[8,128]{1,0:T(8,128)S(1)}, f32[8,128]{1,0:T(8,128)S(1)}, u32[]{:S(2)}, u32[]{:S(2)}) collective-permute-start(f32[8,128]{1,0:T(8,128)S(1)} %get-tuple-element.26.own), channel_id=1, source_target_pairs={{0,1},{1,2},{2,3},{3,0},{4,5},{5,6},{6,7},{7,4},{8,9},{9,10},{10,1... | collective-permute-start | bytes 12296 | tf_op jit(solution)/shard_map/ppermute | solution.py:237
  92.2 13.1 %collective-permute-start.7 = (f32[8,128]{1,0:T(8,128)S(1)}, f32[8,128]{1,0:T(8,128)S(1)}, u32[]{:S(2)}, u32[]{:S(2)}) collective-permute-start(f32[8,128]{1,0:T(8,128)S(1)} %get-tuple-element.26.own), channel_id=1, source_target_pairs={{0,2},{1,3},{2,0},{3,1},{4,6},{5,7},{6,4},{7,5},{8,10},{9,11},{10,... | collective-permute-start | bytes 12296 | tf_op jit(solution)/shard_map/ppermute | solution.py:237
  94.9 10.5 %collective-permute-start.8 = (f32[8,128]{1,0:T(8,128)S(1)}, f32[8,128]{1,0:T(8,128)S(1)}, u32[]{:S(2)}, u32[]{:S(2)}) collective-permute-start(f32[8,128]{1,0:T(8,128)S(1)} %get-tuple-element.26.own), channel_id=1, source_target_pairs={{0,3},{1,0},{2,1},{3,2},{4,7},{5,4},{6,5},{7,6},{8,11},{9,8},{10,9... | collective-permute-start | bytes 12296 | tf_op jit(solution)/shard_map/ppermute | solution.py:237
  95.9 9.4 %copy-start.7 = (f32[16,128]{1,0:T(8,128)S(1)}, f32[16,128]{1,0:T(8,128)}, u32[]{:S(2)}) copy-start(f32[16,128]{1,0:T(8,128)} %gain.1) | copy-start | bytes 24580

commit v2 on v1

--- a/solution.py
+++ b/solution.py
@@ -15,7 +15,8 @@
 GROUPS = 8
 ROWS = TILE * GROUPS
 BLOCK = 4 * TILE + 16
-CHUNK = 256
+CHUNK = 512
+AHEAD = 2
 SCALE = 1.4426950408889634 / D**0.5
 LOWEST = -1e30
 bf16, f32 = jnp.bfloat16, jnp.float32
@@ -76,45 +77,55 @@
     chip, core = place[0], place[1]
     mine = 2 * chip + core
 
-    def attend(h, keys, values_t, causal):
-        for c in range(ROWS // CHUNK):
-            cols = slice(c * CHUNK, (c + 1) * CHUNK)
-            s = dot(keys, qt[h, :, cols])
+    def attend(keys, values_t, causal):
+        jobs = [(h, c * CHUNK) for h in range(KV) for c in range(ROWS // CHUNK)]
+
+        def score(n):
+            h, at = jobs[n]
+            return dot(keys[h], qt[h, :, at : at + CHUNK])
+
+        scores = [score(n) for n in range(AHEAD)]
+        for n, (h, at) in enumerate(jobs):
+            if n + AHEAD < len(jobs):
+                scores.append(score(n + AHEAD))
+            cols = slice(at, at + CHUNK)
+            s = scores[n]
             if causal:
-                keep = iota(s.shape, 0) <= (c * CHUNK + iota(s.shape, 1)) // GROUPS
+                keep = iota(s.shape, 0) <= (at + iota(s.shape, 1)) // GROUPS
                 s = jnp.where(keep, s, LOWEST)
                 top = jnp.max(s, axis=0, keepdims=True)
                 p = jnp.exp2((s - top) * SCALE)
                 total[h, :, cols] = jnp.sum(p, axis=0, keepdims=True)
-                acc[h, :, cols] = dot(values_t, p.astype(bf16))
+                acc[h, :, cols] = dot(values_t[h], p.astype(bf16))
             else:
                 old = peak[h, :, cols]
                 top = jnp.maximum(old, jnp.max(s, axis=0, keepdims=True))
                 fade = jnp.exp2((old - top) * SCALE)
                 p = jnp.exp2((s - top) * SCALE)
                 total[h, :, cols] = total[h, :, cols] * fade + jnp.sum(p, axis=0, keepdims=True)
-                acc[h, :, cols] = acc[h, :, cols] * fade + dot(values_t, p.astype(bf16))
+                acc[h, :, cols] = acc[h, :, cols] * fade + dot(values_t[h], p.astype(bf16))
             peak[h, :, cols] = top
 
     if first:
         q = q_in[...].astype(f32)
         for h in range(KV):
             qt[h] = q[:, h * GROUPS : (h + 1) * GROUPS, :].reshape(ROWS, D).T.astype(bf16)
-        for h in range(KV):
-            attend(h, own[h * D : (h + 1) * D], own[(KV + h) * D : (KV + h + 1) * D], True)
+        attend([own[h * D : (h + 1) * D] for h in range(KV)], [own[(KV + h) * D : (KV + h + 1) * D] for h in range(KV)], True)
     else:
         peak[...] = peak_in[...]
         total[...] = total_in[...]
         acc[...] = acc_in[...]
 
-    entries = [(r, i, dist, other) for r, (dists, other) in enumerate(groups) for i, dist in enumerate(dists)]
-    docs = jnp.concatenate([blocks[r][i, 4 * D : 4 * D + 16, :].astype(f32)[0:1] for r, i, _, _ in entries], axis=0)
+    entries = [(r, i) for r in range(len(groups)) for i in range(len(groups[r][0]))]
+    docs = jnp.concatenate([blocks[r][i, 4 * D : 4 * D + 16, :].astype(f32)[0:1] for r, i in entries], axis=0)
     weight = jnp.left_shift(1, iota(docs.shape, 0)).astype(f32)
     same = (docs == doc[0].astype(f32)) & (iota(docs.shape, 1) == 0)
     bits = jnp.sum(jnp.where(same, weight, 0.0)).astype(jnp.int32)
     count = jnp.int32(0)
-    for n, (r, i, dist, other) in enumerate(entries):
-        tile = 2 * (chip - dist) + (1 - core if other else core)
+    for n, (r, i) in enumerate(entries):
+        dists, swapped = groups[r]
+        carrier = 1 - core if swapped else core
+        tile = 2 * (chip - jnp.where(carrier == 0, dists[i][0], dists[i][1])) + (carrier if i % 2 == 0 else 1 - carrier)
         ok = (jnp.bitwise_and(lax.shift_right_logical(bits, n), 1) == 1) & (tile >= 0) & (tile < mine)
         ok = ok & (mask[0, jnp.maximum(tile, 0)] == 1)
 
@@ -127,18 +138,16 @@
         count = count + ok.astype(jnp.int32)
 
     def pair(n, carry):
-        for h in range(KV):
-            keys = jnp.concatenate([kbuf[h, 2 * n], kbuf[h, 2 * n + 1]], axis=0)
-            values_t = jnp.concatenate([vbuf[h, 2 * n], vbuf[h, 2 * n + 1]], axis=1)
-            attend(h, keys, values_t, False)
+        keys = [jnp.concatenate([kbuf[h, 2 * n], kbuf[h, 2 * n + 1]], axis=0) for h in range(KV)]
+        values_t = [jnp.concatenate([vbuf[h, 2 * n], vbuf[h, 2 * n + 1]], axis=1) for h in range(KV)]
+        attend(keys, values_t, False)
         return carry
 
     lax.fori_loop(0, lax.shift_right_logical(count, 1), pair, 0)
 
     @pl.when(jnp.bitwise_and(count, 1) == 1)
     def _():
-        for h in range(KV):
-            attend(h, kbuf[h, count - 1], vbuf[h, count - 1], False)
+        attend([kbuf[h, count - 1] for h in range(KV)], [vbuf[h, count - 1] for h in range(KV)], False)
 
     if last:
         heads = [(acc[h] / total[h]).T.reshape(TILE, GROUPS, D) for h in range(KV)]
@@ -195,24 +204,80 @@
         q_out[h] = query
 
 
+def power(rate, tokens):
+    return jnp.exp(jnp.full((1, D), -tokens, f32) * rate)
+
+
+def chip_body(place, rate, mine, other, *slices):
+    core, zl = place[1], place[2]
+    first = core == 0
+    for s, out in enumerate(slices):
+        owner = lax.rem(zl + s, 4)
+        for i in range(2):
+            h = core * (LOCAL // 2) + 2 * owner + i
+            fade = power(rate[h], TILE)
+            state, rest = mine[h], other[h].astype(f32)
+            out[i] = jnp.where(first, fade * state + rest, state + fade * rest).astype(bf16)
+
+
+def four_body(place, rate, p0, p1, p2, p3, total, sent):
+    core, zl = place[1], place[2]
+    for i in range(2):
+        r = rate[core * (LOCAL // 2) + 2 * zl + i]
+        row = jnp.zeros((D, D), f32)
+        for s, piece in enumerate((p0, p1, p2, p3)):
+            source = lax.rem(zl + 4 - s, 4)
+            row += piece[i].astype(f32) * power(r, ((3 - source) * 2 * TILE).astype(f32))
+        total[i] = row
+        sent[i] = row.astype(bf16)
+
+
+def eight_body(place, rate, four, other, out):
+    core, zl, zh = place[1], place[2], place[3]
+    for i in range(2):
+        fade = power(rate[core * (LOCAL // 2) + 2 * zl + i], 8 * TILE)
+        mine, rest = four[i], other[i].astype(f32)
+        out[i] = jnp.where(zh == 0, fade * mine + rest, mine + fade * rest).astype(bf16)
+
+
+def entering_body(place, rate, p0, p1, p2, p3, other, x1, x2, x3, *slices):
+    core, zl, zh, x = place[1], place[2], place[3], place[4]
+    for i in range(2):
+        r = rate[core * (LOCAL // 2) + 2 * zl + i]
+        earlier = jnp.zeros((D, D), f32)
+        for k, part in ((3, x3), (2, x2), (1, x1)):
+            earlier = earlier * power(r, 16 * TILE) + jnp.where(x >= k, part[i].astype(f32), 0.0)
+        earlier = jnp.where(zh == 1, power(r, 8 * TILE) * earlier + other[i].astype(f32), earlier)
+        pieces = [p[i].astype(f32) for p in (p0, p1, p2, p3)]
+        for t, out in enumerate(slices):
+            target = lax.rem(zl + t, 4)
+            state = earlier * power(r, (target * 2 * TILE).astype(f32))
+            for s, piece in enumerate(pieces):
+                source = lax.rem(zl + 4 - s, 4)
+                fade = power(r, (jnp.maximum(target - 1 - source, 0) * 2 * TILE).astype(f32))
+                state += jnp.where(source < target, piece * fade, 0.0)
+            out[i] = state.astype(bf16)
+
+
 def outer_body(place, rate, inner, q, near, far, before, mixed_out, sums_out, squares):
-    core = place[1]
+    core, zl = place[1], place[2]
     upper = core == 1
     position = iota((TILE, D), 0).astype(f32)
     squares[...] = jnp.zeros_like(squares)
     for half, source in ((core, near), (1 - core, far)):
-        for i in range(LOCAL // 2):
-            h = half * (LOCAL // 2) + i
-            r = rate[h]
-            fade = jnp.exp(jnp.full((1, D), -TILE, f32) * r)
-            entering = source[i].astype(f32)
-            entering = jnp.where(upper, fade * entering + before[h].astype(f32), entering)
-            high, low = split(entering)
-            query = q[h]
-            outer = (dot(query, high) + dot(query, low)) * jnp.exp(-r * position)
-            mixed = inner[h] + outer
-            mixed_out[h] = mixed
-            squares[...] += mixed * mixed
+        for s in range(4):
+            owner = lax.rem(zl + 4 - s, 4)
+            for i in range(2):
+                h = half * (LOCAL // 2) + 2 * owner + i
+                r = rate[h]
+                entering = source[s, i].astype(f32)
+                entering = jnp.where(upper, power(r, TILE) * entering + before[h].astype(f32), entering)
+                high, low = split(entering)
+                query = q[h]
+                outer = (dot(query, high) + dot(query, low)) * jnp.exp(-r * position)
+                mixed = inner[h] + outer
+                mixed_out[h] = mixed
+                squares[...] += mixed * mixed
     sums_out[...] = jnp.broadcast_to(jnp.sum(squares[...].T, axis=0, keepdims=True), (8, TILE))
 
 
@@ -225,8 +290,9 @@
     out[...] = rows[...].reshape(TILE, LOCAL, D).astype(bf16)
 
 
-def chip_shift(value, steps):
-    return lax.ppermute(value, CHIPS, [(i, (i + steps) % 32) for i in range(32)])
+def two_ways(value, steps0, steps1):
+    pairs = [(2 * i + c, 2 * ((i + s) % 32) + c) for i in range(32) for c, s in ((0, steps0), (1, steps1))]
+    return lax.ppermute(value, (*CHIPS, "core"), pairs)
 
 
 def x_shift(value, steps):
@@ -237,20 +303,25 @@
     return lax.ppermute(value, "head", [(i, (i + steps) % 4) for i in range(4)])
 
 
+def zl_shift(value, steps):
+    return lax.ppermute(value, "zl", [(i, (i + steps) % 4) for i in range(4)])
+
+
 def swap(value, axis="core"):
     return lax.ppermute(value, axis, [(0, 1), (1, 0)])
+
+
+def after(value, *others):
+    return lax.optimization_barrier((value, *others))[0]
 
 
 def on_device(lin_q, lin_k, lin_v, decay_rate, norm_gain, soft_q, soft_k, soft_v, doc_ids, block_mask):
     x, zh, zl, core = (lax.axis_index(a) for a in ("x", "zh", "zl", "core"))
     chip = (x * 2 + zh) * 4 + zl
-    place = jnp.stack([chip, core]).astype(jnp.int32)
+    place = jnp.stack([chip, core, zl, zh, x]).astype(jnp.int32)
     big = pltpu.VMEM((TILE * LOCAL, D), f32)
     heads = (LOCAL, D, D)
-
-    state_high, state = call(
-        state_body, [shape(heads, bf16), shape(heads, f32)], [SMEM, VMEM, VMEM], [big, big], flops=1 << 27
-    )(decay_rate, lin_k, lin_v)
+    pair = (2, D, D)
 
     block = jnp.concatenate(
         [
@@ -260,67 +331,73 @@
         ],
         axis=0,
     )[None]
-
+    mate = swap(block)
+    both = jnp.concatenate((block, mate), axis=0)
+    arrived = two_ways(both, 1, 8), two_ways(both, 9, 16)
+
+    state_high, state = call(
+        state_body, [shape(heads, bf16), shape(heads, f32)], [SMEM, VMEM, VMEM], [big, big], flops=1 << 30
+    )(decay_rate, after(lin_k, both), lin_v)
     other_state = swap(state_high)
-    half = LOCAL // 2
-    half_rate = lax.dynamic_slice_in_dim(decay_rate, core * half, half, 0)
-    tile_fade = jnp.exp(-half_rate * TILE)[:, None, None]
-    state_mine = lax.dynamic_slice_in_dim(state, core * half, half, 0)
-    state_other = lax.dynamic_slice_in_dim(other_state, core * half, half, 0).astype(f32)
-    chip_state = jnp.where(core == 0, tile_fade * state_mine + state_other, state_mine + tile_fade * state_other)
-    pieces = lax.all_to_all(chip_state.astype(bf16), "zl", 0, 0, tiled=True)
-
-    first_blocks = [chip_shift(block, s) for s in (8, 16, 1, 9)]
-    up = jnp.concatenate([first_blocks[2], first_blocks[3]], axis=0)
-    down = jnp.concatenate([first_blocks[0], first_blocks[1]], axis=0)
-    mate = swap(block)
-    qt, *flow = flash(place, doc_ids, block_mask, [mate], [((0,), True)], first=(soft_q, block[0]))
+    slices = call(chip_body, [shape(pair, bf16)] * 4, [SMEM, SMEM, VMEM, VMEM])(place, decay_rate, state, other_state)
+    pieces = [slices[0]] + [zl_shift(slices[k], k) for k in (1, 2, 3)]
 
     inner, query = call(
-        inner_body, [shape(heads, f32), shape(heads, bf16)], [SMEM, VMEM, VMEM, VMEM], [big] * 3, flops=1 << 28
-    )(decay_rate, lin_q, lin_k, lin_v)
-
-    rate = lax.dynamic_slice_in_dim(decay_rate, core * half + 2 * zl, 2, 0)[:, None, None]
-    pieces = pieces.reshape(4, 2, D, D).astype(f32)
-    chip_fade = jnp.exp(-rate * (2 * TILE))
-    row4 = pieces[0]
-    prefix = [jnp.zeros_like(row4), row4]
-    for k in range(1, 4):
-        row4 = row4 * chip_fade + pieces[k]
-        prefix.append(row4)
-    four_fade = jnp.exp(-rate * (8 * TILE))
-    eight_fade = jnp.exp(-rate * (16 * TILE))
-    row4_other = swap(row4, "zh")
-    row8 = jnp.where(zh == 0, four_fade * row4 + row4_other, row4 + four_fade * row4_other)
-    earlier = jnp.zeros_like(row8)
-    for k in (3, 2, 1):
-        earlier = earlier * eight_fade + jnp.where(x >= k, x_shift(row8, k), 0.0)
-    earlier = jnp.where(zh == 1, four_fade * earlier + row4_other, earlier)
-    entering = jnp.stack([prefix[k] + jnp.exp(-rate * (2 * TILE * k)) * earlier for k in range(4)])
-    near = lax.all_to_all(entering.astype(bf16).reshape(half, D, D), "zl", 0, 0, tiled=True)
+        inner_body, [shape(heads, f32), shape(heads, bf16)], [SMEM, VMEM, VMEM, VMEM], [big] * 3, flops=1 << 30
+    )(decay_rate, after(lin_q, slices[0]), lin_k, lin_v)
+
+    row4, row4_sent = call(four_body, [shape(pair, f32), shape(pair, bf16)], [SMEM, SMEM] + [VMEM] * 4)(
+        place, decay_rate, *pieces
+    )
+    row4_other = swap(row4_sent, "zh")
+
+    def attend(blocks, groups, **state):
+        return flash(place, doc_ids, block_mask, blocks, groups, **state)
+
+    def parts(k):
+        dists = ((1 + k, 8 - k),) * 2 + ((9 + k, 16 - k),) * 2
+        return [carried, swap(carried)], [(dists, False), (dists, True)]
+
+    qt, *flow = attend([mate], [(((0, 0),), True)], first=(after(soft_q, row4_sent), block[0]))
+    row4 = after(row4, flow[0])
+    carried = after(jnp.concatenate(after(arrived, query, row4_sent), axis=0), row4_other, flow[0])
+    chips0 = parts(0)
+    carried = two_ways(carried, 1, -1)
+
+    row8 = call(eight_body, shape(pair, bf16), [SMEM, SMEM, VMEM, VMEM])(place, decay_rate, row4, row4_other)
+    earlier = [x_shift(row8, k) for k in (1, 2, 3)]
+    flow = attend(*chips0, state=(qt, *after(tuple(flow), row8)))
+    earlier = after(tuple(earlier), flow[0])
+    carried = after(carried, *earlier)
+    chips1 = parts(1)
+    carried = two_ways(carried, 1, -1)
+
+    entering = call(entering_body, [shape(pair, bf16)] * 4, [SMEM, SMEM] + [VMEM] * 8)(
+        place, decay_rate, *pieces, row4_other, *earlier
+    )
+    near = jnp.stack([entering[0]] + [zl_shift(entering[k], k) for k in (1, 2, 3)])
+    flow = attend(*chips1, state=(qt, *after(tuple(flow), entering[0])))
+    near = after(near, flow[0])
+    carried = after(carried, flow[0])
+    chips2 = parts(2)
+    carried = two_ways(carried, 1, -1)
+
     far = swap(near)
-
     mixed, sums = call(
         outer_body,
         [shape(heads, f32), shape((8, TILE), f32)],
         [SMEM, SMEM] + [VMEM] * 5,
         [pltpu.VMEM((TILE, D), f32)],
-        flops=1 << 28,
+        flops=1 << 30,
     )(place, decay_rate, inner, query, near, far, other_state)
     others = [head_shift(sums, s) for s in (1, 2, 3)]
-
-    up_at, down_at = (1, 9), (8, 16)
-    for step in range(4):
-        groups = [(up_at, False), (down_at, False), (up_at, True), (down_at, True)]
-        blocks = [up, down, swap(up), swap(down)]
-        done = flash(place, doc_ids, block_mask, blocks, groups, state=(qt, *flow), last=step == 3)
-        if step < 3:
-            flow = done
-            up, down = chip_shift(up, 1), chip_shift(down, -1)
-            up_at, down_at = tuple(d + 1 for d in up_at), tuple(d - 1 for d in down_at)
-
-    lin_out = call(norm_body, shape((TILE, LOCAL, D), bf16), [VMEM] * 6, [big])(mixed, sums, *others, norm_gain)
-    return lin_out, done
+    flow = attend(*chips2, state=(qt, *after(tuple(flow), sums)))
+    carried, *flow = after((carried, *flow), *others)
+    soft_out = attend(*parts(3), state=(qt, *flow), last=True)
+    lin_out = call(norm_body, shape((TILE, LOCAL, D), bf16), [VMEM] * 6, [big])(
+        after(mixed, soft_out), sums, *others, norm_gain
+    )
+    return lin_out, soft_out
 
 
 def solution(mesh):

time: 108 us -> 83.9 us (0.78)
  the two profiles are of different devices: /device:TPU:133 before, /device:TPU:1 now
where the time goes in v2:
time: 83.9 us; the launch traced here: 83.7 us
  starting transfers between devices  52.6 us (63%)
  Pallas kernels  14.9 us (18%)
  waiting for transfers between devices  10.8 us (13%)
  other arithmetic  2.05 us (2%)
  local copies, waits for them, and re-layouts  1.79 us (2%)
  between operations  1.55 us (2%)
    ppermute x5, starting transfers between devices, two_ways(): return lax.ppermute(value, (*CHIPS, 'core'), pairs)  23.4 us
    ppermute x8, starting transfers between devices, swap(): return lax.ppermute(value, axis, [(0, 1), (1, 0)])  12.8 us
    ppermute x6, starting transfers between devices, zl_shift(): return lax.ppermute(value, 'zl', [(i, (i + steps) % 4) for i in range(4)])  8.62 us
    pallas_call x5, Pallas kernels, flash(): call(body, outs, [SMEM] * 3 + [VMEM] * (len(blocks) + len(extra)), scratc...  5.9 us
    ppermute x3, starting transfers between devices, head_shift(): return lax.ppermute(value, 'head', [(i, (i + steps) % 4) for i in range(4)])  5.06 us
    ppermute x3, waiting for transfers between devices, x_shift(): return lax.ppermute(value, 'x', [(i, (i + steps) % 4) for i in range(4)])  4.13 us
    ppermute x8, waiting for transfers between devices, swap(): return lax.ppermute(value, axis, [(0, 1), (1, 0)])  3.08 us
    ppermute x3, starting transfers between devices, x_shift(): return lax.ppermute(value, 'x', [(i, (i + steps) % 4) for i in range(4)])  2.75 us
  transfers between devices with their start and end apart: 25, of which 8 were waited for; matrix products, arithmetic and copies ran while one was open for 2% of the time, Pallas kernels for 12%

profile of v2, /device:TPU:1, one launch (start us, length us, event | category | flops | bytes accessed | tf_op | source)
XLA Modules:
  0.0 83.7 jit_solution(13227850117303491716)
XLA Ops:
  1.3 0.9 %copy.12 = bf16[2,128,128]{2,1,0:T(8,128)(2,1)S(1)} copy(bf16[2,128,128]{2,0,1:T(2,128)(2,1)} %bitcast.19) | data formatting | bytes 131072 | tf_op jit(solution)/shard_map/transpose | solution.py:328
  2.2 0.0 copy-start.3
  2.2 0.0 copy-start.4
  2.2 0.1 copy.13
  2.4 0.1 maximum_maximum_fusion
  2.5 0.0 copy-start.1
  2.5 3.3 %collective-permute-start = (bf16[1,528,128]{2,1,0:T(8,128)(2,1)S(1)}, bf16[1,528,128]{2,1,0:T(8,128)(2,1)S(1)}, u32[]{:S(2)}, u32[]{:S(2)}) collective-permute-start(bf16[1,528,128]{2,1,0:T(8,128)(2,1)S(1)} %get-tuple-element.115), channel_id=1, source_target_pairs={{0,4},{4,0},{1,5},{5,1},{2,6},{6,2},{3,7},{7,3},{8,12},{12,8},{9,1... | collective-permute-start | bytes 405512 | tf_op jit(solution)/shard_map/ppermute | solution.py:311
  5.8 1.0 %collective-permute-done.refs_3_ = bf16[1,528,128]{2,1,0:T(8,128)(2,1)S(1)} collective-permute-done((bf16[1,528,128]{2,1,0:T(8,128)(2,1)S(1)}, bf16[1,528,128]{2,1,0:T(8,128)(2,1)S(1)}, u32[]{:S(2)}, u32[]{:S(2)}) %collective-permute-start) | collective-permute-done | bytes 135200 | tf_op jit(solution)/shard_map/ppermute | solution.py:311
  6.8 0.7 pad_maximum_fusion.1
  7.6 1.6 %shard_map.113 = (bf16[16,128,128]{2,1,0:T(8,128)(2,1)S(1)}, f32[16,128,128]{2,1,0:T(8,128)S(1)}) custom-call(f32[16]{0:T(128)S(1)} %copy-done.1, bf16[128,16,128]{2,1,0:T(8,128)(2,1)S(1)} %copy-done.3, bf16[128,16,128]{2,1,0:T(8,128)(2,1)S(1)} %copy-done.4), custom_call_target="tpu_custom_call" | custom-call | flops 1073741824 | bytes 4194304 | tf_op jit(solution)/shard_map/pallas_call | solution.py:338
  9.2 0.4 collective-permute-start.1
  9.7 1.0 %collective-permute-start.10 = (bf16[2,528,128]{2,1,0:T(8,128)(2,1)}, bf16[2,528,128]{2,1,0:T(8,128)(2,1)}, u32[]{:S(2)}, u32[]{:S(2)}) collective-permute-start(bf16[2,528,128]{2,1,0:T(8,128)(2,1)} %pad_maximum_fusion.1), channel_id=1, source_target_pairs={{0,72},{4,132},{8,80},{12,140},{16,88},{20,148},{24,96},{28,156},{... | collective-permute-start | bytes 811016 | tf_op jit(solution)/shard_map/ppermute | solution.py:295
  10.7 0.3 collective-permute-start.9
  11.0 0.1 stack.38.place.refs_0_
  11.1 0.1 collective-permute-done.1.other.before
  11.2 0.7 shard_map.114
  11.9 1.6 %collective-permute-start.2 = (bf16[2,128,128]{2,1,0:T(8,128)(2,1)S(1)}, bf16[2,128,128]{2,1,0:T(8,128)(2,1)S(1)}, u32[]{:S(2)}, u32[]{:S(2)}) collective-permute-start(bf16[2,128,128]{2,1,0:T(8,128)(2,1)S(1)} %get-tuple-element.65), channel_id=1, source_target_pairs={{0,8},{8,16},{16,24},{24,0},{1,9},{9,17},{17,25},{25,1},{2,10},{10... | collective-permute-start | bytes 196616 | tf_op jit(solution)/shard_map/ppermute | solution.py:307
  13.5 3.0 %collective-permute-start.3 = (bf16[2,128,128]{2,1,0:T(8,128)(2,1)S(1)}, bf16[2,128,128]{2,1,0:T(8,128)(2,1)S(1)}, u32[]{:S(2)}, u32[]{:S(2)}) collective-permute-start(bf16[2,128,128]{2,1,0:T(8,128)(2,1)S(1)} %get-tuple-element.66), channel_id=1, source_target_pairs={{0,16},{8,24},{16,0},{24,8},{1,17},{9,25},{17,1},{25,9},{2,18},{10... | collective-permute-start | bytes 196616 | tf_op jit(solution)/shard_map/ppermute | solution.py:307
  16.5 0.7 collective-permute-start.4
  17.2 2.0 %shard_map.115 = (f32[16,128,128]{2,1,0:T(8,128)S(1)}, bf16[16,128,128]{2,1,0:T(8,128)(2,1)S(1)}) custom-call(f32[16]{0:T(128)S(1)} %copy-done.1, bf16[128,16,128]{2,1,0:T(8,128)(2,1)S(1)} %copy-done.2, bf16[128,16,128]{2,1,0:T(8,128)(2,1)S(1)} %copy-done.3, bf16[128,16,128]{2,1,0:T(8,128)(2,1)S(1)} %copy-done.4), custom_call_target="tpu_custom_call" | custom-call | flops 1073741824 | bytes 4194304 | tf_op jit(solution)/shard_map/pallas_call | solution.py:345
  19.2 0.0 collective-permute-done.2.p1
  19.2 0.4 collective-permute-done.3.p2
  19.6 1.6 %collective-permute-done.4.p3 = bf16[2,128,128]{2,1,0:T(8,128)(2,1)S(1)} collective-permute-done((bf16[2,128,128]{2,1,0:T(8,128)(2,1)S(1)}, bf16[2,128,128]{2,1,0:T(8,128)(2,1)S(1)}, u32[]{:S(2)}, u32[]{:S(2)}) %collective-permute-start.4) | collective-permute-done | bytes 65568 | tf_op jit(solution)/shard_map/ppermute | solution.py:307
  21.3 0.6 shard_map.116
  21.9 5.9 %collective-permute-start.5 = (bf16[2,128,128]{2,1,0:T(8,128)(2,1)S(1)}, bf16[2,128,128]{2,1,0:T(8,128)(2,1)S(1)}, u32[]{:S(2)}, u32[]{:S(2)}) collective-permute-start(bf16[2,128,128]{2,1,0:T(8,128)(2,1)S(1)} %get-tuple-element.68), channel_id=1, source_target_pairs={{0,32},{32,0},{1,33},{33,1},{2,34},{34,2},{3,35},{35,3},{4,36},{36... | collective-permute-start | bytes 196616 | tf_op jit(solution)/shard_map/ppermute | solution.py:311
  27.8 1.1 %pad_maximum_fusion.refs_3_ = bf16[4,528,128]{2,1,0:T(8,128)(2,1)S(1)} fusion(bf16[2,528,128]{2,1,0:T(8,128)(2,1)} %collective-permute-done.10, bf16[2,528,128]{2,1,0:T(8,128)(2,1)} %collective-permute-done.9), kind=kLoop, calls=%fused_computation | loop fusion | flops 270336 | bytes 1081344 | tf_op jit(solution)/shard_map/concatenate | solution.py:363
  28.9 0.0 copy-start.6
  28.9 0.0 copy-done.5
  29.0 0.6 copy-done.6
  29.6 1.3 %shard_map.117 = (bf16[2,128,1024]{2,1,0:T(8,128)(2,1)S(1)}, f32[2,1,1024]{2,1,0:T(1,128)S(1)}, f32[2,1,1024]{2,1,0:T(1,128)S(1)}, f32[2,128,1024]{2,1,0:T(8,128)S(1)}) custom-call(s32[5]{0:T(128)S(1)} %stack.38.place.refs_0_, s32[1]{0:T(128)S(6)} %copy.14.refs_1_, s32[1,64]{1,0:T(1,128)S(1)} %copy-done.6, ...), custom_call_target="tpu_custom_call" | custom-call | flops 268435456 | bytes 4194304 | tf_op jit(solution)/shard_map/pallas_call | solution.py:173
  30.9 1.6 %collective-permute-start.11 = (bf16[4,528,128]{2,1,0:T(8,128)(2,1)S(1)}, bf16[4,528,128]{2,1,0:T(8,128)(2,1)S(1)}, u32[]{:S(2)}, u32[]{:S(2)}) collective-permute-start(bf16[4,528,128]{2,1,0:T(8,128)(2,1)S(1)} %pad_maximum_fusion.refs_3_), channel_id=1, source_target_pairs={{0,4},{4,0},{1,5},{5,1},{2,6},{6,2},{3,7},{7,3},{8,12},{12,8},{9,1... | collective-permute-start | bytes 1622024 | tf_op jit(solution)/shard_map/ppermute | solution.py:311
  32.5 9.6 %collective-permute-start.15 = (bf16[4,528,128]{2,1,0:T(8,128)(2,1)S(1)}, bf16[4,528,128]{2,1,0:T(8,128)(2,1)S(1)}, u32[]{:S(2)}, u32[]{:S(2)}) collective-permute-start(bf16[4,528,128]{2,1,0:T(8,128)(2,1)S(1)} %pad_maximum_fusion.refs_3_), channel_id=1, source_target_pairs={{0,8},{4,252},{8,16},{12,4},{16,24},{20,12},{24,32},{28,20},{32,40... | collective-permute-start | bytes 1622024 | tf_op jit(solution)/shard_map/ppermute | solution.py:295
  42.1 0.6 shard_map.118
  42.7 0.1 collective-permute-start.6
  42.8 1.4 %collective-permute-start.7 = (bf16[2,128,128]{2,1,0:T(8,128)(2,1)S(1)}, bf16[2,128,128]{2,1,0:T(8,128)(2,1)S(1)}, u32[]{:S(2)}, u32[]{:S(2)}) collective-permute-start(bf16[2,128,128]{2,1,0:T(8,128)(2,1)S(1)} %shard_map.118), channel_id=1, source_target_pairs={{0,128},{64,192},{128,0},{192,64},{1,129},{65,193},{129,1},{193,65... | collective-permute-start | bytes 196616 | tf_op jit(solution)/shard_map/ppermute | solution.py:299
  44.2 1.3 %collective-permute-start.8 = (bf16[2,128,128]{2,1,0:T(8,128)(2,1)S(1)}, bf16[2,128,128]{2,1,0:T(8,128)(2,1)S(1)}, u32[]{:S(2)}, u32[]{:S(2)}) collective-permute-start(bf16[2,128,128]{2,1,0:T(8,128)(2,1)S(1)} %shard_map.118), channel_id=1, source_target_pairs={{0,192},{64,0},{128,64},{192,128},{1,193},{65,1},{129,65},{193,129... | collective-permute-start | bytes 196616 | tf_op jit(solution)/shard_map/ppermute | solution.py:299
  45.5 0.8 %shard_map.119 = (f32[2,1,1024]{2,1,0:T(1,128)S(1)}, f32[2,1,1024]{2,1,0:T(1,128)S(1)}, f32[2,128,1024]{2,1,0:T(8,128)S(1)}) custom-call(s32[5]{0:T(128)S(1)} %stack.38.place.refs_0_, s32[1]{0:T(128)S(6)} %copy.14.refs_1_, s32[1,64]{1,0:T(1,128)S(1)} %copy-done.6, bf16[4,528,128]{2,1,0:T(8,128)(2,1)S(1)} %pad_maximum_fusion.refs_3_, ...), custom_call_target="tpu_custom_call" | custom-call | flops 2147483648 | bytes 4194304 | tf_op jit(solution)/shard_map/pallas_call | solution.py:173
  46.3 4.1 %collective-permute-done.6.x1 = bf16[2,128,128]{2,1,0:T(8,128)(2,1)S(1)} collective-permute-done((bf16[2,128,128]{2,1,0:T(8,128)(2,1)S(1)}, bf16[2,128,128]{2,1,0:T(8,128)(2,1)S(1)}, u32[]{:S(2)}, u32[]{:S(2)}) %collective-permute-start.6) | collective-permute-done | bytes 65568 | tf_op jit(solution)/shard_map/ppermute | solution.py:299
  50.5 0.0 collective-permute-done.8.x3
  50.5 0.0 collective-permute-done.15.refs_3_
  50.5 0.1 collective-permute-start.16
  50.6 6.5 %collective-permute-start.18 = (bf16[4,528,128]{2,1,0:T(8,128)(2,1)S(1)}, bf16[4,528,128]{2,1,0:T(8,128)(2,1)S(1)}, u32[]{:S(2)}, u32[]{:S(2)}) collective-permute-start(bf16[4,528,128]{2,1,0:T(8,128)(2,1)S(1)} %collective-permute-done.15.refs_3_), channel_id=1, source_target_pairs={{0,8},{4,252},{8,16},{12,4},{16,24},{20,12},{24,32},{28,20},{32,40... | collective-permute-start | bytes 1622024 | tf_op jit(solution)/shard_map/ppermute | solution.py:295
  57.1 0.8 %shard_map.120 = (bf16[2,128,128]{2,1,0:T(8,128)(2,1)S(1)}, bf16[2,128,128]{2,1,0:T(8,128)(2,1)S(1)}, bf16[2,128,128]{2,1,0:T(8,128)(2,1)S(1)}, bf16[2,128,128]{2,1,0:T(8,128)(2,1)S(1)}) custom-call(s32[5]{0:T(128)S(1)} %stack.38.place.refs_0_, f32[16]{0:T(128)S(1)} %copy-done.1, bf16[2,128,128]{2,1,0:T(8,128)(2,1)S(1)} %get-tuple-element.61.p0, ...), custom_call_target="tpu_custom_call" | custom-call | bytes 4194304 | tf_op jit(solution)/shard_map/pallas_call | solution.py:375
  57.9 0.1 collective-permute-start.12
  58.0 0.1 collective-permute-start.13
  58.1 3.2 %collective-permute-start.14 = (bf16[2,128,128]{2,1,0:T(8,128)(2,1)S(1)}, bf16[2,128,128]{2,1,0:T(8,128)(2,1)S(1)}, u32[]{:S(2)}, u32[]{:S(2)}) collective-permute-start(bf16[2,128,128]{2,1,0:T(8,128)(2,1)S(1)} %get-tuple-element.89), channel_id=1, source_target_pairs={{0,24},{8,0},{16,8},{24,16},{1,25},{9,1},{17,9},{25,17},{2,26},{10... | collective-permute-start | bytes 196616 | tf_op jit(solution)/shard_map/ppermute | solution.py:307
  61.3 0.0 collective-permute-done.16.refs_4_
  61.3 0.8 %shard_map.121 = (f32[2,1,1024]{2,1,0:T(1,128)S(1)}, f32[2,1,1024]{2,1,0:T(1,128)S(1)}, f32[2,128,1024]{2,1,0:T(8,128)S(1)}) custom-call(s32[5]{0:T(128)S(1)} %stack.38.place.refs_0_, s32[1]{0:T(128)S(6)} %copy.14.refs_1_, s32[1,64]{1,0:T(1,128)S(1)} %copy-done.6, bf16[4,528,128]{2,1,0:T(8,128)(2,1)S(1)} %collective-permute-done.15.refs_3_, ...), custom_call_target="tpu_custom_call" | custom-call | flops 2147483648 | bytes 4194304 | tf_op jit(solution)/shard_map/pallas_call | solution.py:173
  62.1 1.2 %collective-permute-done.18.refs_3_ = bf16[4,528,128]{2,1,0:T(8,128)(2,1)S(1)} collective-permute-done((bf16[4,528,128]{2,1,0:T(8,128)(2,1)S(1)}, bf16[4,528,128]{2,1,0:T(8,128)(2,1)S(1)}, u32[]{:S(2)}, u32[]{:S(2)}) %collective-permute-start.18) | collective-permute-done | bytes 540704 | tf_op jit(solution)/shard_map/ppermute | solution.py:295
  63.4 1.3 %collective-permute-start.20 = (bf16[4,528,128]{2,1,0:T(8,128)(2,1)S(1)}, bf16[4,528,128]{2,1,0:T(8,128)(2,1)S(1)}, u32[]{:S(2)}, u32[]{:S(2)}) collective-permute-start(bf16[4,528,128]{2,1,0:T(8,128)(2,1)S(1)} %collective-permute-done.18.refs_3_), channel_id=1, source_target_pairs={{0,4},{4,0},{1,5},{5,1},{2,6},{6,2},{3,7},{7,3},{8,12},{12,8},{9,1... | collective-permute-start | bytes 1622024 | tf_op jit(solution)/shard_map/ppermute | solution.py:311
  64.8 0.1 collective-permute-start.17
  64.9 5.9 %collective-permute-start.19 = (bf16[4,528,128]{2,1,0:T(8,128)(2,1)S(1)}, bf16[4,528,128]{2,1,0:T(8,128)(2,1)S(1)}, u32[]{:S(2)}, u32[]{:S(2)}) collective-permute-start(bf16[4,528,128]{2,1,0:T(8,128)(2,1)S(1)} %collective-permute-done.18.refs_3_), channel_id=1, source_target_pairs={{0,8},{4,252},{8,16},{12,4},{16,24},{20,12},{24,32},{28,20},{32,40... | collective-permute-start | bytes 1622024 | tf_op jit(solution)/shard_map/ppermute | solution.py:295
  70.8 0.0 collective-permute-done.17.far
  70.8 1.3 %shard_map.122 = (f32[16,128,128]{2,1,0:T(8,128)S(1)}, f32[8,128]{1,0:T(8,128)S(1)}) custom-call(s32[5]{0:T(128)S(1)} %stack.38.place.refs_0_, f32[16]{0:T(128)S(1)} %copy-done.1, f32[16,128,128]{2,1,0:T(8,128)S(1)} %get-tuple-element.63.inner, bf16[16,128,128]{2,1,0:T(8,128)(2,1)S(1)} %get-tuple-element.64.q, ...), custom_call_target="tpu_custom_call" | custom-call | flops 1073741824 | bytes 4194304 | tf_op jit(solution)/shard_map/pallas_call | solution.py:386
  72.1 1.4 %collective-permute-start.21 = (f32[8,128]{1,0:T(8,128)S(1)}, f32[8,128]{1,0:T(8,128)S(1)}, u32[]{:S(2)}, u32[]{:S(2)}) collective-permute-start(f32[8,128]{1,0:T(8,128)S(1)} %get-tuple-element.102.own), channel_id=1, source_target_pairs={{0,1},{1,2},{2,3},{3,0},{4,5},{5,6},{6,7},{7,4},{8,9},{9,10},{10,1... | collective-permute-start | bytes 12296 | tf_op jit(solution)/shard_map/ppermute | solution.py:303
  73.5 2.6 %collective-permute-start.22 = (f32[8,128]{1,0:T(8,128)S(1)}, f32[8,128]{1,0:T(8,128)S(1)}, u32[]{:S(2)}, u32[]{:S(2)}) collective-permute-start(f32[8,128]{1,0:T(8,128)S(1)} %get-tuple-element.102.own), channel_id=1, source_target_pairs={{0,2},{1,3},{2,0},{3,1},{4,6},{5,7},{6,4},{7,5},{8,10},{9,11},{10,... | collective-permute-start | bytes 12296 | tf_op jit(solution)/shard_map/ppermute | solution.py:303
  76.1 1.1 %collective-permute-start.23 = (f32[8,128]{1,0:T(8,128)S(1)}, f32[8,128]{1,0:T(8,128)S(1)}, u32[]{:S(2)}, u32[]{:S(2)}) collective-permute-start(f32[8,128]{1,0:T(8,128)S(1)} %get-tuple-element.102.own), channel_id=1, source_target_pairs={{0,3},{1,0},{2,1},{3,2},{4,7},{5,4},{6,5},{7,6},{8,11},{9,8},{10,9... | collective-permute-start | bytes 12296 | tf_op jit(solution)/shard_map/ppermute | solution.py:303
  77.2 0.0 collective-permute-done.20.refs_4_
  77.2 1.1 %shard_map.123 = (f32[2,1,1024]{2,1,0:T(1,128)S(1)}, f32[2,1,1024]{2,1,0:T(1,128)S(1)}, f32[2,128,1024]{2,1,0:T(8,128)S(1)}) custom-call(s32[5]{0:T(128)S(1)} %stack.38.place.refs_0_, s32[1]{0:T(128)S(6)} %copy.14.refs_1_, s32[1,64]{1,0:T(1,128)S(1)} %copy-done.6, bf16[4,528,128]{2,1,0:T(8,128)(2,1)S(1)} %collective-permute-done.18.refs_3_, ...), custom_call_target="tpu_custom_call" | custom-call | flops 2147483648 | bytes 4194304 | tf_op jit(solution)/shard_map/pallas_call | solution.py:173
  78.3 0.0 collective-permute-done.21.s1
  78.3 0.3 collective-permute-done.23.s3
  78.6 1.9 %collective-permute-done.24.refs_4_ = bf16[4,528,128]{2,1,0:T(8,128)(2,1)S(1)} collective-permute-done((bf16[4,528,128]{2,1,0:T(8,128)(2,1)S(1)}, bf16[4,528,128]{2,1,0:T(8,128)(2,1)S(1)}, u32[]{:S(2)}, u32[]{:S(2)}) %collective-permute-start.24) | collective-permute-done | bytes 540704 | tf_op jit(solution)/shard_map/ppermute | solution.py:311
  80.5 1.9 %shard_map.124 = bf16[128,16,128]{2,1,0:T(8,128)(2,1)} custom-call(s32[5]{0:T(128)S(1)} %stack.38.place.refs_0_, s32[1]{0:T(128)S(6)} %copy.14.refs_1_, s32[1,64]{1,0:T(1,128)S(1)} %copy-done.6, bf16[4,528,128]{2,1,0:T(8,128)(2,1)S(1)} %collective-permute-done.19.refs_3_, bf16[4,528,128]{2,1,0:T(8,128)(2,1)S(1)} %collective-permute-done.24.refs_4_, ...), custom_call_target="tpu_custom_call" | custom-call | flops 2147483648 | bytes 4194304 | tf_op jit(solution)/shard_map/pallas_call | solution.py:173
  82.4 1.3 %shard_map.125 = bf16[128,16,128]{2,1,0:T(8,128)(2,1)} custom-call(f32[16,128,128]{2,1,0:T(8,128)S(1)} %get-tuple-element.113.mixed, f32[8,128]{1,0:T(8,128)S(1)} %get-tuple-element.102.own, f32[8,128]{1,0:T(8,128)S(1)} %collective-permute-done.21.s1, f32[8,128]{1,0:T(8,128)S(1)} %collective-permute-done.22.s2, f32[8,128]{1,0:T(8,128)S(1)} %collective-permute-done.23.s3, ...), custom_call_target="tpu_custom_call" | custom-call | bytes 4194304 | tf_op jit(solution)/shard_map/pallas_call | solution.py:397
  (24 shorter events, 0.1 us)
Async XLA Ops:
  1.3 0.9 %copy-start.7 = (bf16[128,2,128]{2,1,0:T(2,128)(2,1)S(1)}, bf16[128,2,128]{2,1,0:T(2,128)(2,1)}, u32[]{:S(2)}) copy-start(bf16[128,2,128]{2,1,0:T(2,128)(2,1)} %param.17) | copy-start | bytes 196612
  2.2 5.4 %copy-start.3 = (bf16[128,16,128]{2,1,0:T(8,128)(2,1)S(1)}, bf16[128,16,128]{2,1,0:T(8,128)(2,1)}, u32[]{:S(2)}) copy-start(bf16[128,16,128]{2,1,0:T(8,128)(2,1)} %k_in.2) | copy-start | bytes 1572868
  2.2 5.4 %copy-start.4 = (bf16[128,16,128]{2,1,0:T(8,128)(2,1)S(1)}, bf16[128,16,128]{2,1,0:T(8,128)(2,1)}, u32[]{:S(2)}) copy-start(bf16[128,16,128]{2,1,0:T(8,128)(2,1)} %v_in.3) | copy-start | bytes 1572868
  2.5 5.1 %copy-start.1 = (f32[16]{0:T(128)S(1)}, f32[16]{0:T(128)}, u32[]{:S(2)}) copy-start(f32[16]{0:T(128)} %rate.13) | copy-start | bytes 196
  2.5 4.3 %collective-permute-start = (bf16[1,528,128]{2,1,0:T(8,128)(2,1)S(1)}, bf16[1,528,128]{2,1,0:T(8,128)(2,1)S(1)}, u32[]{:S(2)}, u32[]{:S(2)}) collective-permute-start(bf16[1,528,128]{2,1,0:T(8,128)(2,1)S(1)} %get-tuple-element.115), channel_id=1, source_target_pairs={{0,4},{4,0},{1,5},{5,1},{2,6},{6,2},{3,7},{7,3},{8,12},{12,8},{9,1... | collective-permute-start | bytes 405512 | tf_op jit(solution)/shard_map/ppermute | solution.py:311
  9.2 2.0 %collective-permute-start.1 = (bf16[16,128,128]{2,1,0:T(8,128)(2,1)S(1)}, bf16[16,128,128]{2,1,0:T(8,128)(2,1)S(1)}, u32[]{:S(2)}, u32[]{:S(2)}) collective-permute-start(bf16[16,128,128]{2,1,0:T(8,128)(2,1)S(1)} %get-tuple-element.60), channel_id=1, source_target_pairs={{0,4},{4,0},{1,5},{5,1},{2,6},{6,2},{3,7},{7,3},{8,12},{12,8},{9,1... | collective-permute-start | bytes 1572872 | tf_op jit(solution)/shard_map/ppermute | solution.py:311
  9.7 18.1 %collective-permute-start.10 = (bf16[2,528,128]{2,1,0:T(8,128)(2,1)}, bf16[2,528,128]{2,1,0:T(8,128)(2,1)}, u32[]{:S(2)}, u32[]{:S(2)}) collective-permute-start(bf16[2,528,128]{2,1,0:T(8,128)(2,1)} %pad_maximum_fusion.1), channel_id=1, source_target_pairs={{0,72},{4,132},{8,80},{12,140},{16,88},{20,148},{24,96},{28,156},{... | collective-permute-start | bytes 811016 | tf_op jit(solution)/shard_map/ppermute | solution.py:295
  10.7 17.1 %collective-permute-start.9 = (bf16[2,528,128]{2,1,0:T(8,128)(2,1)}, bf16[2,528,128]{2,1,0:T(8,128)(2,1)}, u32[]{:S(2)}, u32[]{:S(2)}) collective-permute-start(bf16[2,528,128]{2,1,0:T(8,128)(2,1)} %pad_maximum_fusion.1), channel_id=1, source_target_pairs={{0,8},{4,68},{8,16},{12,76},{16,24},{20,84},{24,32},{28,92},{32,40... | collective-permute-start | bytes 811016 | tf_op jit(solution)/shard_map/ppermute | solution.py:295
  11.2 6.0 %copy-start.2 = (bf16[128,16,128]{2,1,0:T(8,128)(2,1)S(1)}, bf16[128,16,128]{2,1,0:T(8,128)(2,1)}, u32[]{:S(2)}) copy-start(bf16[128,16,128]{2,1,0:T(8,128)(2,1)} %q_in) | copy-start | bytes 1572868
  11.9 7.3 %collective-permute-start.2 = (bf16[2,128,128]{2,1,0:T(8,128)(2,1)S(1)}, bf16[2,128,128]{2,1,0:T(8,128)(2,1)S(1)}, u32[]{:S(2)}, u32[]{:S(2)}) collective-permute-start(bf16[2,128,128]{2,1,0:T(8,128)(2,1)S(1)} %get-tuple-element.65), channel_id=1, source_target_pairs={{0,8},{8,16},{16,24},{24,0},{1,9},{9,17},{17,25},{25,1},{2,10},{10... | collective-permute-start | bytes 196616 | tf_op jit(solution)/shard_map/ppermute | solution.py:307
  13.5 6.2 %collective-permute-start.3 = (bf16[2,128,128]{2,1,0:T(8,128)(2,1)S(1)}, bf16[2,128,128]{2,1,0:T(8,128)(2,1)S(1)}, u32[]{:S(2)}, u32[]{:S(2)}) collective-permute-start(bf16[2,128,128]{2,1,0:T(8,128)(2,1)S(1)} %get-tuple-element.66), channel_id=1, source_target_pairs={{0,16},{8,24},{16,0},{24,8},{1,17},{9,25},{17,1},{25,9},{2,18},{10... | collective-permute-start | bytes 196616 | tf_op jit(solution)/shard_map/ppermute | solution.py:307
  16.5 4.8 %collective-permute-start.4 = (bf16[2,128,128]{2,1,0:T(8,128)(2,1)S(1)}, bf16[2,128,128]{2,1,0:T(8,128)(2,1)S(1)}, u32[]{:S(2)}, u32[]{:S(2)}) collective-permute-start(bf16[2,128,128]{2,1,0:T(8,128)(2,1)S(1)} %get-tuple-element.67), channel_id=1, source_target_pairs={{0,24},{8,0},{16,8},{24,16},{1,25},{9,1},{17,9},{25,17},{2,26},{10... | collective-permute-start | bytes 196616 | tf_op jit(solution)/shard_map/ppermute | solution.py:307
  21.9 9.0 %collective-permute-start.5 = (bf16[2,128,128]{2,1,0:T(8,128)(2,1)S(1)}, bf16[2,128,128]{2,1,0:T(8,128)(2,1)S(1)}, u32[]{:S(2)}, u32[]{:S(2)}) collective-permute-start(bf16[2,128,128]{2,1,0:T(8,128)(2,1)S(1)} %get-tuple-element.68), channel_id=1, source_target_pairs={{0,32},{32,0},{1,33},{33,1},{2,34},{34,2},{3,35},{35,3},{4,36},{36... | collective-permute-start | bytes 196616 | tf_op jit(solution)/shard_map/ppermute | solution.py:311
  27.8 1.2 %copy-start.5 = (bf16[128,16,128]{2,1,0:T(8,128)(2,1)S(1)}, bf16[128,16,128]{2,1,0:T(8,128)(2,1)}, u32[]{:S(2)}) copy-start(bf16[128,16,128]{2,1,0:T(8,128)(2,1)} %refs_4_) | copy-start | bytes 1572868
  28.9 0.7 copy-start.6
  30.9 14.6 %collective-permute-start.11 = (bf16[4,528,128]{2,1,0:T(8,128)(2,1)S(1)}, bf16[4,528,128]{2,1,0:T(8,128)(2,1)S(1)}, u32[]{:S(2)}, u32[]{:S(2)}) collective-permute-start(bf16[4,528,128]{2,1,0:T(8,128)(2,1)S(1)} %pad_maximum_fusion.refs_3_), channel_id=1, source_target_pairs={{0,4},{4,0},{1,5},{5,1},{2,6},{6,2},{3,7},{7,3},{8,12},{12,8},{9,1... | collective-permute-start | bytes 1622024 | tf_op jit(solution)/shard_map/ppermute | solution.py:311
  32.5 18.0 %collective-permute-start.15 = (bf16[4,528,128]{2,1,0:T(8,128)(2,1)S(1)}, bf16[4,528,128]{2,1,0:T(8,128)(2,1)S(1)}, u32[]{:S(2)}, u32[]{:S(2)}) collective-permute-start(bf16[4,528,128]{2,1,0:T(8,128)(2,1)S(1)} %pad_maximum_fusion.refs_3_), channel_id=1, source_target_pairs={{0,8},{4,252},{8,16},{12,4},{16,24},{20,12},{24,32},{28,20},{32,40... | collective-permute-start | bytes 1622024 | tf_op jit(solution)/shard_map/ppermute | solution.py:295
  42.7 7.7 %collective-permute-start.6 = (bf16[2,128,128]{2,1,0:T(8,128)(2,1)S(1)}, bf16[2,128,128]{2,1,0:T(8,128)(2,1)S(1)}, u32[]{:S(2)}, u32[]{:S(2)}) collective-permute-start(bf16[2,128,128]{2,1,0:T(8,128)(2,1)S(1)} %shard_map.118), channel_id=1, source_target_pairs={{0,64},{64,128},{128,192},{192,0},{1,65},{65,129},{129,193},{193,1... | collective-permute-start | bytes 196616 | tf_op jit(solution)/shard_map/ppermute | solution.py:299
  42.8 7.7 %collective-permute-start.7 = (bf16[2,128,128]{2,1,0:T(8,128)(2,1)S(1)}, bf16[2,128,128]{2,1,0:T(8,128)(2,1)S(1)}, u32[]{:S(2)}, u32[]{:S(2)}) collective-permute-start(bf16[2,128,128]{2,1,0:T(8,128)(2,1)S(1)} %shard_map.118), channel_id=1, source_target_pairs={{0,128},{64,192},{128,0},{192,64},{1,129},{65,193},{129,1},{193,65... | collective-permute-start | bytes 196616 | tf_op jit(solution)/shard_map/ppermute | solution.py:299
  44.2 6.3 %collective-permute-start.8 = (bf16[2,128,128]{2,1,0:T(8,128)(2,1)S(1)}, bf16[2,128,128]{2,1,0:T(8,128)(2,1)S(1)}, u32[]{:S(2)}, u32[]{:S(2)}) collective-permute-start(bf16[2,128,128]{2,1,0:T(8,128)(2,1)S(1)} %shard_map.118), channel_id=1, source_target_pairs={{0,192},{64,0},{128,64},{192,128},{1,193},{65,1},{129,65},{193,129... | collective-permute-start | bytes 196616 | tf_op jit(solution)/shard_map/ppermute | solution.py:299
  50.5 10.8 %collective-permute-start.16 = (bf16[4,528,128]{2,1,0:T(8,128)(2,1)S(1)}, bf16[4,528,128]{2,1,0:T(8,128)(2,1)S(1)}, u32[]{:S(2)}, u32[]{:S(2)}) collective-permute-start(bf16[4,528,128]{2,1,0:T(8,128)(2,1)S(1)} %collective-permute-done.15.refs_3_), channel_id=1, source_target_pairs={{0,4},{4,0},{1,5},{5,1},{2,6},{6,2},{3,7},{7,3},{8,12},{12,8},{9,1... | collective-permute-start | bytes 1622024 | tf_op jit(solution)/shard_map/ppermute | solution.py:311
  50.6 12.8 %collective-permute-start.18 = (bf16[4,528,128]{2,1,0:T(8,128)(2,1)S(1)}, bf16[4,528,128]{2,1,0:T(8,128)(2,1)S(1)}, u32[]{:S(2)}, u32[]{:S(2)}) collective-permute-start(bf16[4,528,128]{2,1,0:T(8,128)(2,1)S(1)} %collective-permute-done.15.refs_3_), channel_id=1, source_target_pairs={{0,8},{4,252},{8,16},{12,4},{16,24},{20,12},{24,32},{28,20},{32,40... | collective-permute-start | bytes 1622024 | tf_op jit(solution)/shard_map/ppermute | solution.py:295
  57.9 6.8 %collective-permute-start.12 = (bf16[2,128,128]{2,1,0:T(8,128)(2,1)S(1)}, bf16[2,128,128]{2,1,0:T(8,128)(2,1)S(1)}, u32[]{:S(2)}, u32[]{:S(2)}) collective-permute-start(bf16[2,128,128]{2,1,0:T(8,128)(2,1)S(1)} %get-tuple-element.87), channel_id=1, source_target_pairs={{0,8},{8,16},{16,24},{24,0},{1,9},{9,17},{17,25},{25,1},{2,10},{10... | collective-permute-start | bytes 196616 | tf_op jit(solution)/shard_map/ppermute | solution.py:307
  58.0 6.7 %collective-permute-start.13 = (bf16[2,128,128]{2,1,0:T(8,128)(2,1)S(1)}, bf16[2,128,128]{2,1,0:T(8,128)(2,1)S(1)}, u32[]{:S(2)}, u32[]{:S(2)}) collective-permute-start(bf16[2,128,128]{2,1,0:T(8,128)(2,1)S(1)} %get-tuple-element.88), channel_id=1, source_target_pairs={{0,16},{8,24},{16,0},{24,8},{1,17},{9,25},{17,1},{25,9},{2,18},{10... | collective-permute-start | bytes 196616 | tf_op jit(solution)/shard_map/ppermute | solution.py:307
  58.1 6.6 %collective-permute-start.14 = (bf16[2,128,128]{2,1,0:T(8,128)(2,1)S(1)}, bf16[2,128,128]{2,1,0:T(8,128)(2,1)S(1)}, u32[]{:S(2)}, u32[]{:S(2)}) collective-permute-start(bf16[2,128,128]{2,1,0:T(8,128)(2,1)S(1)} %get-tuple-element.89), channel_id=1, source_target_pairs={{0,24},{8,0},{16,8},{24,16},{1,25},{9,1},{17,9},{25,17},{2,26},{10... | collective-permute-start | bytes 196616 | tf_op jit(solution)/shard_map/ppermute | solution.py:307
  63.4 13.8 %collective-permute-start.20 = (bf16[4,528,128]{2,1,0:T(8,128)(2,1)S(1)}, bf16[4,528,128]{2,1,0:T(8,128)(2,1)S(1)}, u32[]{:S(2)}, u32[]{:S(2)}) collective-permute-start(bf16[4,528,128]{2,1,0:T(8,128)(2,1)S(1)} %collective-permute-done.18.refs_3_), channel_id=1, source_target_pairs={{0,4},{4,0},{1,5},{5,1},{2,6},{6,2},{3,7},{7,3},{8,12},{12,8},{9,1... | collective-permute-start | bytes 1622024 | tf_op jit(solution)/shard_map/ppermute | solution.py:311
  64.8 6.0 %collective-permute-start.17 = (bf16[4,2,128,128]{3,2,1,0:T(8,128)(2,1)S(1)}, bf16[4,2,128,128]{3,2,1,0:T(8,128)(2,1)S(1)}, u32[]{:S(2)}, u32[]{:S(2)}) collective-permute-start(bf16[4,2,128,128]{3,2,1,0:T(8,128)(2,1)S(1)} %pad_maximum_fusion.2.near), channel_id=1, source_target_pairs={{0,4},{4,0},{1,5},{5,1},{2,6},{6,2},{3,7},{7,3},{8,12},{12,8},{9,1... | collective-permute-start | bytes 786440 | tf_op jit(solution)/shard_map/ppermute | solution.py:311
  64.9 13.7 %collective-permute-start.19 = (bf16[4,528,128]{2,1,0:T(8,128)(2,1)S(1)}, bf16[4,528,128]{2,1,0:T(8,128)(2,1)S(1)}, u32[]{:S(2)}, u32[]{:S(2)}) collective-permute-start(bf16[4,528,128]{2,1,0:T(8,128)(2,1)S(1)} %collective-permute-done.18.refs_3_), channel_id=1, source_target_pairs={{0,8},{4,252},{8,16},{12,4},{16,24},{20,12},{24,32},{28,20},{32,40... | collective-permute-start | bytes 1622024 | tf_op jit(solution)/shard_map/ppermute | solution.py:295
  72.1 6.1 %collective-permute-start.21 = (f32[8,128]{1,0:T(8,128)S(1)}, f32[8,128]{1,0:T(8,128)S(1)}, u32[]{:S(2)}, u32[]{:S(2)}) collective-permute-start(f32[8,128]{1,0:T(8,128)S(1)} %get-tuple-element.102.own), channel_id=1, source_target_pairs={{0,1},{1,2},{2,3},{3,0},{4,5},{5,6},{6,7},{7,4},{8,9},{9,10},{10,1... | collective-permute-start | bytes 12296 | tf_op jit(solution)/shard_map/ppermute | solution.py:303
  73.5 4.8 %collective-permute-start.22 = (f32[8,128]{1,0:T(8,128)S(1)}, f32[8,128]{1,0:T(8,128)S(1)}, u32[]{:S(2)}, u32[]{:S(2)}) collective-permute-start(f32[8,128]{1,0:T(8,128)S(1)} %get-tuple-element.102.own), channel_id=1, source_target_pairs={{0,2},{1,3},{2,0},{3,1},{4,6},{5,7},{6,4},{7,5},{8,10},{9,11},{10,... | collective-permute-start | bytes 12296 | tf_op jit(solution)/shard_map/ppermute | solution.py:303
  76.1 2.5 %collective-permute-start.23 = (f32[8,128]{1,0:T(8,128)S(1)}, f32[8,128]{1,0:T(8,128)S(1)}, u32[]{:S(2)}, u32[]{:S(2)}) collective-permute-start(f32[8,128]{1,0:T(8,128)S(1)} %get-tuple-element.102.own), channel_id=1, source_target_pairs={{0,3},{1,0},{2,1},{3,2},{4,7},{5,4},{6,5},{7,6},{8,11},{9,8},{10,9... | collective-permute-start | bytes 12296 | tf_op jit(solution)/shard_map/ppermute | solution.py:303
  78.6 3.8 %copy-start = (f32[16,128]{1,0:T(8,128)S(1)}, f32[16,128]{1,0:T(8,128)}, u32[]{:S(2)}) copy-start(f32[16,128]{1,0:T(8,128)} %gain.1) | copy-start | bytes 24580
  78.6 1.9 %collective-permute-start.24 = (bf16[4,528,128]{2,1,0:T(8,128)(2,1)S(1)}, bf16[4,528,128]{2,1,0:T(8,128)(2,1)S(1)}, u32[]{:S(2)}, u32[]{:S(2)}) collective-permute-start(bf16[4,528,128]{2,1,0:T(8,128)(2,1)S(1)} %collective-permute-done.19.refs_3_), channel_id=1, source_target_pairs={{0,4},{4,0},{1,5},{5,1},{2,6},{6,2},{3,7},{7,3},{8,12},{12,8},{9,1... | collective-permute-start | bytes 1622024 | tf_op jit(solution)/shard_map/ppermute | solution.py:311

commit v3 on v2

--- a/solution.py
+++ b/solution.py
@@ -212,7 +212,7 @@
     core, zl = place[1], place[2]
     first = core == 0
     for s, out in enumerate(slices):
-        owner = lax.rem(zl + s, 4)
+        owner = jnp.bitwise_xor(zl, s)
         for i in range(2):
             h = core * (LOCAL // 2) + 2 * owner + i
             fade = power(rate[h], TILE)
@@ -226,34 +226,36 @@
         r = rate[core * (LOCAL // 2) + 2 * zl + i]
         row = jnp.zeros((D, D), f32)
         for s, piece in enumerate((p0, p1, p2, p3)):
-            source = lax.rem(zl + 4 - s, 4)
+            source = jnp.bitwise_xor(zl, s)
             row += piece[i].astype(f32) * power(r, ((3 - source) * 2 * TILE).astype(f32))
         total[i] = row
         sent[i] = row.astype(bf16)
 
 
-def eight_body(place, rate, four, other, out):
-    core, zl, zh = place[1], place[2], place[3]
-    for i in range(2):
-        fade = power(rate[core * (LOCAL // 2) + 2 * zl + i], 8 * TILE)
-        mine, rest = four[i], other[i].astype(f32)
-        out[i] = jnp.where(zh == 0, fade * mine + rest, mine + fade * rest).astype(bf16)
-
-
-def entering_body(place, rate, p0, p1, p2, p3, other, x1, x2, x3, *slices):
+def row_body(place, rate, four, x1, x2, x3, own, out):
     core, zl, zh, x = place[1], place[2], place[3], place[4]
     for i in range(2):
         r = rate[core * (LOCAL // 2) + 2 * zl + i]
         earlier = jnp.zeros((D, D), f32)
-        for k, part in ((3, x3), (2, x2), (1, x1)):
-            earlier = earlier * power(r, 16 * TILE) + jnp.where(x >= k, part[i].astype(f32), 0.0)
-        earlier = jnp.where(zh == 1, power(r, 8 * TILE) * earlier + other[i].astype(f32), earlier)
+        for k, part in ((1, x1), (2, x2), (3, x3)):
+            source = jnp.bitwise_xor(x, k)
+            fade = power(r, (jnp.maximum(x - 1 - source, 0) * 16 * TILE).astype(f32))
+            earlier += jnp.where(source < x, part[i].astype(f32) * fade, 0.0)
+        own[i] = power(r, 8 * TILE) * earlier
+        out[i] = jnp.where(zh == 0, power(r, 16 * TILE) * earlier + four[i], earlier).astype(bf16)
+
+
+def entering_body(place, rate, p0, p1, p2, p3, own, other, *slices):
+    core, zl = place[1], place[2]
+    for i in range(2):
+        r = rate[core * (LOCAL // 2) + 2 * zl + i]
+        earlier = own[i] + other[i].astype(f32)
         pieces = [p[i].astype(f32) for p in (p0, p1, p2, p3)]
         for t, out in enumerate(slices):
-            target = lax.rem(zl + t, 4)
+            target = jnp.bitwise_xor(zl, t)
             state = earlier * power(r, (target * 2 * TILE).astype(f32))
             for s, piece in enumerate(pieces):
-                source = lax.rem(zl + 4 - s, 4)
+                source = jnp.bitwise_xor(zl, s)
                 fade = power(r, (jnp.maximum(target - 1 - source, 0) * 2 * TILE).astype(f32))
                 state += jnp.where(source < target, piece * fade, 0.0)
             out[i] = state.astype(bf16)
@@ -266,7 +268,7 @@
     squares[...] = jnp.zeros_like(squares)
     for half, source in ((core, near), (1 - core, far)):
         for s in range(4):
-            owner = lax.rem(zl + 4 - s, 4)
+            owner = jnp.bitwise_xor(zl, s)
             for i in range(2):
                 h = half * (LOCAL // 2) + 2 * owner + i
                 r = rate[h]
@@ -295,16 +297,8 @@
     return lax.ppermute(value, (*CHIPS, "core"), pairs)
 
 
-def x_shift(value, steps):
-    return lax.ppermute(value, "x", [(i, (i + steps) % 4) for i in range(4)])
-
-
-def head_shift(value, steps):
-    return lax.ppermute(value, "head", [(i, (i + steps) % 4) for i in range(4)])
-
-
-def zl_shift(value, steps):
-    return lax.ppermute(value, "zl", [(i, (i + steps) % 4) for i in range(4)])
+def trade(value, axis, bits):
+    return lax.ppermute(value, axis, [(i, i ^ bits) for i in range(4)])
 
 
 def swap(value, axis="core"):
@@ -340,7 +334,7 @@
     )(decay_rate, after(lin_k, both), lin_v)
     other_state = swap(state_high)
     slices = call(chip_body, [shape(pair, bf16)] * 4, [SMEM, SMEM, VMEM, VMEM])(place, decay_rate, state, other_state)
-    pieces = [slices[0]] + [zl_shift(slices[k], k) for k in (1, 2, 3)]
+    pieces = [slices[0]] + [trade(slices[k], "zl", k) for k in (1, 2, 3)]
 
     inner, query = call(
         inner_body, [shape(heads, f32), shape(heads, bf16)], [SMEM, VMEM, VMEM, VMEM], [big] * 3, flops=1 << 30
@@ -349,7 +343,7 @@
     row4, row4_sent = call(four_body, [shape(pair, f32), shape(pair, bf16)], [SMEM, SMEM] + [VMEM] * 4)(
         place, decay_rate, *pieces
     )
-    row4_other = swap(row4_sent, "zh")
+    earlier = [trade(row4_sent, "x", k) for k in (1, 2, 3)]
 
     def attend(blocks, groups, **state):
         return flash(place, doc_ids, block_mask, blocks, groups, **state)
@@ -360,22 +354,24 @@
 
     qt, *flow = attend([mate], [(((0, 0),), True)], first=(after(soft_q, row4_sent), block[0]))
     row4 = after(row4, flow[0])
-    carried = after(jnp.concatenate(after(arrived, query, row4_sent), axis=0), row4_other, flow[0])
+    carried = after(jnp.concatenate(after(arrived, query, row4_sent), axis=0), flow[0], *earlier)
     chips0 = parts(0)
     carried = two_ways(carried, 1, -1)
 
-    row8 = call(eight_body, shape(pair, bf16), [SMEM, SMEM, VMEM, VMEM])(place, decay_rate, row4, row4_other)
-    earlier = [x_shift(row8, k) for k in (1, 2, 3)]
-    flow = attend(*chips0, state=(qt, *after(tuple(flow), row8)))
-    earlier = after(tuple(earlier), flow[0])
-    carried = after(carried, *earlier)
+    row_own, row_sent = call(row_body, [shape(pair, f32), shape(pair, bf16)], [SMEM, SMEM] + [VMEM] * 4)(
+        place, decay_rate, row4, *earlier
+    )
+    row_other = swap(row_sent, "zh")
+    flow = attend(*chips0, state=(qt, *after(tuple(flow), row_sent)))
+    row_other = after(row_other, flow[0])
+    carried = after(carried, row_other)
     chips1 = parts(1)
     carried = two_ways(carried, 1, -1)
 
-    entering = call(entering_body, [shape(pair, bf16)] * 4, [SMEM, SMEM] + [VMEM] * 8)(
-        place, decay_rate, *pieces, row4_other, *earlier
-    )
-    near = jnp.stack([entering[0]] + [zl_shift(entering[k], k) for k in (1, 2, 3)])
+    entering = call(entering_body, [shape(pair, bf16)] * 4, [SMEM, SMEM] + [VMEM] * 6)(
+        place, decay_rate, *pieces, row_own, row_other
+    )
+    near = jnp.stack([entering[0]] + [trade(entering[k], "zl", k) for k in (1, 2, 3)])
     flow = attend(*chips1, state=(qt, *after(tuple(flow), entering[0])))
     near = after(near, flow[0])
     carried = after(carried, flow[0])
@@ -390,10 +386,12 @@
         [pltpu.VMEM((TILE, D), f32)],
         flops=1 << 30,
     )(place, decay_rate, inner, query, near, far, other_state)
-    others = [head_shift(sums, s) for s in (1, 2, 3)]
+    others = [trade(sums, "head", s) for s in (1, 2, 3)]
     flow = attend(*chips2, state=(qt, *after(tuple(flow), sums)))
     carried, *flow = after((carried, *flow), *others)
-    soft_out = attend(*parts(3), state=(qt, *flow), last=True)
+    (local, swapped), (local_at, swapped_at) = parts(3)
+    flow = attend([local], [local_at], state=(qt, *flow))
+    soft_out = attend([swapped], [swapped_at], state=(qt, *flow), last=True)
     lin_out = call(norm_body, shape((TILE, LOCAL, D), bf16), [VMEM] * 6, [big])(
         after(mixed, soft_out), sums, *others, norm_gain
     )

time: 83.9 us -> 83.6 us (level)
  starting transfers between devices: 52.6 us -> 42.2 us
  waiting for transfers between devices: 10.8 us -> 20.2 us
    ppermute x5, starting transfers between devices: 23.4 us -> 13 us  [two_ways(): return lax.ppermute(value, (*CHIPS, 'core'), pairs)]
    ppermute x8, waiting for transfers between devices: 3.08 us -> 9.48 us  [swap(): return lax.ppermute(value, axis, [(0, 1), (1, 0)])]
    ppermute x12, waiting for transfers between devices: 6.5 us -> 9.68 us  [trade(): return lax.ppermute(value, axis, [(i, i ^ bits) for i in range(4)])]
    transpose x1, local copies, waits for them, and re-layouts: 0.88 us -> 0.01 us  [on_device(): jnp.transpose(soft_k, (1, 0, 2)).reshape(KV * D, D)]
    transpose x1, local copies, waits for them, and re-layouts: 0.12 us -> 0.99 us  [on_device(): jnp.transpose(soft_v, (1, 2, 0)).reshape(KV * D, D)]
    pallas_call x5 -> x6, Pallas kernels: 5.9 us -> 6.6 us  [flash(): call(body, outs, [SMEM] * 3 + [VMEM] * (len(blocks) + len(extra)), scratc...]
  transfers between devices with their start and end apart: 25 -> 25, of which waited for: 8 -> 10; matrix products, arithmetic and copies ran while one was open for 2% -> 2% of each run, Pallas kernels for 12% -> 13%
where the time goes in v3:
time: 83.6 us; the launch traced here: 83.4 us
  starting transfers between devices  42.2 us (50%)
  waiting for transfers between devices  20.2 us (24%)
  Pallas kernels  15.6 us (19%)
  other arithmetic  2.04 us (2%)
  local copies, waits for them, and re-layouts  1.79 us (2%)
  between operations  1.64 us (2%)
    ppermute x12, starting transfers between devices, trade(): return lax.ppermute(value, axis, [(i, i ^ bits) for i in range(4)])  16.3 us
    ppermute x5, starting transfers between devices, two_ways(): return lax.ppermute(value, (*CHIPS, 'core'), pairs)  13 us
    ppermute x8, starting transfers between devices, swap(): return lax.ppermute(value, axis, [(0, 1), (1, 0)])  12.9 us
    ppermute x12, waiting for transfers between devices, trade(): return lax.ppermute(value, axis, [(i, i ^ bits) for i in range(4)])  9.68 us
    ppermute x8, waiting for transfers between devices, swap(): return lax.ppermute(value, axis, [(0, 1), (1, 0)])  9.48 us
    pallas_call x6, Pallas kernels, flash(): call(body, outs, [SMEM] * 3 + [VMEM] * (len(blocks) + len(extra)), scratc...  6.6 us
    pallas_call x1, Pallas kernels, on_device(): call(inner_body, [shape(heads, f32), shape(heads, bf16)], [SMEM, VMEM, VM...  2 us
  transfers between devices with their start and end apart: 25, of which 10 were waited for; matrix products, arithmetic and copies ran while one was open for 2% of the time, Pallas kernels for 13%

profile of v3, /device:TPU:1, one launch (start us, length us, event | category | flops | bytes accessed | tf_op | source)
XLA Modules:
  0.0 83.4 jit_solution(13886183343938900263)
XLA Ops:
  0.6 1.0 %copy.13 = bf16[2,128,128]{2,1,0:T(8,128)(2,1)S(1)} copy(bf16[2,128,128]{1,0,2:T(2,128)(2,1)} %bitcast.19) | data formatting | bytes 131072 | tf_op jit(solution)/shard_map/transpose | solution.py:323
  1.6 0.0 copy-start.3
  1.7 0.0 copy-start.4
  2.5 0.1 maximum_maximum_fusion
  2.6 0.0 copy-start.1
  2.6 3.3 %collective-permute-start = (bf16[1,528,128]{2,1,0:T(8,128)(2,1)S(1)}, bf16[1,528,128]{2,1,0:T(8,128)(2,1)S(1)}, u32[]{:S(2)}, u32[]{:S(2)}) collective-permute-start(bf16[1,528,128]{2,1,0:T(8,128)(2,1)S(1)} %get-tuple-element.121), channel_id=1, source_target_pairs={{0,4},{4,0},{1,5},{5,1},{2,6},{6,2},{3,7},{7,3},{8,12},{12,8},{9,1... | collective-permute-start | bytes 405512 | tf_op jit(solution)/shard_map/ppermute | solution.py:305
  5.9 1.0 %collective-permute-done.refs_3_ = bf16[1,528,128]{2,1,0:T(8,128)(2,1)S(1)} collective-permute-done((bf16[1,528,128]{2,1,0:T(8,128)(2,1)S(1)}, bf16[1,528,128]{2,1,0:T(8,128)(2,1)S(1)}, u32[]{:S(2)}, u32[]{:S(2)}) %collective-permute-start) | collective-permute-done | bytes 135200 | tf_op jit(solution)/shard_map/ppermute | solution.py:305
  6.9 0.7 pad_maximum_fusion.1
  7.7 1.6 %shard_map.113 = (bf16[16,128,128]{2,1,0:T(8,128)(2,1)S(1)}, f32[16,128,128]{2,1,0:T(8,128)S(1)}) custom-call(f32[16]{0:T(128)S(1)} %copy-done.1, bf16[128,16,128]{2,1,0:T(8,128)(2,1)S(1)} %copy-done.3, bf16[128,16,128]{2,1,0:T(8,128)(2,1)S(1)} %copy-done.4), custom_call_target="tpu_custom_call" | custom-call | flops 1073741824 | bytes 4194304 | tf_op jit(solution)/shard_map/pallas_call | solution.py:332
  9.3 0.4 collective-permute-start.1
  9.7 0.0 collective-permute-start.9
  9.7 1.9 %collective-permute-start.10 = (bf16[2,528,128]{2,1,0:T(8,128)(2,1)}, bf16[2,528,128]{2,1,0:T(8,128)(2,1)}, u32[]{:S(2)}, u32[]{:S(2)}) collective-permute-start(bf16[2,528,128]{2,1,0:T(8,128)(2,1)} %pad_maximum_fusion.1), channel_id=1, source_target_pairs={{0,72},{4,132},{8,80},{12,140},{16,88},{20,148},{24,96},{28,156},{... | collective-permute-start | bytes 811016 | tf_op jit(solution)/shard_map/ppermute | solution.py:297
  11.7 0.1 stack.38.place.refs_0_
  11.7 0.0 collective-permute-done.1.other.before
  11.8 0.7 shard_map.114
  12.4 1.7 %collective-permute-start.2 = (bf16[2,128,128]{2,1,0:T(8,128)(2,1)S(1)}, bf16[2,128,128]{2,1,0:T(8,128)(2,1)S(1)}, u32[]{:S(2)}, u32[]{:S(2)}) collective-permute-start(bf16[2,128,128]{2,1,0:T(8,128)(2,1)S(1)} %get-tuple-element.68), channel_id=1, source_target_pairs={{0,8},{8,0},{16,24},{24,16},{1,9},{9,1},{17,25},{25,17},{2,10},{10... | collective-permute-start | bytes 196616 | tf_op jit(solution)/shard_map/ppermute | solution.py:301
  14.2 3.0 %collective-permute-start.3 = (bf16[2,128,128]{2,1,0:T(8,128)(2,1)S(1)}, bf16[2,128,128]{2,1,0:T(8,128)(2,1)S(1)}, u32[]{:S(2)}, u32[]{:S(2)}) collective-permute-start(bf16[2,128,128]{2,1,0:T(8,128)(2,1)S(1)} %get-tuple-element.69), channel_id=1, source_target_pairs={{0,16},{8,24},{16,0},{24,8},{1,17},{9,25},{17,1},{25,9},{2,18},{10... | collective-permute-start | bytes 196616 | tf_op jit(solution)/shard_map/ppermute | solution.py:301
  17.2 2.0 %shard_map.115 = (f32[16,128,128]{2,1,0:T(8,128)S(1)}, bf16[16,128,128]{2,1,0:T(8,128)(2,1)S(1)}) custom-call(f32[16]{0:T(128)S(1)} %copy-done.1, bf16[128,16,128]{2,1,0:T(8,128)(2,1)S(1)} %copy-done.2, bf16[128,16,128]{2,1,0:T(8,128)(2,1)S(1)} %copy-done.3, bf16[128,16,128]{2,1,0:T(8,128)(2,1)S(1)} %copy-done.4), custom_call_target="tpu_custom_call" | custom-call | flops 1073741824 | bytes 4194304 | tf_op jit(solution)/shard_map/pallas_call | solution.py:339
  19.2 0.7 collective-permute-done.3.p2
  19.9 3.2 %collective-permute-done.4.p3 = bf16[2,128,128]{2,1,0:T(8,128)(2,1)S(1)} collective-permute-done((bf16[2,128,128]{2,1,0:T(8,128)(2,1)S(1)}, bf16[2,128,128]{2,1,0:T(8,128)(2,1)S(1)}, u32[]{:S(2)}, u32[]{:S(2)}) %collective-permute-start.4) | collective-permute-done | bytes 65568 | tf_op jit(solution)/shard_map/ppermute | solution.py:301
  23.1 0.6 shard_map.116
  23.7 0.1 collective-permute-start.5
  23.8 2.3 %collective-permute-start.6 = (bf16[2,128,128]{2,1,0:T(8,128)(2,1)S(1)}, bf16[2,128,128]{2,1,0:T(8,128)(2,1)S(1)}, u32[]{:S(2)}, u32[]{:S(2)}) collective-permute-start(bf16[2,128,128]{2,1,0:T(8,128)(2,1)S(1)} %get-tuple-element.72), channel_id=1, source_target_pairs={{0,128},{64,192},{128,0},{192,64},{1,129},{65,193},{129,1},{193,65... | collective-permute-start | bytes 196616 | tf_op jit(solution)/shard_map/ppermute | solution.py:301
  26.1 1.5 %collective-permute-start.7 = (bf16[2,128,128]{2,1,0:T(8,128)(2,1)S(1)}, bf16[2,128,128]{2,1,0:T(8,128)(2,1)S(1)}, u32[]{:S(2)}, u32[]{:S(2)}) collective-permute-start(bf16[2,128,128]{2,1,0:T(8,128)(2,1)S(1)} %get-tuple-element.72), channel_id=1, source_target_pairs={{0,192},{64,128},{128,64},{192,0},{1,193},{65,129},{129,65},{193,1... | collective-permute-start | bytes 196616 | tf_op jit(solution)/shard_map/ppermute | solution.py:301
  27.6 0.0 collective-permute-done.9
  27.6 0.0 collective-permute-done.10
  27.6 1.1 %pad_maximum_fusion.refs_3_ = bf16[4,528,128]{2,1,0:T(8,128)(2,1)S(1)} fusion(bf16[2,528,128]{2,1,0:T(8,128)(2,1)} %collective-permute-done.10, bf16[2,528,128]{2,1,0:T(8,128)(2,1)} %collective-permute-done.9), kind=kLoop, calls=%fused_computation | loop fusion | flops 270336 | bytes 1081344 | tf_op jit(solution)/shard_map/concatenate | solution.py:357
  28.8 0.0 copy-start.6
  28.8 0.0 copy-done.5
  28.8 0.6 copy-done.6
  29.5 1.3 %shard_map.117 = (bf16[2,128,1024]{2,1,0:T(8,128)(2,1)S(1)}, f32[2,1,1024]{2,1,0:T(1,128)S(1)}, f32[2,1,1024]{2,1,0:T(1,128)S(1)}, f32[2,128,1024]{2,1,0:T(8,128)S(1)}) custom-call(s32[5]{0:T(128)S(1)} %stack.38.place.refs_0_, s32[1]{0:T(128)S(6)} %copy.14.refs_1_, s32[1,64]{1,0:T(1,128)S(1)} %copy-done.6, ...), custom_call_target="tpu_custom_call" | custom-call | flops 268435456 | bytes 4194304 | tf_op jit(solution)/shard_map/pallas_call | solution.py:173
  30.8 0.0 collective-permute-done.5.x1
  30.8 0.0 collective-permute-done.6.x2
  30.8 3.9 %collective-permute-start.11 = (bf16[4,528,128]{2,1,0:T(8,128)(2,1)S(1)}, bf16[4,528,128]{2,1,0:T(8,128)(2,1)S(1)}, u32[]{:S(2)}, u32[]{:S(2)}) collective-permute-start(bf16[4,528,128]{2,1,0:T(8,128)(2,1)S(1)} %pad_maximum_fusion.refs_3_), channel_id=1, source_target_pairs={{0,4},{4,0},{1,5},{5,1},{2,6},{6,2},{3,7},{7,3},{8,12},{12,8},{9,1... | collective-permute-start | bytes 1622024 | tf_op jit(solution)/shard_map/ppermute | solution.py:305
  34.7 4.8 %collective-permute-start.15 = (bf16[4,528,128]{2,1,0:T(8,128)(2,1)S(1)}, bf16[4,528,128]{2,1,0:T(8,128)(2,1)S(1)}, u32[]{:S(2)}, u32[]{:S(2)}) collective-permute-start(bf16[4,528,128]{2,1,0:T(8,128)(2,1)S(1)} %pad_maximum_fusion.refs_3_), channel_id=1, source_target_pairs={{0,8},{4,252},{8,16},{12,4},{16,24},{20,12},{24,32},{28,20},{32,40... | collective-permute-start | bytes 1622024 | tf_op jit(solution)/shard_map/ppermute | solution.py:297
  39.5 0.6 shard_map.118
  40.1 0.1 collective-permute-start.8
  40.2 1.0 %shard_map.119 = (f32[2,1,1024]{2,1,0:T(1,128)S(1)}, f32[2,1,1024]{2,1,0:T(1,128)S(1)}, f32[2,128,1024]{2,1,0:T(8,128)S(1)}) custom-call(s32[5]{0:T(128)S(1)} %stack.38.place.refs_0_, s32[1]{0:T(128)S(6)} %copy.14.refs_1_, s32[1,64]{1,0:T(1,128)S(1)} %copy-done.6, bf16[4,528,128]{2,1,0:T(8,128)(2,1)S(1)} %pad_maximum_fusion.refs_3_, ...), custom_call_target="tpu_custom_call" | custom-call | flops 2147483648 | bytes 4194304 | tf_op jit(solution)/shard_map/pallas_call | solution.py:173
  41.3 7.7 %collective-permute-done.8.other = bf16[2,128,128]{2,1,0:T(8,128)(2,1)S(1)} collective-permute-done((bf16[2,128,128]{2,1,0:T(8,128)(2,1)S(1)}, bf16[2,128,128]{2,1,0:T(8,128)(2,1)S(1)}, u32[]{:S(2)}, u32[]{:S(2)}) %collective-permute-start.8) | collective-permute-done | bytes 65568 | tf_op jit(solution)/shard_map/ppermute | solution.py:305
  49.0 1.0 %collective-permute-start.16 = (bf16[4,528,128]{2,1,0:T(8,128)(2,1)S(1)}, bf16[4,528,128]{2,1,0:T(8,128)(2,1)S(1)}, u32[]{:S(2)}, u32[]{:S(2)}) collective-permute-start(bf16[4,528,128]{2,1,0:T(8,128)(2,1)S(1)} %collective-permute-done.15.refs_3_), channel_id=1, source_target_pairs={{0,4},{4,0},{1,5},{5,1},{2,6},{6,2},{3,7},{7,3},{8,12},{12,8},{9,1... | collective-permute-start | bytes 1622024 | tf_op jit(solution)/shard_map/ppermute | solution.py:305
  50.0 3.8 %collective-permute-start.18 = (bf16[4,528,128]{2,1,0:T(8,128)(2,1)S(1)}, bf16[4,528,128]{2,1,0:T(8,128)(2,1)S(1)}, u32[]{:S(2)}, u32[]{:S(2)}) collective-permute-start(bf16[4,528,128]{2,1,0:T(8,128)(2,1)S(1)} %collective-permute-done.15.refs_3_), channel_id=1, source_target_pairs={{0,8},{4,252},{8,16},{12,4},{16,24},{20,12},{24,32},{28,20},{32,40... | collective-permute-start | bytes 1622024 | tf_op jit(solution)/shard_map/ppermute | solution.py:297
  53.8 0.8 shard_map.120
  54.6 0.5 collective-permute-start.14
  55.1 0.0 collective-permute-start.13
  55.1 3.2 %collective-permute-start.12 = (bf16[2,128,128]{2,1,0:T(8,128)(2,1)S(1)}, bf16[2,128,128]{2,1,0:T(8,128)(2,1)S(1)}, u32[]{:S(2)}, u32[]{:S(2)}) collective-permute-start(bf16[2,128,128]{2,1,0:T(8,128)(2,1)S(1)} %get-tuple-element.90), channel_id=1, source_target_pairs={{0,8},{8,0},{16,24},{24,16},{1,9},{9,1},{17,25},{25,17},{2,10},{10... | collective-permute-start | bytes 196616 | tf_op jit(solution)/shard_map/ppermute | solution.py:301
  58.2 0.0 collective-permute-done.16.refs_4_
  58.2 0.8 %shard_map.121 = (f32[2,1,1024]{2,1,0:T(1,128)S(1)}, f32[2,1,1024]{2,1,0:T(1,128)S(1)}, f32[2,128,1024]{2,1,0:T(8,128)S(1)}) custom-call(s32[5]{0:T(128)S(1)} %stack.38.place.refs_0_, s32[1]{0:T(128)S(6)} %copy.14.refs_1_, s32[1,64]{1,0:T(1,128)S(1)} %copy-done.6, bf16[4,528,128]{2,1,0:T(8,128)(2,1)S(1)} %collective-permute-done.15.refs_3_, ...), custom_call_target="tpu_custom_call" | custom-call | flops 2147483648 | bytes 4194304 | tf_op jit(solution)/shard_map/pallas_call | solution.py:173
  59.1 1.0 %collective-permute-done.18.refs_3_ = bf16[4,528,128]{2,1,0:T(8,128)(2,1)S(1)} collective-permute-done((bf16[4,528,128]{2,1,0:T(8,128)(2,1)S(1)}, bf16[4,528,128]{2,1,0:T(8,128)(2,1)S(1)}, u32[]{:S(2)}, u32[]{:S(2)}) %collective-permute-start.18) | collective-permute-done | bytes 540704 | tf_op jit(solution)/shard_map/ppermute | solution.py:297
  60.1 2.6 %collective-permute-start.20 = (bf16[4,528,128]{2,1,0:T(8,128)(2,1)S(1)}, bf16[4,528,128]{2,1,0:T(8,128)(2,1)S(1)}, u32[]{:S(2)}, u32[]{:S(2)}) collective-permute-start(bf16[4,528,128]{2,1,0:T(8,128)(2,1)S(1)} %collective-permute-done.18.refs_3_), channel_id=1, source_target_pairs={{0,4},{4,0},{1,5},{5,1},{2,6},{6,2},{3,7},{7,3},{8,12},{12,8},{9,1... | collective-permute-start | bytes 1622024 | tf_op jit(solution)/shard_map/ppermute | solution.py:305
  62.7 1.1 %collective-permute-done.14 = bf16[2,128,128]{2,1,0:T(8,128)(2,1)S(1)} collective-permute-done((bf16[2,128,128]{2,1,0:T(8,128)(2,1)S(1)}, bf16[2,128,128]{2,1,0:T(8,128)(2,1)S(1)}, u32[]{:S(2)}, u32[]{:S(2)}) %collective-permute-start.14) | collective-permute-done | bytes 65568 | tf_op jit(solution)/shard_map/ppermute | solution.py:301
  63.9 1.5 %collective-permute-done.13 = bf16[2,128,128]{2,1,0:T(8,128)(2,1)S(1)} collective-permute-done((bf16[2,128,128]{2,1,0:T(8,128)(2,1)S(1)}, bf16[2,128,128]{2,1,0:T(8,128)(2,1)S(1)}, u32[]{:S(2)}, u32[]{:S(2)}) %collective-permute-start.13) | collective-permute-done | bytes 65568 | tf_op jit(solution)/shard_map/ppermute | solution.py:301
  65.4 0.1 collective-permute-start.17
  65.5 2.5 %collective-permute-start.19 = (bf16[4,528,128]{2,1,0:T(8,128)(2,1)S(1)}, bf16[4,528,128]{2,1,0:T(8,128)(2,1)S(1)}, u32[]{:S(2)}, u32[]{:S(2)}) collective-permute-start(bf16[4,528,128]{2,1,0:T(8,128)(2,1)S(1)} %collective-permute-done.18.refs_3_), channel_id=1, source_target_pairs={{0,8},{4,252},{8,16},{12,4},{16,24},{20,12},{24,32},{28,20},{32,40... | collective-permute-start | bytes 1622024 | tf_op jit(solution)/shard_map/ppermute | solution.py:297
  68.0 1.3 %shard_map.122 = (f32[16,128,128]{2,1,0:T(8,128)S(1)}, f32[8,128]{1,0:T(8,128)S(1)}) custom-call(s32[5]{0:T(128)S(1)} %stack.38.place.refs_0_, f32[16]{0:T(128)S(1)} %copy-done.1, f32[16,128,128]{2,1,0:T(8,128)S(1)} %get-tuple-element.66.inner, bf16[16,128,128]{2,1,0:T(8,128)(2,1)S(1)} %get-tuple-element.67.q, ...), custom_call_target="tpu_custom_call" | custom-call | flops 1073741824 | bytes 4194304 | tf_op jit(solution)/shard_map/pallas_call | solution.py:382
  69.4 1.4 %collective-permute-start.21 = (f32[8,128]{1,0:T(8,128)S(1)}, f32[8,128]{1,0:T(8,128)S(1)}, u32[]{:S(2)}, u32[]{:S(2)}) collective-permute-start(f32[8,128]{1,0:T(8,128)S(1)} %get-tuple-element.105.own), channel_id=1, source_target_pairs={{0,1},{1,0},{2,3},{3,2},{4,5},{5,4},{6,7},{7,6},{8,9},{9,8},{10,11... | collective-permute-start | bytes 12296 | tf_op jit(solution)/shard_map/ppermute | solution.py:301
  70.7 2.6 %collective-permute-start.22 = (f32[8,128]{1,0:T(8,128)S(1)}, f32[8,128]{1,0:T(8,128)S(1)}, u32[]{:S(2)}, u32[]{:S(2)}) collective-permute-start(f32[8,128]{1,0:T(8,128)S(1)} %get-tuple-element.105.own), channel_id=1, source_target_pairs={{0,2},{1,3},{2,0},{3,1},{4,6},{5,7},{6,4},{7,5},{8,10},{9,11},{10,... | collective-permute-start | bytes 12296 | tf_op jit(solution)/shard_map/ppermute | solution.py:301
  73.4 0.8 %shard_map.123 = (f32[2,1,1024]{2,1,0:T(1,128)S(1)}, f32[2,1,1024]{2,1,0:T(1,128)S(1)}, f32[2,128,1024]{2,1,0:T(8,128)S(1)}) custom-call(s32[5]{0:T(128)S(1)} %stack.38.place.refs_0_, s32[1]{0:T(128)S(6)} %copy.14.refs_1_, s32[1,64]{1,0:T(1,128)S(1)} %copy-done.6, bf16[4,528,128]{2,1,0:T(8,128)(2,1)S(1)} %collective-permute-done.18.refs_3_, ...), custom_call_target="tpu_custom_call" | custom-call | flops 2147483648 | bytes 4194304 | tf_op jit(solution)/shard_map/pallas_call | solution.py:173
  74.2 0.8 collective-permute-done.22.s2
  75.0 2.3 %collective-permute-done.23.s3 = f32[8,128]{1,0:T(8,128)S(1)} collective-permute-done((f32[8,128]{1,0:T(8,128)S(1)}, f32[8,128]{1,0:T(8,128)S(1)}, u32[]{:S(2)}, u32[]{:S(2)}) %collective-permute-start.23) | collective-permute-done | bytes 4128 | tf_op jit(solution)/shard_map/ppermute | solution.py:301
  77.3 1.4 %collective-permute-start.24 = (bf16[4,528,128]{2,1,0:T(8,128)(2,1)S(1)}, bf16[4,528,128]{2,1,0:T(8,128)(2,1)S(1)}, u32[]{:S(2)}, u32[]{:S(2)}) collective-permute-start(bf16[4,528,128]{2,1,0:T(8,128)(2,1)S(1)} %collective-permute-done.19.refs_3_), channel_id=1, source_target_pairs={{0,4},{4,0},{1,5},{5,1},{2,6},{6,2},{3,7},{7,3},{8,12},{12,8},{9,1... | collective-permute-start | bytes 1622024 | tf_op jit(solution)/shard_map/ppermute | solution.py:305
  78.7 0.8 shard_map.124
  79.5 0.8 collective-permute-done.24.refs_3_
  80.3 1.8 %shard_map.125 = bf16[128,16,128]{2,1,0:T(8,128)(2,1)} custom-call(s32[5]{0:T(128)S(1)} %stack.38.place.refs_0_, s32[1]{0:T(128)S(6)} %copy.14.refs_1_, s32[1,64]{1,0:T(1,128)S(1)} %copy-done.6, bf16[4,528,128]{2,1,0:T(8,128)(2,1)S(1)} %collective-permute-done.24.refs_3_, bf16[2,128,1024]{2,1,0:T(8,128)(2,1)S(1)} %get-tuple-element.81.refs_5_.refs_4_, ...), custom_call_target="tpu_custom_call" | custom-call | flops 1073741824 | bytes 4194304 | tf_op jit(solution)/shard_map/pallas_call | solution.py:173
  82.1 1.3 %shard_map.126 = bf16[128,16,128]{2,1,0:T(8,128)(2,1)} custom-call(f32[16,128,128]{2,1,0:T(8,128)S(1)} %get-tuple-element.119.mixed, f32[8,128]{1,0:T(8,128)S(1)} %get-tuple-element.105.own, f32[8,128]{1,0:T(8,128)S(1)} %collective-permute-done.21.s1, f32[8,128]{1,0:T(8,128)S(1)} %collective-permute-done.22.s2, f32[8,128]{1,0:T(8,128)S(1)} %collective-permute-done.23.s3, ...), custom_call_target="tpu_custom_call" | custom-call | bytes 4194304 | tf_op jit(solution)/shard_map/pallas_call | solution.py:395
  (25 shorter events, 0.1 us)
Async XLA Ops:
  0.6 1.0 %copy-start.7 = (bf16[128,2,128]{2,1,0:T(2,128)(2,1)S(1)}, bf16[128,2,128]{2,1,0:T(2,128)(2,1)}, u32[]{:S(2)}) copy-start(bf16[128,2,128]{2,1,0:T(2,128)(2,1)} %param.16) | copy-start | bytes 196612
  1.6 6.0 %copy-start.3 = (bf16[128,16,128]{2,1,0:T(8,128)(2,1)S(1)}, bf16[128,16,128]{2,1,0:T(8,128)(2,1)}, u32[]{:S(2)}) copy-start(bf16[128,16,128]{2,1,0:T(8,128)(2,1)} %k_in.2) | copy-start | bytes 1572868
  1.7 6.0 %copy-start.4 = (bf16[128,16,128]{2,1,0:T(8,128)(2,1)S(1)}, bf16[128,16,128]{2,1,0:T(8,128)(2,1)}, u32[]{:S(2)}) copy-start(bf16[128,16,128]{2,1,0:T(8,128)(2,1)} %v_in.3) | copy-start | bytes 1572868
  2.6 5.1 %copy-start.1 = (f32[16]{0:T(128)S(1)}, f32[16]{0:T(128)}, u32[]{:S(2)}) copy-start(f32[16]{0:T(128)} %rate.13) | copy-start | bytes 196
  2.6 4.3 %collective-permute-start = (bf16[1,528,128]{2,1,0:T(8,128)(2,1)S(1)}, bf16[1,528,128]{2,1,0:T(8,128)(2,1)S(1)}, u32[]{:S(2)}, u32[]{:S(2)}) collective-permute-start(bf16[1,528,128]{2,1,0:T(8,128)(2,1)S(1)} %get-tuple-element.121), channel_id=1, source_target_pairs={{0,4},{4,0},{1,5},{5,1},{2,6},{6,2},{3,7},{7,3},{8,12},{12,8},{9,1... | collective-permute-start | bytes 405512 | tf_op jit(solution)/shard_map/ppermute | solution.py:305
  9.3 2.5 %collective-permute-start.1 = (bf16[16,128,128]{2,1,0:T(8,128)(2,1)S(1)}, bf16[16,128,128]{2,1,0:T(8,128)(2,1)S(1)}, u32[]{:S(2)}, u32[]{:S(2)}) collective-permute-start(bf16[16,128,128]{2,1,0:T(8,128)(2,1)S(1)} %get-tuple-element.63), channel_id=1, source_target_pairs={{0,4},{4,0},{1,5},{5,1},{2,6},{6,2},{3,7},{7,3},{8,12},{12,8},{9,1... | collective-permute-start | bytes 1572872 | tf_op jit(solution)/shard_map/ppermute | solution.py:305
  9.7 17.9 %collective-permute-start.9 = (bf16[2,528,128]{2,1,0:T(8,128)(2,1)}, bf16[2,528,128]{2,1,0:T(8,128)(2,1)}, u32[]{:S(2)}, u32[]{:S(2)}) collective-permute-start(bf16[2,528,128]{2,1,0:T(8,128)(2,1)} %pad_maximum_fusion.1), channel_id=1, source_target_pairs={{0,8},{4,68},{8,16},{12,76},{16,24},{20,84},{24,32},{28,92},{32,40... | collective-permute-start | bytes 811016 | tf_op jit(solution)/shard_map/ppermute | solution.py:297
  9.7 17.9 %collective-permute-start.10 = (bf16[2,528,128]{2,1,0:T(8,128)(2,1)}, bf16[2,528,128]{2,1,0:T(8,128)(2,1)}, u32[]{:S(2)}, u32[]{:S(2)}) collective-permute-start(bf16[2,528,128]{2,1,0:T(8,128)(2,1)} %pad_maximum_fusion.1), channel_id=1, source_target_pairs={{0,72},{4,132},{8,80},{12,140},{16,88},{20,148},{24,96},{28,156},{... | collective-permute-start | bytes 811016 | tf_op jit(solution)/shard_map/ppermute | solution.py:297
  11.8 5.4 %copy-start.2 = (bf16[128,16,128]{2,1,0:T(8,128)(2,1)S(1)}, bf16[128,16,128]{2,1,0:T(8,128)(2,1)}, u32[]{:S(2)}) copy-start(bf16[128,16,128]{2,1,0:T(8,128)(2,1)} %q_in) | copy-start | bytes 1572868
  12.4 6.7 %collective-permute-start.2 = (bf16[2,128,128]{2,1,0:T(8,128)(2,1)S(1)}, bf16[2,128,128]{2,1,0:T(8,128)(2,1)S(1)}, u32[]{:S(2)}, u32[]{:S(2)}) collective-permute-start(bf16[2,128,128]{2,1,0:T(8,128)(2,1)S(1)} %get-tuple-element.68), channel_id=1, source_target_pairs={{0,8},{8,0},{16,24},{24,16},{1,9},{9,1},{17,25},{25,17},{2,10},{10... | collective-permute-start | bytes 196616 | tf_op jit(solution)/shard_map/ppermute | solution.py:301
  14.2 5.7 %collective-permute-start.3 = (bf16[2,128,128]{2,1,0:T(8,128)(2,1)S(1)}, bf16[2,128,128]{2,1,0:T(8,128)(2,1)S(1)}, u32[]{:S(2)}, u32[]{:S(2)}) collective-permute-start(bf16[2,128,128]{2,1,0:T(8,128)(2,1)S(1)} %get-tuple-element.69), channel_id=1, source_target_pairs={{0,16},{8,24},{16,0},{24,8},{1,17},{9,25},{17,1},{25,9},{2,18},{10... | collective-permute-start | bytes 196616 | tf_op jit(solution)/shard_map/ppermute | solution.py:301
  17.2 5.9 %collective-permute-start.4 = (bf16[2,128,128]{2,1,0:T(8,128)(2,1)S(1)}, bf16[2,128,128]{2,1,0:T(8,128)(2,1)S(1)}, u32[]{:S(2)}, u32[]{:S(2)}) collective-permute-start(bf16[2,128,128]{2,1,0:T(8,128)(2,1)S(1)} %get-tuple-element.70), channel_id=1, source_target_pairs={{0,24},{8,16},{16,8},{24,0},{1,25},{9,17},{17,9},{25,1},{2,26},{10... | collective-permute-start | bytes 196616 | tf_op jit(solution)/shard_map/ppermute | solution.py:301
  23.7 7.1 %collective-permute-start.5 = (bf16[2,128,128]{2,1,0:T(8,128)(2,1)S(1)}, bf16[2,128,128]{2,1,0:T(8,128)(2,1)S(1)}, u32[]{:S(2)}, u32[]{:S(2)}) collective-permute-start(bf16[2,128,128]{2,1,0:T(8,128)(2,1)S(1)} %get-tuple-element.72), channel_id=1, source_target_pairs={{0,64},{64,0},{128,192},{192,128},{1,65},{65,1},{129,193},{193,129... | collective-permute-start | bytes 196616 | tf_op jit(solution)/shard_map/ppermute | solution.py:301
  23.8 7.0 %collective-permute-start.6 = (bf16[2,128,128]{2,1,0:T(8,128)(2,1)S(1)}, bf16[2,128,128]{2,1,0:T(8,128)(2,1)S(1)}, u32[]{:S(2)}, u32[]{:S(2)}) collective-permute-start(bf16[2,128,128]{2,1,0:T(8,128)(2,1)S(1)} %get-tuple-element.72), channel_id=1, source_target_pairs={{0,128},{64,192},{128,0},{192,64},{1,129},{65,193},{129,1},{193,65... | collective-permute-start | bytes 196616 | tf_op jit(solution)/shard_map/ppermute | solution.py:301
  26.1 4.6 %collective-permute-start.7 = (bf16[2,128,128]{2,1,0:T(8,128)(2,1)S(1)}, bf16[2,128,128]{2,1,0:T(8,128)(2,1)S(1)}, u32[]{:S(2)}, u32[]{:S(2)}) collective-permute-start(bf16[2,128,128]{2,1,0:T(8,128)(2,1)S(1)} %get-tuple-element.72), channel_id=1, source_target_pairs={{0,192},{64,128},{128,64},{192,0},{1,193},{65,129},{129,65},{193,1... | collective-permute-start | bytes 196616 | tf_op jit(solution)/shard_map/ppermute | solution.py:301
  27.6 1.2 %copy-start.5 = (bf16[128,16,128]{2,1,0:T(8,128)(2,1)S(1)}, bf16[128,16,128]{2,1,0:T(8,128)(2,1)}, u32[]{:S(2)}) copy-start(bf16[128,16,128]{2,1,0:T(8,128)(2,1)} %refs_4_) | copy-start | bytes 1572868
  28.8 0.7 copy-start.6
  30.8 9.4 %collective-permute-start.11 = (bf16[4,528,128]{2,1,0:T(8,128)(2,1)S(1)}, bf16[4,528,128]{2,1,0:T(8,128)(2,1)S(1)}, u32[]{:S(2)}, u32[]{:S(2)}) collective-permute-start(bf16[4,528,128]{2,1,0:T(8,128)(2,1)S(1)} %pad_maximum_fusion.refs_3_), channel_id=1, source_target_pairs={{0,4},{4,0},{1,5},{5,1},{2,6},{6,2},{3,7},{7,3},{8,12},{12,8},{9,1... | collective-permute-start | bytes 1622024 | tf_op jit(solution)/shard_map/ppermute | solution.py:305
  34.7 14.3 %collective-permute-start.15 = (bf16[4,528,128]{2,1,0:T(8,128)(2,1)S(1)}, bf16[4,528,128]{2,1,0:T(8,128)(2,1)S(1)}, u32[]{:S(2)}, u32[]{:S(2)}) collective-permute-start(bf16[4,528,128]{2,1,0:T(8,128)(2,1)S(1)} %pad_maximum_fusion.refs_3_), channel_id=1, source_target_pairs={{0,8},{4,252},{8,16},{12,4},{16,24},{20,12},{24,32},{28,20},{32,40... | collective-permute-start | bytes 1622024 | tf_op jit(solution)/shard_map/ppermute | solution.py:297
  40.1 8.9 %collective-permute-start.8 = (bf16[2,128,128]{2,1,0:T(8,128)(2,1)S(1)}, bf16[2,128,128]{2,1,0:T(8,128)(2,1)S(1)}, u32[]{:S(2)}, u32[]{:S(2)}) collective-permute-start(bf16[2,128,128]{2,1,0:T(8,128)(2,1)S(1)} %get-tuple-element.77), channel_id=1, source_target_pairs={{0,32},{32,0},{1,33},{33,1},{2,34},{34,2},{3,35},{35,3},{4,36},{36... | collective-permute-start | bytes 196616 | tf_op jit(solution)/shard_map/ppermute | solution.py:305
  49.0 9.2 %collective-permute-start.16 = (bf16[4,528,128]{2,1,0:T(8,128)(2,1)S(1)}, bf16[4,528,128]{2,1,0:T(8,128)(2,1)S(1)}, u32[]{:S(2)}, u32[]{:S(2)}) collective-permute-start(bf16[4,528,128]{2,1,0:T(8,128)(2,1)S(1)} %collective-permute-done.15.refs_3_), channel_id=1, source_target_pairs={{0,4},{4,0},{1,5},{5,1},{2,6},{6,2},{3,7},{7,3},{8,12},{12,8},{9,1... | collective-permute-start | bytes 1622024 | tf_op jit(solution)/shard_map/ppermute | solution.py:305
  50.0 10.1 %collective-permute-start.18 = (bf16[4,528,128]{2,1,0:T(8,128)(2,1)S(1)}, bf16[4,528,128]{2,1,0:T(8,128)(2,1)S(1)}, u32[]{:S(2)}, u32[]{:S(2)}) collective-permute-start(bf16[4,528,128]{2,1,0:T(8,128)(2,1)S(1)} %collective-permute-done.15.refs_3_), channel_id=1, source_target_pairs={{0,8},{4,252},{8,16},{12,4},{16,24},{20,12},{24,32},{28,20},{32,40... | collective-permute-start | bytes 1622024 | tf_op jit(solution)/shard_map/ppermute | solution.py:297
  54.6 9.3 %collective-permute-start.14 = (bf16[2,128,128]{2,1,0:T(8,128)(2,1)S(1)}, bf16[2,128,128]{2,1,0:T(8,128)(2,1)S(1)}, u32[]{:S(2)}, u32[]{:S(2)}) collective-permute-start(bf16[2,128,128]{2,1,0:T(8,128)(2,1)S(1)} %get-tuple-element.92), channel_id=1, source_target_pairs={{0,24},{8,16},{16,8},{24,0},{1,25},{9,17},{17,9},{25,1},{2,26},{10... | collective-permute-start | bytes 196616 | tf_op jit(solution)/shard_map/ppermute | solution.py:301
  55.1 10.3 %collective-permute-start.13 = (bf16[2,128,128]{2,1,0:T(8,128)(2,1)S(1)}, bf16[2,128,128]{2,1,0:T(8,128)(2,1)S(1)}, u32[]{:S(2)}, u32[]{:S(2)}) collective-permute-start(bf16[2,128,128]{2,1,0:T(8,128)(2,1)S(1)} %get-tuple-element.91), channel_id=1, source_target_pairs={{0,16},{8,24},{16,0},{24,8},{1,17},{9,25},{17,1},{25,9},{2,18},{10... | collective-permute-start | bytes 196616 | tf_op jit(solution)/shard_map/ppermute | solution.py:301
  55.1 10.3 %collective-permute-start.12 = (bf16[2,128,128]{2,1,0:T(8,128)(2,1)S(1)}, bf16[2,128,128]{2,1,0:T(8,128)(2,1)S(1)}, u32[]{:S(2)}, u32[]{:S(2)}) collective-permute-start(bf16[2,128,128]{2,1,0:T(8,128)(2,1)S(1)} %get-tuple-element.90), channel_id=1, source_target_pairs={{0,8},{8,0},{16,24},{24,16},{1,9},{9,1},{17,25},{25,17},{2,10},{10... | collective-permute-start | bytes 196616 | tf_op jit(solution)/shard_map/ppermute | solution.py:301
  60.1 13.2 %collective-permute-start.20 = (bf16[4,528,128]{2,1,0:T(8,128)(2,1)S(1)}, bf16[4,528,128]{2,1,0:T(8,128)(2,1)S(1)}, u32[]{:S(2)}, u32[]{:S(2)}) collective-permute-start(bf16[4,528,128]{2,1,0:T(8,128)(2,1)S(1)} %collective-permute-done.18.refs_3_), channel_id=1, source_target_pairs={{0,4},{4,0},{1,5},{5,1},{2,6},{6,2},{3,7},{7,3},{8,12},{12,8},{9,1... | collective-permute-start | bytes 1622024 | tf_op jit(solution)/shard_map/ppermute | solution.py:305
  65.4 2.6 %collective-permute-start.17 = (bf16[4,2,128,128]{3,2,1,0:T(8,128)(2,1)S(1)}, bf16[4,2,128,128]{3,2,1,0:T(8,128)(2,1)S(1)}, u32[]{:S(2)}, u32[]{:S(2)}) collective-permute-start(bf16[4,2,128,128]{3,2,1,0:T(8,128)(2,1)S(1)} %pad_maximum_fusion.2.near), channel_id=1, source_target_pairs={{0,4},{4,0},{1,5},{5,1},{2,6},{6,2},{3,7},{7,3},{8,12},{12,8},{9,1... | collective-permute-start | bytes 786440 | tf_op jit(solution)/shard_map/ppermute | solution.py:305
  65.5 11.8 %collective-permute-start.19 = (bf16[4,528,128]{2,1,0:T(8,128)(2,1)S(1)}, bf16[4,528,128]{2,1,0:T(8,128)(2,1)S(1)}, u32[]{:S(2)}, u32[]{:S(2)}) collective-permute-start(bf16[4,528,128]{2,1,0:T(8,128)(2,1)S(1)} %collective-permute-done.18.refs_3_), channel_id=1, source_target_pairs={{0,8},{4,252},{8,16},{12,4},{16,24},{20,12},{24,32},{28,20},{32,40... | collective-permute-start | bytes 1622024 | tf_op jit(solution)/shard_map/ppermute | solution.py:297
  69.4 4.9 %collective-permute-start.21 = (f32[8,128]{1,0:T(8,128)S(1)}, f32[8,128]{1,0:T(8,128)S(1)}, u32[]{:S(2)}, u32[]{:S(2)}) collective-permute-start(f32[8,128]{1,0:T(8,128)S(1)} %get-tuple-element.105.own), channel_id=1, source_target_pairs={{0,1},{1,0},{2,3},{3,2},{4,5},{5,4},{6,7},{7,6},{8,9},{9,8},{10,11... | collective-permute-start | bytes 12296 | tf_op jit(solution)/shard_map/ppermute | solution.py:301
  70.7 4.3 %collective-permute-start.22 = (f32[8,128]{1,0:T(8,128)S(1)}, f32[8,128]{1,0:T(8,128)S(1)}, u32[]{:S(2)}, u32[]{:S(2)}) collective-permute-start(f32[8,128]{1,0:T(8,128)S(1)} %get-tuple-element.105.own), channel_id=1, source_target_pairs={{0,2},{1,3},{2,0},{3,1},{4,6},{5,7},{6,4},{7,5},{8,10},{9,11},{10,... | collective-permute-start | bytes 12296 | tf_op jit(solution)/shard_map/ppermute | solution.py:301
  73.4 4.0 %collective-permute-start.23 = (f32[8,128]{1,0:T(8,128)S(1)}, f32[8,128]{1,0:T(8,128)S(1)}, u32[]{:S(2)}, u32[]{:S(2)}) collective-permute-start(f32[8,128]{1,0:T(8,128)S(1)} %get-tuple-element.105.own), channel_id=1, source_target_pairs={{0,3},{1,2},{2,1},{3,0},{4,7},{5,6},{6,5},{7,4},{8,11},{9,10},{10,... | collective-permute-start | bytes 12296 | tf_op jit(solution)/shard_map/ppermute | solution.py:301
  77.3 2.9 %collective-permute-start.24 = (bf16[4,528,128]{2,1,0:T(8,128)(2,1)S(1)}, bf16[4,528,128]{2,1,0:T(8,128)(2,1)S(1)}, u32[]{:S(2)}, u32[]{:S(2)}) collective-permute-start(bf16[4,528,128]{2,1,0:T(8,128)(2,1)S(1)} %collective-permute-done.19.refs_3_), channel_id=1, source_target_pairs={{0,4},{4,0},{1,5},{5,1},{2,6},{6,2},{3,7},{7,3},{8,12},{12,8},{9,1... | collective-permute-start | bytes 1622024 | tf_op jit(solution)/shard_map/ppermute | solution.py:305
  80.3 1.8 %copy-start = (f32[16,128]{1,0:T(8,128)S(1)}, f32[16,128]{1,0:T(8,128)}, u32[]{:S(2)}) copy-start(f32[16,128]{1,0:T(8,128)} %gain.1) | copy-start | bytes 24580

commit v4 on v3

--- a/solution.py
+++ b/solution.py
@@ -334,7 +334,8 @@
     )(decay_rate, after(lin_k, both), lin_v)
     other_state = swap(state_high)
     slices = call(chip_body, [shape(pair, bf16)] * 4, [SMEM, SMEM, VMEM, VMEM])(place, decay_rate, state, other_state)
-    pieces = [slices[0]] + [trade(slices[k], "zl", k) for k in (1, 2, 3)]
+    far3, far2, far1 = (trade(slices[k], "zl", k) for k in (3, 2, 1))
+    pieces = [slices[0], far1, far2, far3]
 
     inner, query = call(
         inner_body, [shape(heads, f32), shape(heads, bf16)], [SMEM, VMEM, VMEM, VMEM], [big] * 3, flops=1 << 30
@@ -343,7 +344,8 @@
     row4, row4_sent = call(four_body, [shape(pair, f32), shape(pair, bf16)], [SMEM, SMEM] + [VMEM] * 4)(
         place, decay_rate, *pieces
     )
-    earlier = [trade(row4_sent, "x", k) for k in (1, 2, 3)]
+    x2, x3, x1 = (trade(row4_sent, "x", k) for k in (2, 3, 1))
+    earlier = [x1, x2, x3]
 
     def attend(blocks, groups, **state):
         return flash(place, doc_ids, block_mask, blocks, groups, **state)

time: 83.6 us -> 83.6 us (level)
  no operation moved by 1% of the time
where the time goes in v4:
time: 83.6 us; the launch traced here: 83.4 us
  starting transfers between devices  42.2 us (50%)
  waiting for transfers between devices  20.2 us (24%)
  Pallas kernels  15.6 us (19%)
  other arithmetic  2.04 us (2%)
  local copies, waits for them, and re-layouts  1.79 us (2%)
  between operations  1.64 us (2%)
    ppermute x12, starting transfers between devices, trade(): return lax.ppermute(value, axis, [(i, i ^ bits) for i in range(4)])  16.3 us
    ppermute x5, starting transfers between devices, two_ways(): return lax.ppermute(value, (*CHIPS, 'core'), pairs)  13 us
    ppermute x8, starting transfers between devices, swap(): return lax.ppermute(value, axis, [(0, 1), (1, 0)])  12.9 us
    ppermute x12, waiting for transfers between devices, trade(): return lax.ppermute(value, axis, [(i, i ^ bits) for i in range(4)])  9.68 us
    ppermute x8, waiting for transfers between devices, swap(): return lax.ppermute(value, axis, [(0, 1), (1, 0)])  9.48 us
    pallas_call x6, Pallas kernels, flash(): call(body, outs, [SMEM] * 3 + [VMEM] * (len(blocks) + len(extra)), scratc...  6.6 us
    pallas_call x1, Pallas kernels, on_device(): call(inner_body, [shape(heads, f32), shape(heads, bf16)], [SMEM, VMEM, VM...  2 us
  transfers between devices with their start and end apart: 25, of which 10 were waited for; matrix products, arithmetic and copies ran while one was open for 2% of the time, Pallas kernels for 13%

profile of v4, /device:TPU:1, one launch (start us, length us, event | category | flops | bytes accessed | tf_op | source)
XLA Modules:
  0.0 83.4 jit_solution(13886183343938900263)
XLA Ops:
  0.6 1.0 %copy.13 = bf16[2,128,128]{2,1,0:T(8,128)(2,1)S(1)} copy(bf16[2,128,128]{1,0,2:T(2,128)(2,1)} %bitcast.19) | data formatting | bytes 131072 | tf_op jit(solution)/shard_map/transpose | solution.py:323
  1.6 0.0 copy-start.3
  1.7 0.0 copy-start.4
  2.5 0.1 maximum_maximum_fusion
  2.6 0.0 copy-start.1
  2.6 3.3 %collective-permute-start = (bf16[1,528,128]{2,1,0:T(8,128)(2,1)S(1)}, bf16[1,528,128]{2,1,0:T(8,128)(2,1)S(1)}, u32[]{:S(2)}, u32[]{:S(2)}) collective-permute-start(bf16[1,528,128]{2,1,0:T(8,128)(2,1)S(1)} %get-tuple-element.121), channel_id=1, source_target_pairs={{0,4},{4,0},{1,5},{5,1},{2,6},{6,2},{3,7},{7,3},{8,12},{12,8},{9,1... | collective-permute-start | bytes 405512 | tf_op jit(solution)/shard_map/ppermute | solution.py:305
  5.9 1.0 %collective-permute-done.refs_3_ = bf16[1,528,128]{2,1,0:T(8,128)(2,1)S(1)} collective-permute-done((bf16[1,528,128]{2,1,0:T(8,128)(2,1)S(1)}, bf16[1,528,128]{2,1,0:T(8,128)(2,1)S(1)}, u32[]{:S(2)}, u32[]{:S(2)}) %collective-permute-start) | collective-permute-done | bytes 135200 | tf_op jit(solution)/shard_map/ppermute | solution.py:305
  6.9 0.7 pad_maximum_fusion.1
  7.7 1.6 %shard_map.113 = (bf16[16,128,128]{2,1,0:T(8,128)(2,1)S(1)}, f32[16,128,128]{2,1,0:T(8,128)S(1)}) custom-call(f32[16]{0:T(128)S(1)} %copy-done.1, bf16[128,16,128]{2,1,0:T(8,128)(2,1)S(1)} %copy-done.3, bf16[128,16,128]{2,1,0:T(8,128)(2,1)S(1)} %copy-done.4), custom_call_target="tpu_custom_call" | custom-call | flops 1073741824 | bytes 4194304 | tf_op jit(solution)/shard_map/pallas_call | solution.py:332
  9.3 0.4 collective-permute-start.1
  9.7 0.0 collective-permute-start.9
  9.7 1.9 %collective-permute-start.10 = (bf16[2,528,128]{2,1,0:T(8,128)(2,1)}, bf16[2,528,128]{2,1,0:T(8,128)(2,1)}, u32[]{:S(2)}, u32[]{:S(2)}) collective-permute-start(bf16[2,528,128]{2,1,0:T(8,128)(2,1)} %pad_maximum_fusion.1), channel_id=1, source_target_pairs={{0,72},{4,132},{8,80},{12,140},{16,88},{20,148},{24,96},{28,156},{... | collective-permute-start | bytes 811016 | tf_op jit(solution)/shard_map/ppermute | solution.py:297
  11.7 0.1 stack.38.place.refs_0_
  11.7 0.0 collective-permute-done.1.other.before
  11.8 0.7 shard_map.114
  12.4 1.7 %collective-permute-start.2 = (bf16[2,128,128]{2,1,0:T(8,128)(2,1)S(1)}, bf16[2,128,128]{2,1,0:T(8,128)(2,1)S(1)}, u32[]{:S(2)}, u32[]{:S(2)}) collective-permute-start(bf16[2,128,128]{2,1,0:T(8,128)(2,1)S(1)} %get-tuple-element.68), channel_id=1, source_target_pairs={{0,8},{8,0},{16,24},{24,16},{1,9},{9,1},{17,25},{25,17},{2,10},{10... | collective-permute-start | bytes 196616 | tf_op jit(solution)/shard_map/ppermute | solution.py:301
  14.2 3.0 %collective-permute-start.3 = (bf16[2,128,128]{2,1,0:T(8,128)(2,1)S(1)}, bf16[2,128,128]{2,1,0:T(8,128)(2,1)S(1)}, u32[]{:S(2)}, u32[]{:S(2)}) collective-permute-start(bf16[2,128,128]{2,1,0:T(8,128)(2,1)S(1)} %get-tuple-element.69), channel_id=1, source_target_pairs={{0,16},{8,24},{16,0},{24,8},{1,17},{9,25},{17,1},{25,9},{2,18},{10... | collective-permute-start | bytes 196616 | tf_op jit(solution)/shard_map/ppermute | solution.py:301
  17.2 2.0 %shard_map.115 = (f32[16,128,128]{2,1,0:T(8,128)S(1)}, bf16[16,128,128]{2,1,0:T(8,128)(2,1)S(1)}) custom-call(f32[16]{0:T(128)S(1)} %copy-done.1, bf16[128,16,128]{2,1,0:T(8,128)(2,1)S(1)} %copy-done.2, bf16[128,16,128]{2,1,0:T(8,128)(2,1)S(1)} %copy-done.3, bf16[128,16,128]{2,1,0:T(8,128)(2,1)S(1)} %copy-done.4), custom_call_target="tpu_custom_call" | custom-call | flops 1073741824 | bytes 4194304 | tf_op jit(solution)/shard_map/pallas_call | solution.py:340
  19.2 0.0 collective-permute-done.2.p1
  19.2 0.7 collective-permute-done.3.p2
  19.9 3.2 %collective-permute-done.4.p3 = bf16[2,128,128]{2,1,0:T(8,128)(2,1)S(1)} collective-permute-done((bf16[2,128,128]{2,1,0:T(8,128)(2,1)S(1)}, bf16[2,128,128]{2,1,0:T(8,128)(2,1)S(1)}, u32[]{:S(2)}, u32[]{:S(2)}) %collective-permute-start.4) | collective-permute-done | bytes 65568 | tf_op jit(solution)/shard_map/ppermute | solution.py:301
  23.1 0.6 shard_map.116
  23.7 0.1 collective-permute-start.5
  23.8 2.3 %collective-permute-start.6 = (bf16[2,128,128]{2,1,0:T(8,128)(2,1)S(1)}, bf16[2,128,128]{2,1,0:T(8,128)(2,1)S(1)}, u32[]{:S(2)}, u32[]{:S(2)}) collective-permute-start(bf16[2,128,128]{2,1,0:T(8,128)(2,1)S(1)} %get-tuple-element.72), channel_id=1, source_target_pairs={{0,128},{64,192},{128,0},{192,64},{1,129},{65,193},{129,1},{193,65... | collective-permute-start | bytes 196616 | tf_op jit(solution)/shard_map/ppermute | solution.py:301
  26.1 1.5 %collective-permute-start.7 = (bf16[2,128,128]{2,1,0:T(8,128)(2,1)S(1)}, bf16[2,128,128]{2,1,0:T(8,128)(2,1)S(1)}, u32[]{:S(2)}, u32[]{:S(2)}) collective-permute-start(bf16[2,128,128]{2,1,0:T(8,128)(2,1)S(1)} %get-tuple-element.72), channel_id=1, source_target_pairs={{0,192},{64,128},{128,64},{192,0},{1,193},{65,129},{129,65},{193,1... | collective-permute-start | bytes 196616 | tf_op jit(solution)/shard_map/ppermute | solution.py:301
  27.6 0.0 collective-permute-done.9
  27.6 0.0 collective-permute-done.10
  27.6 1.1 %pad_maximum_fusion.refs_3_ = bf16[4,528,128]{2,1,0:T(8,128)(2,1)S(1)} fusion(bf16[2,528,128]{2,1,0:T(8,128)(2,1)} %collective-permute-done.10, bf16[2,528,128]{2,1,0:T(8,128)(2,1)} %collective-permute-done.9), kind=kLoop, calls=%fused_computation | loop fusion | flops 270336 | bytes 1081344 | tf_op jit(solution)/shard_map/concatenate | solution.py:359
  28.8 0.0 copy-start.6
  28.8 0.0 copy-done.5
  28.8 0.6 copy-done.6
  29.5 1.3 %shard_map.117 = (bf16[2,128,1024]{2,1,0:T(8,128)(2,1)S(1)}, f32[2,1,1024]{2,1,0:T(1,128)S(1)}, f32[2,1,1024]{2,1,0:T(1,128)S(1)}, f32[2,128,1024]{2,1,0:T(8,128)S(1)}) custom-call(s32[5]{0:T(128)S(1)} %stack.38.place.refs_0_, s32[1]{0:T(128)S(6)} %copy.14.refs_1_, s32[1,64]{1,0:T(1,128)S(1)} %copy-done.6, ...), custom_call_target="tpu_custom_call" | custom-call | flops 268435456 | bytes 4194304 | tf_op jit(solution)/shard_map/pallas_call | solution.py:173
  30.8 0.0 collective-permute-done.6.x2
  30.8 0.0 collective-permute-done.7.x3
  30.8 3.9 %collective-permute-start.11 = (bf16[4,528,128]{2,1,0:T(8,128)(2,1)S(1)}, bf16[4,528,128]{2,1,0:T(8,128)(2,1)S(1)}, u32[]{:S(2)}, u32[]{:S(2)}) collective-permute-start(bf16[4,528,128]{2,1,0:T(8,128)(2,1)S(1)} %pad_maximum_fusion.refs_3_), channel_id=1, source_target_pairs={{0,4},{4,0},{1,5},{5,1},{2,6},{6,2},{3,7},{7,3},{8,12},{12,8},{9,1... | collective-permute-start | bytes 1622024 | tf_op jit(solution)/shard_map/ppermute | solution.py:305
  34.7 4.8 %collective-permute-start.15 = (bf16[4,528,128]{2,1,0:T(8,128)(2,1)S(1)}, bf16[4,528,128]{2,1,0:T(8,128)(2,1)S(1)}, u32[]{:S(2)}, u32[]{:S(2)}) collective-permute-start(bf16[4,528,128]{2,1,0:T(8,128)(2,1)S(1)} %pad_maximum_fusion.refs_3_), channel_id=1, source_target_pairs={{0,8},{4,252},{8,16},{12,4},{16,24},{20,12},{24,32},{28,20},{32,40... | collective-permute-start | bytes 1622024 | tf_op jit(solution)/shard_map/ppermute | solution.py:297
  39.5 0.6 shard_map.118
  40.1 0.1 collective-permute-start.8
  40.2 1.0 %shard_map.119 = (f32[2,1,1024]{2,1,0:T(1,128)S(1)}, f32[2,1,1024]{2,1,0:T(1,128)S(1)}, f32[2,128,1024]{2,1,0:T(8,128)S(1)}) custom-call(s32[5]{0:T(128)S(1)} %stack.38.place.refs_0_, s32[1]{0:T(128)S(6)} %copy.14.refs_1_, s32[1,64]{1,0:T(1,128)S(1)} %copy-done.6, bf16[4,528,128]{2,1,0:T(8,128)(2,1)S(1)} %pad_maximum_fusion.refs_3_, ...), custom_call_target="tpu_custom_call" | custom-call | flops 2147483648 | bytes 4194304 | tf_op jit(solution)/shard_map/pallas_call | solution.py:173
  41.3 7.7 %collective-permute-done.8.other = bf16[2,128,128]{2,1,0:T(8,128)(2,1)S(1)} collective-permute-done((bf16[2,128,128]{2,1,0:T(8,128)(2,1)S(1)}, bf16[2,128,128]{2,1,0:T(8,128)(2,1)S(1)}, u32[]{:S(2)}, u32[]{:S(2)}) %collective-permute-start.8) | collective-permute-done | bytes 65568 | tf_op jit(solution)/shard_map/ppermute | solution.py:305
  49.0 1.0 %collective-permute-start.16 = (bf16[4,528,128]{2,1,0:T(8,128)(2,1)S(1)}, bf16[4,528,128]{2,1,0:T(8,128)(2,1)S(1)}, u32[]{:S(2)}, u32[]{:S(2)}) collective-permute-start(bf16[4,528,128]{2,1,0:T(8,128)(2,1)S(1)} %collective-permute-done.15.refs_3_), channel_id=1, source_target_pairs={{0,4},{4,0},{1,5},{5,1},{2,6},{6,2},{3,7},{7,3},{8,12},{12,8},{9,1... | collective-permute-start | bytes 1622024 | tf_op jit(solution)/shard_map/ppermute | solution.py:305
  50.0 3.8 %collective-permute-start.18 = (bf16[4,528,128]{2,1,0:T(8,128)(2,1)S(1)}, bf16[4,528,128]{2,1,0:T(8,128)(2,1)S(1)}, u32[]{:S(2)}, u32[]{:S(2)}) collective-permute-start(bf16[4,528,128]{2,1,0:T(8,128)(2,1)S(1)} %collective-permute-done.15.refs_3_), channel_id=1, source_target_pairs={{0,8},{4,252},{8,16},{12,4},{16,24},{20,12},{24,32},{28,20},{32,40... | collective-permute-start | bytes 1622024 | tf_op jit(solution)/shard_map/ppermute | solution.py:297
  53.8 0.8 shard_map.120
  54.6 0.5 collective-permute-start.14
  55.1 3.2 %collective-permute-start.12 = (bf16[2,128,128]{2,1,0:T(8,128)(2,1)S(1)}, bf16[2,128,128]{2,1,0:T(8,128)(2,1)S(1)}, u32[]{:S(2)}, u32[]{:S(2)}) collective-permute-start(bf16[2,128,128]{2,1,0:T(8,128)(2,1)S(1)} %get-tuple-element.90), channel_id=1, source_target_pairs={{0,8},{8,0},{16,24},{24,16},{1,9},{9,1},{17,25},{25,17},{2,10},{10... | collective-permute-start | bytes 196616 | tf_op jit(solution)/shard_map/ppermute | solution.py:301
  58.2 0.0 collective-permute-done.16.refs_4_
  58.2 0.8 %shard_map.121 = (f32[2,1,1024]{2,1,0:T(1,128)S(1)}, f32[2,1,1024]{2,1,0:T(1,128)S(1)}, f32[2,128,1024]{2,1,0:T(8,128)S(1)}) custom-call(s32[5]{0:T(128)S(1)} %stack.38.place.refs_0_, s32[1]{0:T(128)S(6)} %copy.14.refs_1_, s32[1,64]{1,0:T(1,128)S(1)} %copy-done.6, bf16[4,528,128]{2,1,0:T(8,128)(2,1)S(1)} %collective-permute-done.15.refs_3_, ...), custom_call_target="tpu_custom_call" | custom-call | flops 2147483648 | bytes 4194304 | tf_op jit(solution)/shard_map/pallas_call | solution.py:173
  59.1 1.0 %collective-permute-done.18.refs_3_ = bf16[4,528,128]{2,1,0:T(8,128)(2,1)S(1)} collective-permute-done((bf16[4,528,128]{2,1,0:T(8,128)(2,1)S(1)}, bf16[4,528,128]{2,1,0:T(8,128)(2,1)S(1)}, u32[]{:S(2)}, u32[]{:S(2)}) %collective-permute-start.18) | collective-permute-done | bytes 540704 | tf_op jit(solution)/shard_map/ppermute | solution.py:297
  60.1 2.6 %collective-permute-start.20 = (bf16[4,528,128]{2,1,0:T(8,128)(2,1)S(1)}, bf16[4,528,128]{2,1,0:T(8,128)(2,1)S(1)}, u32[]{:S(2)}, u32[]{:S(2)}) collective-permute-start(bf16[4,528,128]{2,1,0:T(8,128)(2,1)S(1)} %collective-permute-done.18.refs_3_), channel_id=1, source_target_pairs={{0,4},{4,0},{1,5},{5,1},{2,6},{6,2},{3,7},{7,3},{8,12},{12,8},{9,1... | collective-permute-start | bytes 1622024 | tf_op jit(solution)/shard_map/ppermute | solution.py:305
  62.7 1.1 %collective-permute-done.14 = bf16[2,128,128]{2,1,0:T(8,128)(2,1)S(1)} collective-permute-done((bf16[2,128,128]{2,1,0:T(8,128)(2,1)S(1)}, bf16[2,128,128]{2,1,0:T(8,128)(2,1)S(1)}, u32[]{:S(2)}, u32[]{:S(2)}) %collective-permute-start.14) | collective-permute-done | bytes 65568 | tf_op jit(solution)/shard_map/ppermute | solution.py:301
  63.9 1.5 %collective-permute-done.13 = bf16[2,128,128]{2,1,0:T(8,128)(2,1)S(1)} collective-permute-done((bf16[2,128,128]{2,1,0:T(8,128)(2,1)S(1)}, bf16[2,128,128]{2,1,0:T(8,128)(2,1)S(1)}, u32[]{:S(2)}, u32[]{:S(2)}) %collective-permute-start.13) | collective-permute-done | bytes 65568 | tf_op jit(solution)/shard_map/ppermute | solution.py:301
  65.4 0.1 collective-permute-start.17
  65.5 2.5 %collective-permute-start.19 = (bf16[4,528,128]{2,1,0:T(8,128)(2,1)S(1)}, bf16[4,528,128]{2,1,0:T(8,128)(2,1)S(1)}, u32[]{:S(2)}, u32[]{:S(2)}) collective-permute-start(bf16[4,528,128]{2,1,0:T(8,128)(2,1)S(1)} %collective-permute-done.18.refs_3_), channel_id=1, source_target_pairs={{0,8},{4,252},{8,16},{12,4},{16,24},{20,12},{24,32},{28,20},{32,40... | collective-permute-start | bytes 1622024 | tf_op jit(solution)/shard_map/ppermute | solution.py:297
  68.0 1.3 %shard_map.122 = (f32[16,128,128]{2,1,0:T(8,128)S(1)}, f32[8,128]{1,0:T(8,128)S(1)}) custom-call(s32[5]{0:T(128)S(1)} %stack.38.place.refs_0_, f32[16]{0:T(128)S(1)} %copy-done.1, f32[16,128,128]{2,1,0:T(8,128)S(1)} %get-tuple-element.66.inner, bf16[16,128,128]{2,1,0:T(8,128)(2,1)S(1)} %get-tuple-element.67.q, ...), custom_call_target="tpu_custom_call" | custom-call | flops 1073741824 | bytes 4194304 | tf_op jit(solution)/shard_map/pallas_call | solution.py:384
  69.4 1.4 %collective-permute-start.21 = (f32[8,128]{1,0:T(8,128)S(1)}, f32[8,128]{1,0:T(8,128)S(1)}, u32[]{:S(2)}, u32[]{:S(2)}) collective-permute-start(f32[8,128]{1,0:T(8,128)S(1)} %get-tuple-element.105.own), channel_id=1, source_target_pairs={{0,1},{1,0},{2,3},{3,2},{4,5},{5,4},{6,7},{7,6},{8,9},{9,8},{10,11... | collective-permute-start | bytes 12296 | tf_op jit(solution)/shard_map/ppermute | solution.py:301
  70.7 2.6 %collective-permute-start.22 = (f32[8,128]{1,0:T(8,128)S(1)}, f32[8,128]{1,0:T(8,128)S(1)}, u32[]{:S(2)}, u32[]{:S(2)}) collective-permute-start(f32[8,128]{1,0:T(8,128)S(1)} %get-tuple-element.105.own), channel_id=1, source_target_pairs={{0,2},{1,3},{2,0},{3,1},{4,6},{5,7},{6,4},{7,5},{8,10},{9,11},{10,... | collective-permute-start | bytes 12296 | tf_op jit(solution)/shard_map/ppermute | solution.py:301
  73.4 0.8 %shard_map.123 = (f32[2,1,1024]{2,1,0:T(1,128)S(1)}, f32[2,1,1024]{2,1,0:T(1,128)S(1)}, f32[2,128,1024]{2,1,0:T(8,128)S(1)}) custom-call(s32[5]{0:T(128)S(1)} %stack.38.place.refs_0_, s32[1]{0:T(128)S(6)} %copy.14.refs_1_, s32[1,64]{1,0:T(1,128)S(1)} %copy-done.6, bf16[4,528,128]{2,1,0:T(8,128)(2,1)S(1)} %collective-permute-done.18.refs_3_, ...), custom_call_target="tpu_custom_call" | custom-call | flops 2147483648 | bytes 4194304 | tf_op jit(solution)/shard_map/pallas_call | solution.py:173
  74.2 0.8 collective-permute-done.22.s2
  75.0 2.3 %collective-permute-done.23.s3 = f32[8,128]{1,0:T(8,128)S(1)} collective-permute-done((f32[8,128]{1,0:T(8,128)S(1)}, f32[8,128]{1,0:T(8,128)S(1)}, u32[]{:S(2)}, u32[]{:S(2)}) %collective-permute-start.23) | collective-permute-done | bytes 4128 | tf_op jit(solution)/shard_map/ppermute | solution.py:301
  77.3 1.4 %collective-permute-start.24 = (bf16[4,528,128]{2,1,0:T(8,128)(2,1)S(1)}, bf16[4,528,128]{2,1,0:T(8,128)(2,1)S(1)}, u32[]{:S(2)}, u32[]{:S(2)}) collective-permute-start(bf16[4,528,128]{2,1,0:T(8,128)(2,1)S(1)} %collective-permute-done.19.refs_3_), channel_id=1, source_target_pairs={{0,4},{4,0},{1,5},{5,1},{2,6},{6,2},{3,7},{7,3},{8,12},{12,8},{9,1... | collective-permute-start | bytes 1622024 | tf_op jit(solution)/shard_map/ppermute | solution.py:305
  78.7 0.8 shard_map.124
  79.5 0.8 collective-permute-done.24.refs_3_
  80.3 1.8 %shard_map.125 = bf16[128,16,128]{2,1,0:T(8,128)(2,1)} custom-call(s32[5]{0:T(128)S(1)} %stack.38.place.refs_0_, s32[1]{0:T(128)S(6)} %copy.14.refs_1_, s32[1,64]{1,0:T(1,128)S(1)} %copy-done.6, bf16[4,528,128]{2,1,0:T(8,128)(2,1)S(1)} %collective-permute-done.24.refs_3_, bf16[2,128,1024]{2,1,0:T(8,128)(2,1)S(1)} %get-tuple-element.81.refs_5_.refs_4_, ...), custom_call_target="tpu_custom_call" | custom-call | flops 1073741824 | bytes 4194304 | tf_op jit(solution)/shard_map/pallas_call | solution.py:173
  82.1 1.3 %shard_map.126 = bf16[128,16,128]{2,1,0:T(8,128)(2,1)} custom-call(f32[16,128,128]{2,1,0:T(8,128)S(1)} %get-tuple-element.119.mixed, f32[8,128]{1,0:T(8,128)S(1)} %get-tuple-element.105.own, f32[8,128]{1,0:T(8,128)S(1)} %collective-permute-done.21.s1, f32[8,128]{1,0:T(8,128)S(1)} %collective-permute-done.22.s2, f32[8,128]{1,0:T(8,128)S(1)} %collective-permute-done.23.s3, ...), custom_call_target="tpu_custom_call" | custom-call | bytes 4194304 | tf_op jit(solution)/shard_map/pallas_call | solution.py:397
  (25 shorter events, 0.1 us)
Async XLA Ops:
  0.6 1.0 %copy-start.7 = (bf16[128,2,128]{2,1,0:T(2,128)(2,1)S(1)}, bf16[128,2,128]{2,1,0:T(2,128)(2,1)}, u32[]{:S(2)}) copy-start(bf16[128,2,128]{2,1,0:T(2,128)(2,1)} %param.16) | copy-start | bytes 196612
  1.6 6.0 %copy-start.3 = (bf16[128,16,128]{2,1,0:T(8,128)(2,1)S(1)}, bf16[128,16,128]{2,1,0:T(8,128)(2,1)}, u32[]{:S(2)}) copy-start(bf16[128,16,128]{2,1,0:T(8,128)(2,1)} %k_in.2) | copy-start | bytes 1572868
  1.7 6.0 %copy-start.4 = (bf16[128,16,128]{2,1,0:T(8,128)(2,1)S(1)}, bf16[128,16,128]{2,1,0:T(8,128)(2,1)}, u32[]{:S(2)}) copy-start(bf16[128,16,128]{2,1,0:T(8,128)(2,1)} %v_in.3) | copy-start | bytes 1572868
  2.6 5.1 %copy-start.1 = (f32[16]{0:T(128)S(1)}, f32[16]{0:T(128)}, u32[]{:S(2)}) copy-start(f32[16]{0:T(128)} %rate.13) | copy-start | bytes 196
  2.6 4.3 %collective-permute-start = (bf16[1,528,128]{2,1,0:T(8,128)(2,1)S(1)}, bf16[1,528,128]{2,1,0:T(8,128)(2,1)S(1)}, u32[]{:S(2)}, u32[]{:S(2)}) collective-permute-start(bf16[1,528,128]{2,1,0:T(8,128)(2,1)S(1)} %get-tuple-element.121), channel_id=1, source_target_pairs={{0,4},{4,0},{1,5},{5,1},{2,6},{6,2},{3,7},{7,3},{8,12},{12,8},{9,1... | collective-permute-start | bytes 405512 | tf_op jit(solution)/shard_map/ppermute | solution.py:305
  9.3 2.5 %collective-permute-start.1 = (bf16[16,128,128]{2,1,0:T(8,128)(2,1)S(1)}, bf16[16,128,128]{2,1,0:T(8,128)(2,1)S(1)}, u32[]{:S(2)}, u32[]{:S(2)}) collective-permute-start(bf16[16,128,128]{2,1,0:T(8,128)(2,1)S(1)} %get-tuple-element.63), channel_id=1, source_target_pairs={{0,4},{4,0},{1,5},{5,1},{2,6},{6,2},{3,7},{7,3},{8,12},{12,8},{9,1... | collective-permute-start | bytes 1572872 | tf_op jit(solution)/shard_map/ppermute | solution.py:305
  9.7 17.9 %collective-permute-start.9 = (bf16[2,528,128]{2,1,0:T(8,128)(2,1)}, bf16[2,528,128]{2,1,0:T(8,128)(2,1)}, u32[]{:S(2)}, u32[]{:S(2)}) collective-permute-start(bf16[2,528,128]{2,1,0:T(8,128)(2,1)} %pad_maximum_fusion.1), channel_id=1, source_target_pairs={{0,8},{4,68},{8,16},{12,76},{16,24},{20,84},{24,32},{28,92},{32,40... | collective-permute-start | bytes 811016 | tf_op jit(solution)/shard_map/ppermute | solution.py:297
  9.7 17.9 %collective-permute-start.10 = (bf16[2,528,128]{2,1,0:T(8,128)(2,1)}, bf16[2,528,128]{2,1,0:T(8,128)(2,1)}, u32[]{:S(2)}, u32[]{:S(2)}) collective-permute-start(bf16[2,528,128]{2,1,0:T(8,128)(2,1)} %pad_maximum_fusion.1), channel_id=1, source_target_pairs={{0,72},{4,132},{8,80},{12,140},{16,88},{20,148},{24,96},{28,156},{... | collective-permute-start | bytes 811016 | tf_op jit(solution)/shard_map/ppermute | solution.py:297
  11.8 5.4 %copy-start.2 = (bf16[128,16,128]{2,1,0:T(8,128)(2,1)S(1)}, bf16[128,16,128]{2,1,0:T(8,128)(2,1)}, u32[]{:S(2)}) copy-start(bf16[128,16,128]{2,1,0:T(8,128)(2,1)} %q_in) | copy-start | bytes 1572868
  12.4 6.7 %collective-permute-start.2 = (bf16[2,128,128]{2,1,0:T(8,128)(2,1)S(1)}, bf16[2,128,128]{2,1,0:T(8,128)(2,1)S(1)}, u32[]{:S(2)}, u32[]{:S(2)}) collective-permute-start(bf16[2,128,128]{2,1,0:T(8,128)(2,1)S(1)} %get-tuple-element.68), channel_id=1, source_target_pairs={{0,8},{8,0},{16,24},{24,16},{1,9},{9,1},{17,25},{25,17},{2,10},{10... | collective-permute-start | bytes 196616 | tf_op jit(solution)/shard_map/ppermute | solution.py:301
  14.2 5.7 %collective-permute-start.3 = (bf16[2,128,128]{2,1,0:T(8,128)(2,1)S(1)}, bf16[2,128,128]{2,1,0:T(8,128)(2,1)S(1)}, u32[]{:S(2)}, u32[]{:S(2)}) collective-permute-start(bf16[2,128,128]{2,1,0:T(8,128)(2,1)S(1)} %get-tuple-element.69), channel_id=1, source_target_pairs={{0,16},{8,24},{16,0},{24,8},{1,17},{9,25},{17,1},{25,9},{2,18},{10... | collective-permute-start | bytes 196616 | tf_op jit(solution)/shard_map/ppermute | solution.py:301
  17.2 5.9 %collective-permute-start.4 = (bf16[2,128,128]{2,1,0:T(8,128)(2,1)S(1)}, bf16[2,128,128]{2,1,0:T(8,128)(2,1)S(1)}, u32[]{:S(2)}, u32[]{:S(2)}) collective-permute-start(bf16[2,128,128]{2,1,0:T(8,128)(2,1)S(1)} %get-tuple-element.70), channel_id=1, source_target_pairs={{0,24},{8,16},{16,8},{24,0},{1,25},{9,17},{17,9},{25,1},{2,26},{10... | collective-permute-start | bytes 196616 | tf_op jit(solution)/shard_map/ppermute | solution.py:301
  23.7 7.1 %collective-permute-start.5 = (bf16[2,128,128]{2,1,0:T(8,128)(2,1)S(1)}, bf16[2,128,128]{2,1,0:T(8,128)(2,1)S(1)}, u32[]{:S(2)}, u32[]{:S(2)}) collective-permute-start(bf16[2,128,128]{2,1,0:T(8,128)(2,1)S(1)} %get-tuple-element.72), channel_id=1, source_target_pairs={{0,64},{64,0},{128,192},{192,128},{1,65},{65,1},{129,193},{193,129... | collective-permute-start | bytes 196616 | tf_op jit(solution)/shard_map/ppermute | solution.py:301
  23.8 7.0 %collective-permute-start.6 = (bf16[2,128,128]{2,1,0:T(8,128)(2,1)S(1)}, bf16[2,128,128]{2,1,0:T(8,128)(2,1)S(1)}, u32[]{:S(2)}, u32[]{:S(2)}) collective-permute-start(bf16[2,128,128]{2,1,0:T(8,128)(2,1)S(1)} %get-tuple-element.72), channel_id=1, source_target_pairs={{0,128},{64,192},{128,0},{192,64},{1,129},{65,193},{129,1},{193,65... | collective-permute-start | bytes 196616 | tf_op jit(solution)/shard_map/ppermute | solution.py:301
  26.1 4.6 %collective-permute-start.7 = (bf16[2,128,128]{2,1,0:T(8,128)(2,1)S(1)}, bf16[2,128,128]{2,1,0:T(8,128)(2,1)S(1)}, u32[]{:S(2)}, u32[]{:S(2)}) collective-permute-start(bf16[2,128,128]{2,1,0:T(8,128)(2,1)S(1)} %get-tuple-element.72), channel_id=1, source_target_pairs={{0,192},{64,128},{128,64},{192,0},{1,193},{65,129},{129,65},{193,1... | collective-permute-start | bytes 196616 | tf_op jit(solution)/shard_map/ppermute | solution.py:301
  27.6 1.2 %copy-start.5 = (bf16[128,16,128]{2,1,0:T(8,128)(2,1)S(1)}, bf16[128,16,128]{2,1,0:T(8,128)(2,1)}, u32[]{:S(2)}) copy-start(bf16[128,16,128]{2,1,0:T(8,128)(2,1)} %refs_4_) | copy-start | bytes 1572868
  28.8 0.7 copy-start.6
  30.8 9.4 %collective-permute-start.11 = (bf16[4,528,128]{2,1,0:T(8,128)(2,1)S(1)}, bf16[4,528,128]{2,1,0:T(8,128)(2,1)S(1)}, u32[]{:S(2)}, u32[]{:S(2)}) collective-permute-start(bf16[4,528,128]{2,1,0:T(8,128)(2,1)S(1)} %pad_maximum_fusion.refs_3_), channel_id=1, source_target_pairs={{0,4},{4,0},{1,5},{5,1},{2,6},{6,2},{3,7},{7,3},{8,12},{12,8},{9,1... | collective-permute-start | bytes 1622024 | tf_op jit(solution)/shard_map/ppermute | solution.py:305
  34.7 14.3 %collective-permute-start.15 = (bf16[4,528,128]{2,1,0:T(8,128)(2,1)S(1)}, bf16[4,528,128]{2,1,0:T(8,128)(2,1)S(1)}, u32[]{:S(2)}, u32[]{:S(2)}) collective-permute-start(bf16[4,528,128]{2,1,0:T(8,128)(2,1)S(1)} %pad_maximum_fusion.refs_3_), channel_id=1, source_target_pairs={{0,8},{4,252},{8,16},{12,4},{16,24},{20,12},{24,32},{28,20},{32,40... | collective-permute-start | bytes 1622024 | tf_op jit(solution)/shard_map/ppermute | solution.py:297
  40.1 8.9 %collective-permute-start.8 = (bf16[2,128,128]{2,1,0:T(8,128)(2,1)S(1)}, bf16[2,128,128]{2,1,0:T(8,128)(2,1)S(1)}, u32[]{:S(2)}, u32[]{:S(2)}) collective-permute-start(bf16[2,128,128]{2,1,0:T(8,128)(2,1)S(1)} %get-tuple-element.77), channel_id=1, source_target_pairs={{0,32},{32,0},{1,33},{33,1},{2,34},{34,2},{3,35},{35,3},{4,36},{36... | collective-permute-start | bytes 196616 | tf_op jit(solution)/shard_map/ppermute | solution.py:305
  49.0 9.2 %collective-permute-start.16 = (bf16[4,528,128]{2,1,0:T(8,128)(2,1)S(1)}, bf16[4,528,128]{2,1,0:T(8,128)(2,1)S(1)}, u32[]{:S(2)}, u32[]{:S(2)}) collective-permute-start(bf16[4,528,128]{2,1,0:T(8,128)(2,1)S(1)} %collective-permute-done.15.refs_3_), channel_id=1, source_target_pairs={{0,4},{4,0},{1,5},{5,1},{2,6},{6,2},{3,7},{7,3},{8,12},{12,8},{9,1... | collective-permute-start | bytes 1622024 | tf_op jit(solution)/shard_map/ppermute | solution.py:305
  50.0 10.1 %collective-permute-start.18 = (bf16[4,528,128]{2,1,0:T(8,128)(2,1)S(1)}, bf16[4,528,128]{2,1,0:T(8,128)(2,1)S(1)}, u32[]{:S(2)}, u32[]{:S(2)}) collective-permute-start(bf16[4,528,128]{2,1,0:T(8,128)(2,1)S(1)} %collective-permute-done.15.refs_3_), channel_id=1, source_target_pairs={{0,8},{4,252},{8,16},{12,4},{16,24},{20,12},{24,32},{28,20},{32,40... | collective-permute-start | bytes 1622024 | tf_op jit(solution)/shard_map/ppermute | solution.py:297
  54.6 9.3 %collective-permute-start.14 = (bf16[2,128,128]{2,1,0:T(8,128)(2,1)S(1)}, bf16[2,128,128]{2,1,0:T(8,128)(2,1)S(1)}, u32[]{:S(2)}, u32[]{:S(2)}) collective-permute-start(bf16[2,128,128]{2,1,0:T(8,128)(2,1)S(1)} %get-tuple-element.92), channel_id=1, source_target_pairs={{0,24},{8,16},{16,8},{24,0},{1,25},{9,17},{17,9},{25,1},{2,26},{10... | collective-permute-start | bytes 196616 | tf_op jit(solution)/shard_map/ppermute | solution.py:301
  55.1 10.3 %collective-permute-start.13 = (bf16[2,128,128]{2,1,0:T(8,128)(2,1)S(1)}, bf16[2,128,128]{2,1,0:T(8,128)(2,1)S(1)}, u32[]{:S(2)}, u32[]{:S(2)}) collective-permute-start(bf16[2,128,128]{2,1,0:T(8,128)(2,1)S(1)} %get-tuple-element.91), channel_id=1, source_target_pairs={{0,16},{8,24},{16,0},{24,8},{1,17},{9,25},{17,1},{25,9},{2,18},{10... | collective-permute-start | bytes 196616 | tf_op jit(solution)/shard_map/ppermute | solution.py:301
  55.1 10.3 %collective-permute-start.12 = (bf16[2,128,128]{2,1,0:T(8,128)(2,1)S(1)}, bf16[2,128,128]{2,1,0:T(8,128)(2,1)S(1)}, u32[]{:S(2)}, u32[]{:S(2)}) collective-permute-start(bf16[2,128,128]{2,1,0:T(8,128)(2,1)S(1)} %get-tuple-element.90), channel_id=1, source_target_pairs={{0,8},{8,0},{16,24},{24,16},{1,9},{9,1},{17,25},{25,17},{2,10},{10... | collective-permute-start | bytes 196616 | tf_op jit(solution)/shard_map/ppermute | solution.py:301
  60.1 13.2 %collective-permute-start.20 = (bf16[4,528,128]{2,1,0:T(8,128)(2,1)S(1)}, bf16[4,528,128]{2,1,0:T(8,128)(2,1)S(1)}, u32[]{:S(2)}, u32[]{:S(2)}) collective-permute-start(bf16[4,528,128]{2,1,0:T(8,128)(2,1)S(1)} %collective-permute-done.18.refs_3_), channel_id=1, source_target_pairs={{0,4},{4,0},{1,5},{5,1},{2,6},{6,2},{3,7},{7,3},{8,12},{12,8},{9,1... | collective-permute-start | bytes 1622024 | tf_op jit(solution)/shard_map/ppermute | solution.py:305
  65.4 2.6 %collective-permute-start.17 = (bf16[4,2,128,128]{3,2,1,0:T(8,128)(2,1)S(1)}, bf16[4,2,128,128]{3,2,1,0:T(8,128)(2,1)S(1)}, u32[]{:S(2)}, u32[]{:S(2)}) collective-permute-start(bf16[4,2,128,128]{3,2,1,0:T(8,128)(2,1)S(1)} %pad_maximum_fusion.2.near), channel_id=1, source_target_pairs={{0,4},{4,0},{1,5},{5,1},{2,6},{6,2},{3,7},{7,3},{8,12},{12,8},{9,1... | collective-permute-start | bytes 786440 | tf_op jit(solution)/shard_map/ppermute | solution.py:305
  65.5 11.8 %collective-permute-start.19 = (bf16[4,528,128]{2,1,0:T(8,128)(2,1)S(1)}, bf16[4,528,128]{2,1,0:T(8,128)(2,1)S(1)}, u32[]{:S(2)}, u32[]{:S(2)}) collective-permute-start(bf16[4,528,128]{2,1,0:T(8,128)(2,1)S(1)} %collective-permute-done.18.refs_3_), channel_id=1, source_target_pairs={{0,8},{4,252},{8,16},{12,4},{16,24},{20,12},{24,32},{28,20},{32,40... | collective-permute-start | bytes 1622024 | tf_op jit(solution)/shard_map/ppermute | solution.py:297
  69.4 4.9 %collective-permute-start.21 = (f32[8,128]{1,0:T(8,128)S(1)}, f32[8,128]{1,0:T(8,128)S(1)}, u32[]{:S(2)}, u32[]{:S(2)}) collective-permute-start(f32[8,128]{1,0:T(8,128)S(1)} %get-tuple-element.105.own), channel_id=1, source_target_pairs={{0,1},{1,0},{2,3},{3,2},{4,5},{5,4},{6,7},{7,6},{8,9},{9,8},{10,11... | collective-permute-start | bytes 12296 | tf_op jit(solution)/shard_map/ppermute | solution.py:301
  70.7 4.3 %collective-permute-start.22 = (f32[8,128]{1,0:T(8,128)S(1)}, f32[8,128]{1,0:T(8,128)S(1)}, u32[]{:S(2)}, u32[]{:S(2)}) collective-permute-start(f32[8,128]{1,0:T(8,128)S(1)} %get-tuple-element.105.own), channel_id=1, source_target_pairs={{0,2},{1,3},{2,0},{3,1},{4,6},{5,7},{6,4},{7,5},{8,10},{9,11},{10,... | collective-permute-start | bytes 12296 | tf_op jit(solution)/shard_map/ppermute | solution.py:301
  73.4 4.0 %collective-permute-start.23 = (f32[8,128]{1,0:T(8,128)S(1)}, f32[8,128]{1,0:T(8,128)S(1)}, u32[]{:S(2)}, u32[]{:S(2)}) collective-permute-start(f32[8,128]{1,0:T(8,128)S(1)} %get-tuple-element.105.own), channel_id=1, source_target_pairs={{0,3},{1,2},{2,1},{3,0},{4,7},{5,6},{6,5},{7,4},{8,11},{9,10},{10,... | collective-permute-start | bytes 12296 | tf_op jit(solution)/shard_map/ppermute | solution.py:301
  77.3 2.9 %collective-permute-start.24 = (bf16[4,528,128]{2,1,0:T(8,128)(2,1)S(1)}, bf16[4,528,128]{2,1,0:T(8,128)(2,1)S(1)}, u32[]{:S(2)}, u32[]{:S(2)}) collective-permute-start(bf16[4,528,128]{2,1,0:T(8,128)(2,1)S(1)} %collective-permute-done.19.refs_3_), channel_id=1, source_target_pairs={{0,4},{4,0},{1,5},{5,1},{2,6},{6,2},{3,7},{7,3},{8,12},{12,8},{9,1... | collective-permute-start | bytes 1622024 | tf_op jit(solution)/shard_map/ppermute | solution.py:305
  80.3 1.8 %copy-start = (f32[16,128]{1,0:T(8,128)S(1)}, f32[16,128]{1,0:T(8,128)}, u32[]{:S(2)}) copy-start(f32[16,128]{1,0:T(8,128)} %gain.1) | copy-start | bytes 24580
